TPU v7x, 256 devices: a whole 4x4x8 slice. The times are simulated.
256 devices in a mesh: intra: 8 (over y_lo, x), inter: 32 (over z, y_hi, core).
Axes of the slice: x: 4, y: 4 (y_hi: 2, y_lo: 2; y = y_hi * 2 + y_lo), z: 8, core: 2. Of those that a mesh axis runs over, the one named last changes fastest.
Arguments:
- acts: bfloat16 [32768, 4096], P(('intra', 'inter')), may hold values from -24 to 24
- grad_out: bfloat16 [32768, 512], P(('intra', 'inter')), may hold values from -6 to 6
- codes: int32 [4096, 512], P('intra'), may hold values from -127 to 127
- scales: float32 [2048], P('intra'), may hold values from 0.0002 to 0.0008
Outputs:
- grad_in: bfloat16 [32768, 4096], P(('intra', 'inter'))
- grad_w: float32 [4096, 512], P(('intra', 'inter'))
All inputs are finite; a program needn't handle non-finite values.
Results may differ from a plain program's by a relative error of at most 0.0049.
Values may be sent and summed in bfloat16 or wider, within the bound.
No kernel may reach another device: no remote copies, remote signals or barrier semaphores. Data moves between devices by JAX's collectives and lax.ppermute only.
A program may use at most 64 MiB of HBM per device.

v0:
```python
import math

import jax
import jax.numpy as jnp
from jax import lax
from jax.sharding import PartitionSpec as P


def laid_out(parts, dim):
    parts = jnp.moveaxis(parts, 0, dim)
    lengths = parts.shape
    return parts.reshape(*lengths[:dim], lengths[dim] * lengths[dim + 1], *lengths[dim + 2 :])


def sent_to_all(value, axis):
    copies = jnp.broadcast_to(value, (lax.axis_size(axis), *value.shape))
    return lax.all_to_all(copies, axis, split_axis=0, concat_axis=0, tiled=True)


def gather_directly(value, axis, dim):
    return laid_out(sent_to_all(value, axis), dim)


def in_blocks(value, dim, devices):
    before, after = (value.shape[:dim], value.shape[dim + 1 :])
    return jnp.moveaxis(value.reshape(*before, devices, -1, *after), dim, 0)


def sent_and_summed(value, axis, dim):
    parts = in_blocks(value, dim, lax.axis_size(axis))
    arrived = lax.all_to_all(parts, axis, split_axis=0, concat_axis=0, tiled=True)
    return arrived.astype(jnp.float32).sum(axis=0)


def per_device(acts, grad_out, codes, scales):
    rows = codes.shape[0]
    width_kv = codes.shape[1]
    blocks = codes.astype(jnp.float32).reshape(rows // 2, 2 * width_kv) * scales[:, None]
    local_weight = blocks.reshape(rows, width_kv).astype(jnp.bfloat16)
    n_group = lax.axis_size("intra")
    n_cross = lax.axis_size("inter")
    tok_rows = acts.shape[0]
    factor = 1.0 / math.sqrt(tok_rows * n_group * n_cross)
    contract = (((0,), (0,)), ((), ()))
    group_cot = gather_directly(grad_out, "intra", 0)
    columns_owned = lax.all_to_all(acts, "intra", split_axis=1, concat_axis=0, tiled=True)
    grad_w = sent_and_summed(
        (
            lax.dot_general(columns_owned, group_cot, contract, preferred_element_type=jnp.float32)
            * factor
        ).astype(jnp.bfloat16),
        "inter",
        0,
    )
    pieces = jnp.dot(group_cot, local_weight.T, preferred_element_type=jnp.float32).astype(
        jnp.bfloat16
    )
    grad_in = lax.all_to_all(pieces, "intra", split_axis=0, concat_axis=1, tiled=True)
    return (grad_in, grad_w)


def solution(mesh):
    in_specs = (
        P(("intra", "inter"), None),
        P(("intra", "inter"), None),
        P("intra", None),
        P("intra"),
    )
    out_specs = (P(("intra", "inter"), None), P(("intra", "inter"), None))
    return jax.shard_map(
        per_device, mesh=mesh, in_specs=in_specs, out_specs=out_specs, check_vma=False
    )
```

profile of v0, /device:TPU:1, one launch (start us, length us, event | category | flops | bytes accessed | tf_op | source)
XLA Modules:
  0.0 92.7 jit_solution(9063897795220184609)
XLA Ops:
  0.6 2.0 %broadcast_in_dim.4 = bf16[8,128,512]{2,1,0:T(8,128)(2,1)} broadcast(bf16[128,512]{1,0:T(8,128)(2,1)} %param.5), dimensions={1,2} | broadcast | bytes 1179648 | tf_op jit(solution)/shard_map/broadcast_in_dim | solution.py:16
  2.6 0.0 copy-start
  2.6 6.0 %all-to-all-start = ((bf16[8,128,512]{2,1,0:T(8,128)(2,1)}), bf16[8,128,512]{2,1,0:T(8,128)(2,1)S(1)}, u32[]{:S(2)}, u32[]{:S(2)}) async-start(bf16[8,128,512]{2,1,0:T(8,128)(2,1)} %broadcast_in_dim.4), calls=%async_computation | async-start | bytes 2097152 | tf_op jit(solution)/shard_map/all_to_all | solution.py:17
  8.6 0.0 copy-done
  8.6 1.3 %copy.11 = bf16[128,4096]{0,1:T(8,128)(2,1)} copy(bf16[128,4096]{1,0:T(8,128)(2,1)S(1)} %copy-done) | data formatting | bytes 2097152 | tf_op args[0]
  9.9 14.5 %all-to-all-done = bf16[8,128,512]{2,1,0:T(8,128)(2,1)S(1)} async-done(((bf16[8,128,512]{2,1,0:T(8,128)(2,1)}), bf16[8,128,512]{2,1,0:T(8,128)(2,1)S(1)}, u32[]{:S(2)}, u32[]{:S(2)}) %all-to-all-start) | async-done | bytes 1048608 | tf_op jit(solution)/shard_map/all_to_all | solution.py:17
  24.4 0.0 copy-start.2
  24.4 0.0 copy-start.1
  24.4 3.7 %all-to-all-start.2 = ((bf16[128,8,512]{0,2,1:T(8,128)(2,1)}), bf16[128,8,512]{0,2,1:T(8,128)(2,1)S(1)}, u32[]{:S(2)}, u32[]{:S(2)}) async-start(bf16[128,8,512]{0,2,1:T(8,128)(2,1)} %bitcast.4), calls=%async_computation.2 | async-start | bytes 2097152 | tf_op jit(solution)/shard_map/all_to_all | solution.py:46
  28.1 0.0 copy-done.2
  28.1 0.1 mul.19
  28.2 0.1 mul.20
  28.4 0.0 copy-done.1
  28.4 0.8 fusion.1
  29.1 1.2 %copy.15 = bf16[64,8,8,128]{3,2,0,1:T(8,128)(2,1)} copy(bf16[64,8,8,128]{3,2,1,0:T(8,128)(2,1)S(1)} %fusion.1) | data formatting | bytes 2097152 | tf_op jit(solution)/shard_map/all_to_all | solution.py:58
  30.3 13.6 %all-to-all-done.2 = bf16[128,8,512]{0,2,1:T(8,128)(2,1)S(1)} async-done(((bf16[128,8,512]{0,2,1:T(8,128)(2,1)}), bf16[128,8,512]{0,2,1:T(8,128)(2,1)S(1)}, u32[]{:S(2)}, u32[]{:S(2)}) %all-to-all-start.2) | async-done | bytes 1048608 | tf_op jit(solution)/shard_map/all_to_all | solution.py:46
  43.9 3.6 %all-to-all-start.1 = ((bf16[8,128,512]{1,2,0:T(8,128)(2,1)}), bf16[8,128,512]{1,2,0:T(8,128)(2,1)S(1)}, u32[]{:S(2)}, u32[]{:S(2)}) async-start(bf16[8,128,512]{1,2,0:T(8,128)(2,1)} %bitcast.22), calls=%async_computation.1 | async-start | bytes 2097152 | tf_op jit(solution)/shard_map/all_to_all | solution.py:58
  47.4 1.5 %fusion.2 = bf16[512,512]{1,0:T(8,128)(2,1)} fusion(bf16[8,128,512]{2,1,0:T(8,128)(2,1)S(1)} %all-to-all-done, bf16[128,8,512]{0,2,1:T(8,128)(2,1)S(1)} %all-to-all-done.2), kind=kOutput, calls=%fused_computation.4 | convolution fusion | flops 537395200 | bytes 2621440 | tf_op jit(solution)/shard_map/dot_general | solution.py:49
  49.0 14.3 %all-to-all-done.1 = bf16[8,128,512]{1,2,0:T(8,128)(2,1)S(1)} async-done(((bf16[8,128,512]{1,2,0:T(8,128)(2,1)}), bf16[8,128,512]{1,2,0:T(8,128)(2,1)S(1)}, u32[]{:S(2)}, u32[]{:S(2)}) %all-to-all-start.1) | async-done | bytes 1048608 | tf_op jit(solution)/shard_map/all_to_all | solution.py:58
  63.2 11.8 %all-to-all-start.3 = ((bf16[32,16,512]{2,1,0:T(8,128)(2,1)}), bf16[32,16,512]{2,1,0:T(8,128)(2,1)S(1)}, u32[]{:S(2)}, u32[]{:S(2)}) async-start(bf16[32,16,512]{2,1,0:T(8,128)(2,1)} %bitcast.25), calls=%async_computation.3 | async-start | bytes 1048576 | tf_op jit(solution)/shard_map/all_to_all | solution.py:31
  75.0 1.3 %copy.12 = bf16[128,4096]{1,0:T(8,128)(2,1)} copy(bf16[128,4096]{0,1:T(8,128)(2,1)S(1)} %bitcast.23) | data formatting | bytes 2097152
  76.3 15.7 %all-to-all-done.3 = bf16[32,16,512]{2,1,0:T(8,128)(2,1)S(1)} async-done(((bf16[32,16,512]{2,1,0:T(8,128)(2,1)}), bf16[32,16,512]{2,1,0:T(8,128)(2,1)S(1)}, u32[]{:S(2)}, u32[]{:S(2)}) %all-to-all-start.3) | async-done | bytes 524320 | tf_op jit(solution)/shard_map/all_to_all | solution.py:31
  92.0 0.7 convert_reduce_fusion
Async XLA Ops:
  2.6 6.0 %copy-start = (bf16[128,4096]{1,0:T(8,128)(2,1)S(1)}, bf16[128,4096]{1,0:T(8,128)(2,1)}, u32[]{:S(2)}) copy-start(bf16[128,4096]{1,0:T(8,128)(2,1)} %param.4) | copy-start | bytes 3145732
  2.6 21.8 %all-to-all-start = ((bf16[8,128,512]{2,1,0:T(8,128)(2,1)}), bf16[8,128,512]{2,1,0:T(8,128)(2,1)S(1)}, u32[]{:S(2)}, u32[]{:S(2)}) async-start(bf16[8,128,512]{2,1,0:T(8,128)(2,1)} %broadcast_in_dim.4), calls=%async_computation | async-start | bytes 2097152 | tf_op jit(solution)/shard_map/all_to_all | solution.py:17
  24.4 3.7 %copy-start.2 = (f32[256]{0:T(256)S(1)}, f32[256]{0:T(256)}, u32[]{:S(2)}) copy-start(f32[256]{0:T(256)} %param.7) | copy-start | bytes 3076
  24.4 4.0 %copy-start.1 = (s32[512,512]{1,0:T(8,128)S(1)}, s32[512,512]{1,0:T(8,128)}, u32[]{:S(2)}) copy-start(s32[512,512]{1,0:T(8,128)} %param.6) | copy-start | bytes 3145732
  24.4 19.5 %all-to-all-start.2 = ((bf16[128,8,512]{0,2,1:T(8,128)(2,1)}), bf16[128,8,512]{0,2,1:T(8,128)(2,1)S(1)}, u32[]{:S(2)}, u32[]{:S(2)}) async-start(bf16[128,8,512]{0,2,1:T(8,128)(2,1)} %bitcast.4), calls=%async_computation.2 | async-start | bytes 2097152 | tf_op jit(solution)/shard_map/all_to_all | solution.py:46
  43.9 19.3 %all-to-all-start.1 = ((bf16[8,128,512]{1,2,0:T(8,128)(2,1)}), bf16[8,128,512]{1,2,0:T(8,128)(2,1)S(1)}, u32[]{:S(2)}, u32[]{:S(2)}) async-start(bf16[8,128,512]{1,2,0:T(8,128)(2,1)} %bitcast.22), calls=%async_computation.1 | async-start | bytes 2097152 | tf_op jit(solution)/shard_map/all_to_all | solution.py:58
  63.2 28.8 %all-to-all-start.3 = ((bf16[32,16,512]{2,1,0:T(8,128)(2,1)}), bf16[32,16,512]{2,1,0:T(8,128)(2,1)S(1)}, u32[]{:S(2)}, u32[]{:S(2)}) async-start(bf16[32,16,512]{2,1,0:T(8,128)(2,1)} %bitcast.25), calls=%async_computation.3 | async-start | bytes 1048576 | tf_op jit(solution)/shard_map/all_to_all | solution.py:31
where the time goes:
time: 93.1 us; the launch traced here: 92.7 us
  waiting for transfers between devices  58 us (62%)
  starting transfers between devices  25 us (27%)
  local copies, waits for them, and re-layouts  6 us (6%)
  matrix products  2.28 us (2%)
    all_to_all x1, waiting for transfers between devices, sent_and_summed(): lax.all_to_all(parts, axis, split_axis=0, concat_axis=0, tiled=True)  15.7 us
    all_to_all x1, waiting for transfers between devices, sent_to_all(): return lax.all_to_all(copies, axis, split_axis=0, concat_axis=0, tiled=True)  14.5 us
    all_to_all x1, waiting for transfers between devices, per_device(): lax.all_to_all(pieces, 'intra', split_axis=0, concat_axis=1, tiled=True)  14.3 us
    all_to_all x1, waiting for transfers between devices, per_device(): lax.all_to_all(acts, 'intra', split_axis=1, concat_axis=0, tiled=True)  13.6 us
    all_to_all x1, starting transfers between devices, sent_and_summed(): lax.all_to_all(parts, axis, split_axis=0, concat_axis=0, tiled=True)  11.8 us
    all_to_all x1, starting transfers between devices, sent_to_all(): return lax.all_to_all(copies, axis, split_axis=0, concat_axis=0, tiled=True)  5.99 us
    all_to_all x1, starting transfers between devices, per_device(): lax.all_to_all(acts, 'intra', split_axis=1, concat_axis=0, tiled=True)  3.69 us
    all_to_all x1, starting transfers between devices, per_device(): lax.all_to_all(pieces, 'intra', split_axis=0, concat_axis=1, tiled=True)  3.56 us
  transfers between devices with their start and end apart: 4, of which 4 were waited for; matrix products, arithmetic and copies ran while one was open for 7% of the time, Pallas kernels for 0%

commit v1 on v0

v1 whole, which is shorter than its diff:
```python
import math

import jax
import jax.numpy as jnp
from jax import lax
from jax.sharding import Mesh
from jax.sharding import PartitionSpec as P

NYL, NX, NZ, NYH, NC = 2, 4, 8, 2, 2
NY = NYL * NYH
AXES = ("yl", "x", "z", "yh", "c")


def device(x, y, z, c):
    x, y, z = x % NX, y % NY, z % NZ
    return (((y % NYL * NX + x) * NZ + z) * NYH + y // NYL) * NC + c


def moved(value, step):
    places = [(x, y, z, c) for x in range(NX) for y in range(NY) for z in range(NZ) for c in range(NC)]
    return lax.ppermute(value, AXES, [(device(*p), device(*step(*p))) for p in places])


def along_x(value, by):
    return moved(value, lambda x, y, z, c: (x + by, y, z, c))


def along_y(value, by):
    return moved(value, lambda x, y, z, c: (x, y + by, z, c))


def per_device(acts, grad_out, codes, scales):
    tokens, width = acts.shape
    rows, kv = codes.shape
    yl, x, yh, c = (lax.axis_index(a) for a in ("yl", "x", "yh", "c"))
    y = NYL * yh + yl
    factor = 1.0 / math.sqrt(tokens * NYL * NX * NZ * NYH * NC)
    shifts = (1, NX - 1, 2)

    cots = [grad_out] + [along_x(grad_out, s) for s in shifts]
    acts4 = acts.reshape(tokens, NYL, NX, rows)

    def columns_of(xx):
        picked = lax.dynamic_slice_in_dim(acts4, xx % NX, 1, axis=2)
        return picked.reshape(tokens, NYL * rows)

    cols = [columns_of(x)] + [along_x(columns_of(x + s), s) for s in shifts]

    blocks = codes.astype(jnp.float32).reshape(rows // 2, 2 * kv) * scales[:, None]
    own = blocks.reshape(rows, kv).astype(jnp.bfloat16)
    other = moved(own, lambda x, y, z, c: (x, y + 1 - 2 * c, z, c))
    first = jnp.where(yl == 0, own, other)
    second = jnp.where(yl == 0, other, own)
    weight = jnp.concatenate([first, second], axis=0)

    def product(cot):
        return jnp.dot(cot, weight.T, preferred_element_type=jnp.float32).astype(jnp.bfloat16)

    pieces = [product(cots[0])] + [along_x(product(cot), -s) for cot, s in zip(cots[1:], shifts)]
    grad_in = jnp.zeros((tokens, NYL, NX, rows), jnp.bfloat16)
    for piece, s in zip(pieces, (0,) + shifts):
        grad_in = lax.dynamic_update_slice_in_dim(
            grad_in, piece.reshape(tokens, NYL, 1, rows), (x + s) % NX, axis=2
        )
    grad_in = grad_in.reshape(tokens, width)

    contract = (((0,), (0,)), ((), ()))
    terms = sum(
        lax.dot_general(a, g, contract, preferred_element_type=jnp.float32) for a, g in zip(cols, cots)
    ) * factor
    terms = terms.reshape(NYL, NZ, NYH, NC, -1, kv)
    sent = lax.dynamic_index_in_dim(terms, 1 - c, 3, keepdims=False).astype(jnp.bfloat16)
    kept = lax.dynamic_index_in_dim(terms, c, 3, keepdims=False)
    arrived = moved(sent, lambda x, y, z, c: (x, y, z, 1 - c))
    chip = (kept + arrived.astype(jnp.float32)).astype(jnp.bfloat16)
    by_y = chip.transpose(2, 0, 1, 3, 4).reshape(NY, NZ, -1, kv)

    def of_y(yy):
        return lax.dynamic_index_in_dim(by_y, yy % NY, 0, keepdims=False)

    column = of_y(y).astype(jnp.float32)
    for s in (1, NY - 1, 2):
        column = column + along_y(of_y(y + s), s).astype(jnp.float32)
    ring = lax.all_to_all(column.astype(jnp.bfloat16), "z", split_axis=0, concat_axis=0, tiled=True)
    grad_w = ring.astype(jnp.float32).sum(axis=0)
    return (grad_in, grad_w)


def solution(mesh):
    fine = Mesh(mesh.devices.reshape(NYL, NX, NZ, NYH, NC), AXES)
    whole = ("yl", "x", "z", "yh", "c")
    in_specs = (P(whole, None), P(whole, None), P(("yl", "x"), None), P(("yl", "x")))
    out_specs = (P(whole, None), P(whole, None))
    return jax.shard_map(
        per_device, mesh=fine, in_specs=in_specs, out_specs=out_specs, check_vma=False
    )
```

time: 93.1 us -> 79.3 us (0.85)
  the two profiles are of different devices: /device:TPU:1 before, /device:TPU:34 now
where the time goes in v1:
time: 79.3 us; the launch traced here: 79 us
  starting transfers between devices  25.4 us (32%)
  local copies, waits for them, and re-layouts  23.8 us (30%)
  waiting for transfers between devices  16.3 us (21%)
  matrix products  9.78 us (12%)
  other arithmetic  2.82 us (4%)
  between operations  0.93 us (1%)
    dynamic_update_slice x4, local copies, waits for them, and re-layouts, per_device(): lax.dynamic_update_slice_in_dim(grad_in, piece.reshape(tokens, NYL, 1, ro...  17.1 us
    ppermute x14, starting transfers between devices, moved(): lax.ppermute(value, AXES, [(device(*p), device(*step(*p))) for p in places])  16.8 us
    ppermute x14, waiting for transfers between devices, moved(): lax.ppermute(value, AXES, [(device(*p), device(*step(*p))) for p in places])  16.3 us
    all_to_all x1, starting transfers between devices, per_device(): lax.all_to_all(column.astype(jnp.bfloat16), 'z', split_axis=0, concat_axi...  8.57 us
    dot_general x4, matrix products, product(): jnp.dot(cot, weight.T, preferred_element_type=jnp.float32)  5.13 us
    dot_general x4, matrix products, per_device(): lax.dot_general(a, g, contract, preferred_element_type=jnp.float32)  4.65 us
    reshape x4, local copies, waits for them, and re-layouts, per_device(): piece.reshape(tokens, NYL, 1, rows)  1.95 us
    unnamed x9, local copies, waits for them, and re-layouts  1.67 us
  transfers between devices with their start and end apart: 15, of which 5 were waited for; matrix products, arithmetic and copies ran while one was open for 45% of the time, Pallas kernels for 0%

profile of v1, /device:TPU:34, one launch (start us, length us, event | category | flops | bytes accessed | tf_op | source)
XLA Modules:
  0.0 79.0 jit_solution(5037847167282380094)
XLA Ops:
  1.2 1.5 %collective-permute-start.1 = (bf16[128,512]{1,0:T(8,128)(2,1)}, bf16[128,512]{1,0:T(8,128)(2,1)}, u32[]{:S(2)}, u32[]{:S(2)}) collective-permute-start(bf16[128,512]{1,0:T(8,128)(2,1)} %param.5), channel_id=1, source_target_pairs={{0,32},{1,33},{4,36},{5,37},{8,40},{9,41},{12,44},{13,45},{16,48},... | collective-permute-start | bytes 393224 | tf_op jit(solution)/shard_map/ppermute | solution.py:21
  2.7 3.3 %collective-permute-start.5 = (bf16[128,512]{1,0:T(8,128)(2,1)}, bf16[128,512]{1,0:T(8,128)(2,1)}, u32[]{:S(2)}, u32[]{:S(2)}) collective-permute-start(bf16[128,512]{1,0:T(8,128)(2,1)} %param.5), channel_id=1, source_target_pairs={{0,64},{1,65},{4,68},{5,69},{8,72},{9,73},{12,76},{13,77},{16,80},... | collective-permute-start | bytes 393224 | tf_op jit(solution)/shard_map/ppermute | solution.py:21
  6.1 1.6 %copy.20 = bf16[128,4096]{0,1:T(8,128)(2,1)S(1)} copy(bf16[128,4096]{1,0:T(8,128)(2,1)} %param.4) | data formatting | bytes 2097152 | tf_op args[0]
  8.9 1.8 %collective-permute-start.7 = (bf16[128,1024]{0,1:T(8,128)(2,1)}, bf16[128,1024]{0,1:T(8,128)(2,1)}, u32[]{:S(2)}, u32[]{:S(2)}) collective-permute-start(bf16[128,1024]{0,1:T(8,128)(2,1)} %bitcast.10), channel_id=1, source_target_pairs={{0,32},{1,33},{4,36},{5,37},{8,40},{9,41},{12,44},{13,45},{16,48},... | collective-permute-start | bytes 786440 | tf_op jit(solution)/shard_map/ppermute | solution.py:21
  12.3 1.4 %collective-permute-start.9 = (bf16[128,1024]{0,1:T(8,128)(2,1)S(1)}, bf16[128,1024]{0,1:T(8,128)(2,1)S(1)}, u32[]{:S(2)}, u32[]{:S(2)}) collective-permute-start(bf16[128,1024]{0,1:T(8,128)(2,1)S(1)} %bitcast.54), channel_id=1, source_target_pairs={{0,64},{1,65},{4,68},{5,69},{8,72},{9,73},{12,76},{13,77},{16,80},... | collective-permute-start | bytes 786440 | tf_op jit(solution)/shard_map/ppermute | solution.py:21
  13.7 8.1 %collective-permute-done.8 = bf16[128,1024]{0,1:T(8,128)(2,1)} collective-permute-done((bf16[128,1024]{0,1:T(8,128)(2,1)}, bf16[128,1024]{0,1:T(8,128)(2,1)}, u32[]{:S(2)}, u32[]{:S(2)}) %collective-permute-start.8) | collective-permute-done | bytes 262176 | tf_op jit(solution)/shard_map/ppermute | solution.py:21
  21.8 1.6 %collective-permute-start = (bf16[512,512]{1,0:T(8,128)(2,1)}, bf16[512,512]{1,0:T(8,128)(2,1)S(1)}, u32[]{:S(2)}, u32[]{:S(2)}) collective-permute-start(bf16[512,512]{1,0:T(8,128)(2,1)} %multiply_convert_fusion), channel_id=1, source_target_pairs={{0,128},{1,131},{4,132},{5,135},{8,136},{9,139},{12,140},{13,143},... | collective-permute-start | bytes 1572872 | tf_op jit(solution)/shard_map/ppermute | solution.py:21
  23.4 1.4 %fusion.10 = f32[1024,512]{1,0:T(8,128)S(1)} fusion(bf16[128,1024]{0,1:T(8,128)(2,1)} %collective-permute-done.8, bf16[128,512]{1,0:T(8,128)(2,1)} %collective-permute-done.3), kind=kOutput, calls=%fused_computation.32 | convolution fusion | flops 134217728 | bytes 2490368 | tf_op jit(solution)/shard_map/dot_general | solution.py:69
  24.8 1.4 %fusion.9 = f32[1024,512]{1,0:T(8,128)S(1)} fusion(bf16[128,1024]{0,1:T(8,128)(2,1)} %collective-permute-done.7, bf16[128,512]{1,0:T(8,128)(2,1)} %collective-permute-done.1), kind=kOutput, calls=%fused_computation.31 | convolution fusion | flops 134217728 | bytes 2490368 | tf_op jit(solution)/shard_map/dot_general | solution.py:69
  26.2 1.5 %add_multiply_fusion = f32[1024,512]{1,0:T(8,128)S(1)} fusion(f32[1024,512]{1,0:T(8,128)S(1)} %fusion.10, f32[1024,512]{1,0:T(8,128)S(1)} %fusion.8, f32[1024,512]{1,0:T(8,128)S(1)} %fusion.9, bf16[128,1024]{0,1:T(8,128)(2,1)S(1)} %collective-permute-done.9, bf16[128,512]{1,0:T(8,128)(2,1)} %collective-permute-done.5), kind=kOutput, calls=%fused_computation | convolution fusion | flops 136314880 | bytes 8781824 | tf_op jit(solution)/shard_map/dot_general | solution.py:69
  27.9 4.5 %collective-permute-done = bf16[512,512]{1,0:T(8,128)(2,1)S(1)} collective-permute-done((bf16[512,512]{1,0:T(8,128)(2,1)}, bf16[512,512]{1,0:T(8,128)(2,1)S(1)}, u32[]{:S(2)}, u32[]{:S(2)}) %collective-permute-start) | collective-permute-done | bytes 524320 | tf_op jit(solution)/shard_map/ppermute | solution.py:21
  32.7 1.3 %fusion = bf16[128,1024]{0,1:T(8,128)(2,1)S(1)} fusion(bf16[128,512]{1,0:T(8,128)(2,1)} %collective-permute-done.1, bf16[512,512]{1,0:T(8,128)(2,1)S(1)} %get-tuple-element.7, bf16[512,512]{1,0:T(8,128)(2,1)S(1)} %get-tuple-element.6), kind=kOutput, calls=%fused_computation.5 | convolution fusion | flops 136445952 | bytes 1441792 | tf_op jit(solution)/shard_map/dot_general | solution.py:57
  34.1 1.3 %fusion.1 = bf16[128,1024]{0,1:T(8,128)(2,1)S(1)} fusion(bf16[128,512]{1,0:T(8,128)(2,1)} %collective-permute-done.3, bf16[512,512]{1,0:T(8,128)(2,1)S(1)} %get-tuple-element.7, bf16[512,512]{1,0:T(8,128)(2,1)S(1)} %get-tuple-element.6), kind=kOutput, calls=%fused_computation.6 | convolution fusion | flops 136445952 | bytes 1441792 | tf_op jit(solution)/shard_map/dot_general | solution.py:57
  35.5 2.1 %collective-permute-start.4 = (bf16[128,1024]{0,1:T(8,128)(2,1)S(1)}, bf16[128,1024]{0,1:T(8,128)(2,1)S(1)}, u32[]{:S(2)}, u32[]{:S(2)}) collective-permute-start(bf16[128,1024]{0,1:T(8,128)(2,1)S(1)} %fusion.1), channel_id=1, source_target_pairs={{0,32},{1,33},{4,36},{5,37},{8,40},{9,41},{12,44},{13,45},{16,48},... | collective-permute-start | bytes 786440 | tf_op jit(solution)/shard_map/ppermute | solution.py:21
  38.2 2.9 %collective-permute-start.12 = (bf16[8,16,512]{2,1,0:T(8,128)(2,1)S(1)}, bf16[8,16,512]{2,1,0:T(8,128)(2,1)S(1)}, u32[]{:S(2)}, u32[]{:S(2)}) collective-permute-start(bf16[8,16,512]{2,1,0:T(8,128)(2,1)S(1)} %get-tuple-element.10), channel_id=1, source_target_pairs={{0,130},{1,131},{4,134},{5,135},{8,138},{9,139},{12,142},{13,143},... | collective-permute-start | bytes 393224 | tf_op jit(solution)/shard_map/ppermute | solution.py:21
  41.9 2.0 %fusion.2 = bf16[128,1024]{0,1:T(8,128)(2,1)} fusion(bf16[128,512]{1,0:T(8,128)(2,1)} %collective-permute-done.5, bf16[512,512]{1,0:T(8,128)(2,1)S(1)} %get-tuple-element.7, bf16[512,512]{1,0:T(8,128)(2,1)S(1)} %get-tuple-element.6), kind=kOutput, calls=%fused_computation.7 | convolution fusion | flops 136445952 | bytes 1441792 | tf_op jit(solution)/shard_map/dot_general | solution.py:57
  44.1 1.0 %collective-permute-done.12 = bf16[8,16,512]{2,1,0:T(8,128)(2,1)S(1)} collective-permute-done((bf16[8,16,512]{2,1,0:T(8,128)(2,1)S(1)}, bf16[8,16,512]{2,1,0:T(8,128)(2,1)S(1)}, u32[]{:S(2)}, u32[]{:S(2)}) %collective-permute-start.12) | collective-permute-done | bytes 131104 | tf_op jit(solution)/shard_map/ppermute | solution.py:21
  45.1 2.5 %collective-permute-done.13 = bf16[8,16,512]{2,1,0:T(8,128)(2,1)S(1)} collective-permute-done((bf16[8,16,512]{2,1,0:T(8,128)(2,1)S(1)}, bf16[8,16,512]{2,1,0:T(8,128)(2,1)S(1)}, u32[]{:S(2)}, u32[]{:S(2)}) %collective-permute-start.13) | collective-permute-done | bytes 131104 | tf_op jit(solution)/shard_map/ppermute | solution.py:21
  48.3 8.6 %all-to-all-start = ((bf16[8,16,512]{2,1,0:T(8,128)(2,1)}), bf16[8,16,512]{2,1,0:T(8,128)(2,1)S(1)}, u32[]{:S(2)}, u32[]{:S(2)}) async-start(bf16[8,16,512]{2,1,0:T(8,128)(2,1)} %fusion.7), calls=%async_computation | async-start | bytes 262144 | tf_op jit(solution)/shard_map/all_to_all | solution.py:84
  58.1 4.3 %dynamic_update_slice.12 = bf16[128,2,4,512]{3,2,1,0:T(4,128)(2,1)S(1)} dynamic-update-slice(bf16[128,2,4,512]{3,2,1,0:T(4,128)(2,1)S(1)} %broadcast_in_dim.4, bf16[128,2,1,512]{3,2,1,0:T(2,128)(2,1)S(1)} %copy.16, s32[]{:T(128)} %constant.85.clone.1, s32[]{:T(128)} %constant.85.clone.1, s32[]{:T(128)S(6)} %select_n.95, s32[]{:T(128)} %constant.85.clone.1) | dynamic-update-slice | bytes 524292 | tf_op jit(solution)/shard_map/dynamic_update_slice | solution.py:62
  63.9 4.3 %dynamic_update_slice.13 = bf16[128,2,4,512]{3,2,1,0:T(4,128)(2,1)S(1)} dynamic-update-slice(bf16[128,2,4,512]{3,2,1,0:T(4,128)(2,1)S(1)} %dynamic_update_slice.12, bf16[128,2,1,512]{3,2,1,0:T(2,128)(2,1)S(1)} %copy.17, s32[]{:T(128)} %constant.85.clone.1, s32[]{:T(128)} %constant.85.clone.1, s32[]{:T(128)S(6)} %select_n.97, s32[]{:T(128)} %constant.85.clone.1) | dynamic-update-slice | bytes 524292 | tf_op jit(solution)/shard_map/dynamic_update_slice | solution.py:62
  68.2 4.3 %dynamic_update_slice.14 = bf16[128,2,4,512]{3,2,1,0:T(4,128)(2,1)S(1)} dynamic-update-slice(bf16[128,2,4,512]{3,2,1,0:T(4,128)(2,1)S(1)} %dynamic_update_slice.13, bf16[128,2,1,512]{3,2,1,0:T(2,128)(2,1)S(1)} %copy.18, s32[]{:T(128)} %constant.85.clone.1, s32[]{:T(128)} %constant.85.clone.1, s32[]{:T(128)S(6)} %select_n.99, s32[]{:T(128)} %constant.85.clone.1) | dynamic-update-slice | bytes 524292 | tf_op jit(solution)/shard_map/dynamic_update_slice | solution.py:62
  72.5 4.3 %dynamic_update_slice.15 = bf16[128,2,4,512]{3,2,1,0:T(4,128)(2,1)S(1)} dynamic-update-slice(bf16[128,2,4,512]{3,2,1,0:T(4,128)(2,1)S(1)} %dynamic_update_slice.14, bf16[128,2,1,512]{3,2,1,0:T(2,128)(2,1)S(1)} %copy.19, s32[]{:T(128)} %constant.85.clone.1, s32[]{:T(128)} %constant.85.clone.1, s32[]{:T(128)S(6)} %select_n.101, s32[]{:T(128)} %constant.85.clone.1) | dynamic-update-slice | bytes 524292 | tf_op jit(solution)/shard_map/dynamic_update_slice | solution.py:62
  76.8 1.6 %reshape.51 = bf16[128,4096]{1,0:T(8,128)(2,1)} reshape(bf16[128,2,4,512]{3,2,1,0:T(4,128)(2,1)S(1)} %dynamic_update_slice.15) | data formatting | bytes 2097152 | tf_op jit(solution)/shard_map/reshape | solution.py:65
  (43 shorter events, 9.5 us)
Async XLA Ops:
  0.6 11.7 %collective-permute-start.3 = (bf16[128,512]{1,0:T(8,128)(2,1)}, bf16[128,512]{1,0:T(8,128)(2,1)}, u32[]{:S(2)}, u32[]{:S(2)}) collective-permute-start(bf16[128,512]{1,0:T(8,128)(2,1)} %param.5), channel_id=1, source_target_pairs={{0,96},{1,97},{4,100},{5,101},{8,104},{9,105},{12,108},{13,109},{1... | collective-permute-start | bytes 393224 | tf_op jit(solution)/shard_map/ppermute | solution.py:21
  1.2 23.5 %collective-permute-start.1 = (bf16[128,512]{1,0:T(8,128)(2,1)}, bf16[128,512]{1,0:T(8,128)(2,1)}, u32[]{:S(2)}, u32[]{:S(2)}) collective-permute-start(bf16[128,512]{1,0:T(8,128)(2,1)} %param.5), channel_id=1, source_target_pairs={{0,32},{1,33},{4,36},{5,37},{8,40},{9,41},{12,44},{13,45},{16,48},... | collective-permute-start | bytes 393224 | tf_op jit(solution)/shard_map/ppermute | solution.py:21
  2.7 23.4 %collective-permute-start.5 = (bf16[128,512]{1,0:T(8,128)(2,1)}, bf16[128,512]{1,0:T(8,128)(2,1)}, u32[]{:S(2)}, u32[]{:S(2)}) collective-permute-start(bf16[128,512]{1,0:T(8,128)(2,1)} %param.5), channel_id=1, source_target_pairs={{0,64},{1,65},{4,68},{5,69},{8,72},{9,73},{12,76},{13,77},{16,80},... | collective-permute-start | bytes 393224 | tf_op jit(solution)/shard_map/ppermute | solution.py:21
  6.1 4.6 %copy-start.1 = (bf16[128,512]{1,0:T(8,128)(2,1)S(1)}, bf16[128,512]{1,0:T(8,128)(2,1)}, u32[]{:S(2)}) copy-start(bf16[128,512]{1,0:T(8,128)(2,1)} %param.5) | copy-start | bytes 393220
  7.7 3.3 %copy-start.3 = (f32[256]{0:T(256)S(1)}, f32[256]{0:T(256)}, u32[]{:S(2)}) copy-start(f32[256]{0:T(256)} %param.7) | copy-start | bytes 3076
  7.8 3.6 %copy-start = (s32[512,512]{1,0:T(8,128)S(1)}, s32[512,512]{1,0:T(8,128)}, u32[]{:S(2)}) copy-start(s32[512,512]{1,0:T(8,128)} %param.6) | copy-start | bytes 3145732
  8.7 13.1 %collective-permute-start.8 = (bf16[128,1024]{0,1:T(8,128)(2,1)}, bf16[128,1024]{0,1:T(8,128)(2,1)}, u32[]{:S(2)}, u32[]{:S(2)}) collective-permute-start(bf16[128,1024]{0,1:T(8,128)(2,1)} %bitcast.11), channel_id=1, source_target_pairs={{0,96},{1,97},{4,100},{5,101},{8,104},{9,105},{12,108},{13,109},{1... | collective-permute-start | bytes 786440 | tf_op jit(solution)/shard_map/ppermute | solution.py:21
  8.9 15.9 %collective-permute-start.7 = (bf16[128,1024]{0,1:T(8,128)(2,1)}, bf16[128,1024]{0,1:T(8,128)(2,1)}, u32[]{:S(2)}, u32[]{:S(2)}) collective-permute-start(bf16[128,1024]{0,1:T(8,128)(2,1)} %bitcast.10), channel_id=1, source_target_pairs={{0,32},{1,33},{4,36},{5,37},{8,40},{9,41},{12,44},{13,45},{16,48},... | collective-permute-start | bytes 786440 | tf_op jit(solution)/shard_map/ppermute | solution.py:21
  12.3 13.9 %collective-permute-start.9 = (bf16[128,1024]{0,1:T(8,128)(2,1)S(1)}, bf16[128,1024]{0,1:T(8,128)(2,1)S(1)}, u32[]{:S(2)}, u32[]{:S(2)}) collective-permute-start(bf16[128,1024]{0,1:T(8,128)(2,1)S(1)} %bitcast.54), channel_id=1, source_target_pairs={{0,64},{1,65},{4,68},{5,69},{8,72},{9,73},{12,76},{13,77},{16,80},... | collective-permute-start | bytes 786440 | tf_op jit(solution)/shard_map/ppermute | solution.py:21
  21.8 10.6 %collective-permute-start = (bf16[512,512]{1,0:T(8,128)(2,1)}, bf16[512,512]{1,0:T(8,128)(2,1)S(1)}, u32[]{:S(2)}, u32[]{:S(2)}) collective-permute-start(bf16[512,512]{1,0:T(8,128)(2,1)} %multiply_convert_fusion), channel_id=1, source_target_pairs={{0,128},{1,131},{4,132},{5,135},{8,136},{9,139},{12,140},{13,143},... | collective-permute-start | bytes 1572872 | tf_op jit(solution)/shard_map/ppermute | solution.py:21
  27.8 9.8 %collective-permute-start.10 = (bf16[2,8,2,16,512]{4,3,1,0,2:T(8,128)(2,1)S(1)}, bf16[2,8,2,16,512]{4,3,1,0,2:T(8,128)(2,1)S(1)}, u32[]{:S(2)}, u32[]{:S(2)}) collective-permute-start(bf16[2,8,2,16,512]{4,3,1,0,2:T(8,128)(2,1)S(1)} %fusion.4), channel_id=1, source_target_pairs={{0,1},{1,0},{4,5},{5,4},{8,9},{9,8},{12,13},{13,12},{16,17},{17,16... | collective-permute-start | bytes 1572872 | tf_op jit(solution)/shard_map/ppermute | solution.py:21
  34.0 28.3 %collective-permute-start.2 = (bf16[128,1024]{0,1:T(8,128)(2,1)S(1)}, bf16[128,1024]{0,1:T(8,128)(2,1)S(1)}, u32[]{:S(2)}, u32[]{:S(2)}) collective-permute-start(bf16[128,1024]{0,1:T(8,128)(2,1)S(1)} %fusion), channel_id=1, source_target_pairs={{0,96},{1,97},{4,100},{5,101},{8,104},{9,105},{12,108},{13,109},{1... | collective-permute-start | bytes 786440 | tf_op jit(solution)/shard_map/ppermute | solution.py:21
  35.5 27.4 %collective-permute-start.4 = (bf16[128,1024]{0,1:T(8,128)(2,1)S(1)}, bf16[128,1024]{0,1:T(8,128)(2,1)S(1)}, u32[]{:S(2)}, u32[]{:S(2)}) collective-permute-start(bf16[128,1024]{0,1:T(8,128)(2,1)S(1)} %fusion.1), channel_id=1, source_target_pairs={{0,32},{1,33},{4,36},{5,37},{8,40},{9,41},{12,44},{13,45},{16,48},... | collective-permute-start | bytes 786440 | tf_op jit(solution)/shard_map/ppermute | solution.py:21
  37.8 19.1 %copy-start.2 = (bf16[128,512]{1,0:T(8,128)(2,1)S(1)}, bf16[128,512]{1,0:T(8,128)(2,1)}, u32[]{:S(2)}) copy-start(bf16[128,512]{1,0:T(8,128)(2,1)} %param.5) | copy-start | bytes 393220
  37.8 6.3 %collective-permute-start.11 = (bf16[8,16,512]{2,1,0:T(8,128)(2,1)S(1)}, bf16[8,16,512]{2,1,0:T(8,128)(2,1)S(1)}, u32[]{:S(2)}, u32[]{:S(2)}) collective-permute-start(bf16[8,16,512]{2,1,0:T(8,128)(2,1)S(1)} %get-tuple-element.8), channel_id=1, source_target_pairs={{0,128},{1,129},{4,132},{5,133},{8,136},{9,137},{12,140},{13,141},... | collective-permute-start | bytes 393224 | tf_op jit(solution)/shard_map/ppermute | solution.py:21
  38.2 6.8 %collective-permute-start.12 = (bf16[8,16,512]{2,1,0:T(8,128)(2,1)S(1)}, bf16[8,16,512]{2,1,0:T(8,128)(2,1)S(1)}, u32[]{:S(2)}, u32[]{:S(2)}) collective-permute-start(bf16[8,16,512]{2,1,0:T(8,128)(2,1)S(1)} %get-tuple-element.10), channel_id=1, source_target_pairs={{0,130},{1,131},{4,134},{5,135},{8,138},{9,139},{12,142},{13,143},... | collective-permute-start | bytes 393224 | tf_op jit(solution)/shard_map/ppermute | solution.py:21
  41.1 6.5 %collective-permute-start.13 = (bf16[8,16,512]{2,1,0:T(8,128)(2,1)S(1)}, bf16[8,16,512]{2,1,0:T(8,128)(2,1)S(1)}, u32[]{:S(2)}, u32[]{:S(2)}) collective-permute-start(bf16[8,16,512]{2,1,0:T(8,128)(2,1)S(1)} %get-tuple-element.9), channel_id=1, source_target_pairs={{0,2},{1,3},{4,6},{5,7},{8,10},{9,11},{12,14},{13,15},{16,18},{17,... | collective-permute-start | bytes 393224 | tf_op jit(solution)/shard_map/ppermute | solution.py:21
  44.1 19.3 %collective-permute-start.6 = (bf16[128,1024]{0,1:T(8,128)(2,1)}, bf16[128,1024]{0,1:T(8,128)(2,1)S(1)}, u32[]{:S(2)}, u32[]{:S(2)}) collective-permute-start(bf16[128,1024]{0,1:T(8,128)(2,1)} %fusion.2), channel_id=1, source_target_pairs={{0,64},{1,65},{4,68},{5,69},{8,72},{9,73},{12,76},{13,77},{16,80},... | collective-permute-start | bytes 786440 | tf_op jit(solution)/shard_map/ppermute | solution.py:21
  48.3 30.0 %all-to-all-start = ((bf16[8,16,512]{2,1,0:T(8,128)(2,1)}), bf16[8,16,512]{2,1,0:T(8,128)(2,1)S(1)}, u32[]{:S(2)}, u32[]{:S(2)}) async-start(bf16[8,16,512]{2,1,0:T(8,128)(2,1)} %fusion.7), calls=%async_computation | async-start | bytes 262144 | tf_op jit(solution)/shard_map/all_to_all | solution.py:84

commit v2 on v1

v2 whole, which is shorter than its diff:
```python
import functools
import math

import jax
import jax.numpy as jnp
from jax import lax
from jax.experimental import pallas as pl
from jax.experimental.pallas import tpu as pltpu
from jax.sharding import Mesh
from jax.sharding import PartitionSpec as P

NYL, NX, NZ, NYH, NC = 2, 4, 8, 2, 2
NY = NYL * NYH
AXES = ("yl", "x", "z", "yh", "c")
BF16, F32 = jnp.bfloat16, jnp.float32


def device(x, y, z, c):
    x, y, z = x % NX, y % NY, z % NZ
    return (((y % NYL * NX + x) * NZ + z) * NYH + y // NYL) * NC + c


def moved(value, step):
    places = [(x, y, z, c) for x in range(NX) for y in range(NY) for z in range(NZ) for c in range(NC)]
    return lax.ppermute(value, AXES, [(device(*p), device(*step(*p))) for p in places])


def along_x(value, by):
    return moved(value, lambda x, y, z, c: (x + by, y, z, c))


def along_y(value, by):
    return moved(value, lambda x, y, z, c: (x, y + by, z, c))


def to_other_core(value):
    return moved(value, lambda x, y, z, c: (x, y, z, 1 - c))


def call(kernel, outs, place, *arrays, flops=0):
    moved_bytes = sum(a.size * a.dtype.itemsize for a in arrays)
    return pl.pallas_call(
        kernel,
        out_shape=outs,
        in_specs=[pl.BlockSpec(memory_space=pltpu.SMEM)]
        + [pl.BlockSpec(memory_space=pltpu.VMEM)] * len(arrays),
        out_specs=jax.tree.map(lambda _: pl.BlockSpec(memory_space=pltpu.VMEM), outs),
        cost_estimate=pl.CostEstimate(flops=flops, bytes_accessed=moved_bytes, transcendentals=0),
        compiler_params=pltpu.CompilerParams(vmem_limit_bytes=32 * 2**20),
    )(place, *arrays)


def start(multiple, factor):
    return pl.multiple_of(multiple * factor, factor)


def pack_kernel(rows, place_ref, acts_ref, *out_refs):
    x, c = place_ref[0], place_ref[2]
    half = rows // NC
    unit = rows // (NZ * NYH * NC)
    row = lax.broadcasted_iota(jnp.int32, (rows, rows), 0)
    col = lax.broadcasted_iota(jnp.int32, (rows, rows), 1)
    part, yh, rest = col // half, col % half // (half // NYH), col % (half // NYH)
    core = jnp.where(part == 0, c, 1 - c)
    source = ((rest // unit * NYH + yh) * NC + core) * unit + rest % unit
    order = (row == source).astype(F32).astype(BF16)
    for s, out in enumerate(out_refs):
        chip = lax.rem(x + s, NX)
        for yl in range(NYL):
            block = acts_ref[:, pl.ds(start(yl * NX + chip, rows), rows)]
            both = jnp.dot(block, order, preferred_element_type=F32).astype(BF16)
            out[0, :, yl * half : (yl + 1) * half] = both[:, :half]
            out[1, :, yl * half : (yl + 1) * half] = both[:, half:]


def pieces_kernel(place_ref, own_ref, other_ref, *refs):
    yl = lax.rem(place_ref[1], NYL)
    rows = own_ref.shape[0]
    n = len(refs) // 2
    for cot, out in zip(refs[:n], refs[n:]):
        for weight, at in ((own_ref, yl), (other_ref, 1 - yl)):
            product = lax.dot_general(
                cot[...], weight[...], (((1,), (1,)), ((), ())), preferred_element_type=F32
            )
            out[:, pl.ds(start(at, rows), rows)] = product.astype(BF16)


def laid_kernel(rows, place_ref, *refs):
    x = place_ref[0]
    out = refs[-1]
    for s, piece in enumerate(refs[:-1]):
        chip = lax.rem(x + s, NX)
        for yl in range(NYL):
            out[:, pl.ds(start(yl * NX + chip, rows), rows)] = piece[:, yl * rows : (yl + 1) * rows]


def terms_kernel(factor, place_ref, *refs):
    y = place_ref[1]
    outs = refs[-NY:]
    n = len(refs[:-NY]) // 4
    kept, swapped, cots, cots_swapped = (refs[k * n : (k + 1) * n] for k in range(4))
    rows = outs[0].shape[0]
    for s, out in enumerate(outs):
        to = lax.rem(y + s, NY)
        at = pl.ds(start(lax.rem(to, NYL) * NYH + to // NYL, rows), rows)
        total = None
        for a, b, g, h in zip(kept, swapped, cots, cots_swapped):
            left = jnp.concatenate([a[0, :, at], b[:, at]], axis=0)
            right = jnp.concatenate([g[...], h[...]], axis=0)
            term = lax.dot_general(
                left, right, (((0,), (0,)), ((), ())), preferred_element_type=F32
            )
            total = term if total is None else total + term
        out[...] = (total * factor).astype(out.dtype)


def per_device(acts, grad_out, codes, scales):
    tokens, width = acts.shape
    rows, kv = codes.shape
    yl, x, yh, c = (lax.axis_index(a) for a in ("yl", "x", "yh", "c"))
    place = jnp.stack([x, NYL * yh + yl, c]).astype(jnp.int32)
    factor = 1.0 / math.sqrt(tokens * NYL * NX * NZ * NYH * NC)
    shifts = (1, 2, 3)
    shape = jax.ShapeDtypeStruct

    cots = [grad_out] + [along_x(grad_out, s) for s in shifts]

    packed = call(
        functools.partial(pack_kernel, rows),
        [shape((NC, tokens, NYL * rows // NC), BF16)] * NX,
        place,
        acts,
    )
    columns = [packed[0]] + [along_x(packed[s], s) for s in shifts]

    blocks = codes.astype(F32).reshape(rows // 2, 2 * kv) * scales[:, None]
    own = blocks.reshape(rows, kv).astype(BF16)
    other = moved(own, lambda x, y, z, c: (x, y + 1 - 2 * c, z, c))

    pieces = call(
        pieces_kernel, [shape((tokens, NYL * rows), BF16)] * NX, place, own, other, *cots
    )
    pieces = [pieces[0]] + [along_x(pieces[s], -s) for s in shifts]
    grad_in = call(
        functools.partial(laid_kernel, rows), shape((tokens, width), BF16), place, *pieces
    )

    cots_swapped = [to_other_core(g) for g in cots]
    swapped = [to_other_core(a[1]) for a in columns]
    part = rows * NYL // NC // NY
    terms = call(
        functools.partial(terms_kernel, factor),
        [shape((part, kv), F32)] + [shape((part, kv), BF16)] * (NY - 1),
        place,
        *columns,
        *swapped,
        *cots,
        *cots_swapped,
    )
    column = terms[0]
    for s in shifts:
        column = column + along_y(terms[s], s).astype(F32)
    column = column.astype(BF16).reshape(NZ, part // NZ, kv)
    ring = lax.all_to_all(column, "z", split_axis=0, concat_axis=0, tiled=True)
    grad_w = ring.astype(F32).sum(axis=0)
    return (grad_in, grad_w)


def solution(mesh):
    fine = Mesh(mesh.devices.reshape(NYL, NX, NZ, NYH, NC), AXES)
    in_specs = (P(AXES, None), P(AXES, None), P(("yl", "x"), None), P(("yl", "x")))
    out_specs = (P(AXES, None), P(AXES, None))
    return jax.shard_map(
        per_device, mesh=fine, in_specs=in_specs, out_specs=out_specs, check_vma=False
    )
```

time: 79.3 us -> 72.9 us (0.919)
  the two profiles are of different devices: /device:TPU:34 before, /device:TPU:25 now
where the time goes in v2:
time: 72.9 us; the launch traced here: 72.7 us
  waiting for transfers between devices  36.7 us (50%)
  starting transfers between devices  25.2 us (35%)
  Pallas kernels  6.21 us (9%)
  local copies, waits for them, and re-layouts  2.17 us (3%)
  other arithmetic  1.62 us (2%)
  between operations  0.75 us (1%)
    ppermute x21, waiting for transfers between devices, moved(): lax.ppermute(value, AXES, [(device(*p), device(*step(*p))) for p in places])  32 us
    ppermute x21, starting transfers between devices, moved(): lax.ppermute(value, AXES, [(device(*p), device(*step(*p))) for p in places])  17 us
    all_to_all x1, starting transfers between devices, per_device(): ring = lax.all_to_all(column, 'z', split_axis=0, concat_axis=0, tiled=True)  8.18 us
    pallas_call x4, Pallas kernels, call(): pl.pallas_call(kernel, out_shape=outs, in_specs=[pl.BlockSpec(memory_spac...  6.21 us
    all_to_all x1, waiting for transfers between devices, per_device(): ring = lax.all_to_all(column, 'z', split_axis=0, concat_axis=0, tiled=True)  4.72 us
    unnamed x8, local copies, waits for them, and re-layouts  1.9 us
  transfers between devices with their start and end apart: 22, of which 11 were waited for; matrix products, arithmetic and copies ran while one was open for 2% of the time, Pallas kernels for 5%

profile of v2, /device:TPU:25, one launch (start us, length us, event | category | flops | bytes accessed | tf_op | source)
XLA Modules:
  0.0 72.7 jit_solution(16991426623633479931)
XLA Ops:
  0.7 1.2 %copy-done = bf16[128,4096]{1,0:T(8,128)(2,1)S(1)} copy-done((bf16[128,4096]{1,0:T(8,128)(2,1)S(1)}, bf16[128,4096]{1,0:T(8,128)(2,1)}, u32[]{:S(2)}) %copy-start) | copy-done | bytes 1048600
  1.9 1.3 %shard_map.61 = (bf16[2,128,512]{2,1,0:T(8,128)(2,1)S(1)}, bf16[2,128,512]{2,1,0:T(8,128)(2,1)S(1)}, bf16[2,128,512]{2,1,0:T(8,128)(2,1)S(1)}, bf16[2,128,512]{2,1,0:T(8,128)(2,1)S(1)}) custom-call(s32[3]{0:T(128)S(1)} %pad_add_fusion.place_ref, bf16[128,4096]{1,0:T(8,128)(2,1)S(1)} %copy-done), custom_call_target="tpu_custom_call" | custom-call | bytes 1048576 | tf_op jit(solution)/shard_map/pallas_call | solution.py:42
  3.2 1.3 %collective-permute-start.7 = (bf16[2,128,512]{2,1,0:T(8,128)(2,1)S(1)}, bf16[2,128,512]{2,1,0:T(8,128)(2,1)S(1)}, u32[]{:S(2)}, u32[]{:S(2)}) collective-permute-start(bf16[2,128,512]{2,1,0:T(8,128)(2,1)S(1)} %get-tuple-element.19), channel_id=1, source_target_pairs={{0,32},{1,33},{4,36},{5,37},{8,40},{9,41},{12,44},{13,45},{16,48},... | collective-permute-start | bytes 786440 | tf_op jit(solution)/shard_map/ppermute | solution.py:25
  4.5 1.2 %collective-permute-start.1 = (bf16[128,512]{1,0:T(8,128)(2,1)S(1)}, bf16[128,512]{1,0:T(8,128)(2,1)S(1)}, u32[]{:S(2)}, u32[]{:S(2)}) collective-permute-start(bf16[128,512]{1,0:T(8,128)(2,1)S(1)} %copy-done.1), channel_id=1, source_target_pairs={{0,32},{1,33},{4,36},{5,37},{8,40},{9,41},{12,44},{13,45},{16,48},... | collective-permute-start | bytes 393224 | tf_op jit(solution)/shard_map/ppermute | solution.py:25
  5.8 1.4 %collective-permute-start.2 = (bf16[128,512]{1,0:T(8,128)(2,1)S(1)}, bf16[128,512]{1,0:T(8,128)(2,1)S(1)}, u32[]{:S(2)}, u32[]{:S(2)}) collective-permute-start(bf16[128,512]{1,0:T(8,128)(2,1)S(1)} %copy-done.1), channel_id=1, source_target_pairs={{0,64},{1,65},{4,68},{5,69},{8,72},{9,73},{12,76},{13,77},{16,80},... | collective-permute-start | bytes 393224 | tf_op jit(solution)/shard_map/ppermute | solution.py:25
  7.2 1.9 %collective-permute-start.3 = (bf16[128,512]{1,0:T(8,128)(2,1)S(1)}, bf16[128,512]{1,0:T(8,128)(2,1)S(1)}, u32[]{:S(2)}, u32[]{:S(2)}) collective-permute-start(bf16[128,512]{1,0:T(8,128)(2,1)S(1)} %copy-done.1), channel_id=1, source_target_pairs={{0,96},{1,97},{4,100},{5,101},{8,104},{9,105},{12,108},{13,109},{1... | collective-permute-start | bytes 393224 | tf_op jit(solution)/shard_map/ppermute | solution.py:25
  10.5 1.2 %collective-permute-done.7.refs_1_ = bf16[2,128,512]{2,1,0:T(8,128)(2,1)S(1)} collective-permute-done((bf16[2,128,512]{2,1,0:T(8,128)(2,1)S(1)}, bf16[2,128,512]{2,1,0:T(8,128)(2,1)S(1)}, u32[]{:S(2)}, u32[]{:S(2)}) %collective-permute-start.7) | collective-permute-done | bytes 262176 | tf_op jit(solution)/shard_map/ppermute | solution.py:25
  11.7 1.3 %collective-permute-start.9 = (bf16[2,128,512]{2,1,0:T(8,128)(2,1)S(1)}, bf16[2,128,512]{2,1,0:T(8,128)(2,1)S(1)}, u32[]{:S(2)}, u32[]{:S(2)}) collective-permute-start(bf16[2,128,512]{2,1,0:T(8,128)(2,1)S(1)} %get-tuple-element.21), channel_id=1, source_target_pairs={{0,96},{1,97},{4,100},{5,101},{8,104},{9,105},{12,108},{13,109},{1... | collective-permute-start | bytes 786440 | tf_op jit(solution)/shard_map/ppermute | solution.py:25
  13.0 10.9 %collective-permute-done.8.refs_2_ = bf16[2,128,512]{2,1,0:T(8,128)(2,1)S(1)} collective-permute-done((bf16[2,128,512]{2,1,0:T(8,128)(2,1)S(1)}, bf16[2,128,512]{2,1,0:T(8,128)(2,1)S(1)}, u32[]{:S(2)}, u32[]{:S(2)}) %collective-permute-start.8) | collective-permute-done | bytes 262176 | tf_op jit(solution)/shard_map/ppermute | solution.py:25
  23.9 1.6 %collective-permute-start.14 = (bf16[128,512]{1,0:T(8,128)(2,1)S(1)}, bf16[128,512]{1,0:T(8,128)(2,1)S(1)}, u32[]{:S(2)}, u32[]{:S(2)}) collective-permute-start(bf16[128,512]{1,0:T(8,128)(2,1)S(1)} %copy-done.1), channel_id=1, source_target_pairs={{0,1},{1,0},{4,5},{5,4},{8,9},{9,8},{12,13},{13,12},{16,17},{17,16... | collective-permute-start | bytes 393224 | tf_op jit(solution)/shard_map/ppermute | solution.py:25
  28.8 1.3 %shard_map.62 = (f32[128,512]{1,0:T(8,128)S(1)}, bf16[128,512]{1,0:T(8,128)(2,1)S(1)}, bf16[128,512]{1,0:T(8,128)(2,1)S(1)}, bf16[128,512]{1,0:T(8,128)(2,1)S(1)}) custom-call(s32[3]{0:T(128)S(1)} %pad_add_fusion.place_ref, bf16[2,128,512]{2,1,0:T(8,128)(2,1)S(1)} %get-tuple-element.18.refs_0_, bf16[2,128,512]{2,1,0:T(8,128)(2,1)S(1)} %collective-permute-done.7.refs_1_, ...), custom_call_target="tpu_custom_call" | custom-call | bytes 2621440 | tf_op jit(solution)/shard_map/pallas_call | solution.py:42
  30.1 1.9 %collective-permute-start.18 = (bf16[128,512]{1,0:T(8,128)(2,1)S(1)}, bf16[128,512]{1,0:T(8,128)(2,1)S(1)}, u32[]{:S(2)}, u32[]{:S(2)}) collective-permute-start(bf16[128,512]{1,0:T(8,128)(2,1)S(1)} %get-tuple-element.23), channel_id=1, source_target_pairs={{0,128},{1,129},{4,132},{5,133},{8,136},{9,137},{12,140},{13,141},... | collective-permute-start | bytes 393224 | tf_op jit(solution)/shard_map/ppermute | solution.py:25
  32.9 2.9 %collective-permute-done.18 = bf16[128,512]{1,0:T(8,128)(2,1)S(1)} collective-permute-done((bf16[128,512]{1,0:T(8,128)(2,1)S(1)}, bf16[128,512]{1,0:T(8,128)(2,1)S(1)}, u32[]{:S(2)}, u32[]{:S(2)}) %collective-permute-start.18) | collective-permute-done | bytes 131104 | tf_op jit(solution)/shard_map/ppermute | solution.py:25
  35.8 3.2 %collective-permute-done.19 = bf16[128,512]{1,0:T(8,128)(2,1)S(1)} collective-permute-done((bf16[128,512]{1,0:T(8,128)(2,1)S(1)}, bf16[128,512]{1,0:T(8,128)(2,1)S(1)}, u32[]{:S(2)}, u32[]{:S(2)}) %collective-permute-start.19) | collective-permute-done | bytes 131104 | tf_op jit(solution)/shard_map/ppermute | solution.py:25
  39.0 3.8 %collective-permute-done.20 = bf16[128,512]{1,0:T(8,128)(2,1)S(1)} collective-permute-done((bf16[128,512]{1,0:T(8,128)(2,1)S(1)}, bf16[128,512]{1,0:T(8,128)(2,1)S(1)}, u32[]{:S(2)}, u32[]{:S(2)}) %collective-permute-start.20) | collective-permute-done | bytes 131104 | tf_op jit(solution)/shard_map/ppermute | solution.py:25
  42.8 0.7 add_convert_fusion
  43.5 8.2 %all-to-all-start = ((bf16[8,16,512]{2,1,0:T(8,128)(2,1)}), bf16[8,16,512]{2,1,0:T(8,128)(2,1)S(1)}, u32[]{:S(2)}, u32[]{:S(2)}) async-start(bf16[8,16,512]{2,1,0:T(8,128)(2,1)} %bitcast.7), calls=%async_computation | async-start | bytes 262144 | tf_op jit(solution)/shard_map/all_to_all | solution.py:164
  51.7 2.0 %shard_map.59 = (bf16[128,1024]{1,0:T(8,128)(2,1)S(1)}, bf16[128,1024]{1,0:T(8,128)(2,1)S(1)}, bf16[128,1024]{1,0:T(8,128)(2,1)S(1)}, bf16[128,1024]{1,0:T(8,128)(2,1)S(1)}) custom-call(s32[3]{0:T(128)S(1)} %pad_add_fusion.place_ref, bf16[512,512]{1,0:T(8,128)(2,1)S(1)} %multiply_convert_fusion.own_ref, bf16[512,512]{1,0:T(8,128)(2,1)S(1)} %collective-permute-done.other_ref, ...), custom_call_target="tpu_custom_call" | custom-call | bytes 1572864 | tf_op jit(solution)/shard_map/pallas_call | solution.py:42
  53.7 2.0 %collective-permute-start.4 = (bf16[128,1024]{1,0:T(8,128)(2,1)S(1)}, bf16[128,1024]{1,0:T(8,128)(2,1)S(1)}, u32[]{:S(2)}, u32[]{:S(2)}) collective-permute-start(bf16[128,1024]{1,0:T(8,128)(2,1)S(1)} %get-tuple-element.15), channel_id=1, source_target_pairs={{0,96},{1,97},{4,100},{5,101},{8,104},{9,105},{12,108},{13,109},{1... | collective-permute-start | bytes 786440 | tf_op jit(solution)/shard_map/ppermute | solution.py:25
  55.7 0.7 collective-permute-start.5
  56.5 4.7 %all-to-all-done = bf16[8,16,512]{2,1,0:T(8,128)(2,1)S(1)} async-done(((bf16[8,16,512]{2,1,0:T(8,128)(2,1)}), bf16[8,16,512]{2,1,0:T(8,128)(2,1)S(1)}, u32[]{:S(2)}, u32[]{:S(2)}) %all-to-all-start) | async-done | bytes 131104 | tf_op jit(solution)/shard_map/all_to_all | solution.py:164
  61.9 5.2 %collective-permute-done.4.refs_1_ = bf16[128,1024]{1,0:T(8,128)(2,1)S(1)} collective-permute-done((bf16[128,1024]{1,0:T(8,128)(2,1)S(1)}, bf16[128,1024]{1,0:T(8,128)(2,1)S(1)}, u32[]{:S(2)}, u32[]{:S(2)}) %collective-permute-start.4) | collective-permute-done | bytes 262176 | tf_op jit(solution)/shard_map/ppermute | solution.py:25
  67.1 4.0 %collective-permute-done.6.refs_3_ = bf16[128,1024]{1,0:T(8,128)(2,1)S(1)} collective-permute-done((bf16[128,1024]{1,0:T(8,128)(2,1)S(1)}, bf16[128,1024]{1,0:T(8,128)(2,1)S(1)}, u32[]{:S(2)}, u32[]{:S(2)}) %collective-permute-start.6) | collective-permute-done | bytes 262176 | tf_op jit(solution)/shard_map/ppermute | solution.py:25
  71.1 1.6 %shard_map.60 = bf16[128,4096]{1,0:T(8,128)(2,1)} custom-call(s32[3]{0:T(128)S(1)} %pad_add_fusion.place_ref, bf16[128,1024]{1,0:T(8,128)(2,1)S(1)} %get-tuple-element.14.refs_0_, bf16[128,1024]{1,0:T(8,128)(2,1)S(1)} %collective-permute-done.4.refs_1_, bf16[128,1024]{1,0:T(8,128)(2,1)S(1)} %collective-permute-done.5.refs_2_, ...), custom_call_target="tpu_custom_call" | custom-call | bytes 1048576 | tf_op jit(solution)/shard_map/pallas_call | solution.py:42
  (42 shorter events, 6.4 us)
Async XLA Ops:
  1.9 2.6 %copy-start.1 = (bf16[128,512]{1,0:T(8,128)(2,1)S(1)}, bf16[128,512]{1,0:T(8,128)(2,1)}, u32[]{:S(2)}) copy-start(bf16[128,512]{1,0:T(8,128)(2,1)} %refs_8_.1) | copy-start | bytes 393220
  1.9 25.7 %copy-start.2 = (s32[512,512]{1,0:T(8,128)S(1)}, s32[512,512]{1,0:T(8,128)}, u32[]{:S(2)}) copy-start(s32[512,512]{1,0:T(8,128)} %param.6) | copy-start | bytes 3145732
  3.2 8.5 %collective-permute-start.7 = (bf16[2,128,512]{2,1,0:T(8,128)(2,1)S(1)}, bf16[2,128,512]{2,1,0:T(8,128)(2,1)S(1)}, u32[]{:S(2)}, u32[]{:S(2)}) collective-permute-start(bf16[2,128,512]{2,1,0:T(8,128)(2,1)S(1)} %get-tuple-element.19), channel_id=1, source_target_pairs={{0,32},{1,33},{4,36},{5,37},{8,40},{9,41},{12,44},{13,45},{16,48},... | collective-permute-start | bytes 786440 | tf_op jit(solution)/shard_map/ppermute | solution.py:25
  4.5 21.0 %collective-permute-start.1 = (bf16[128,512]{1,0:T(8,128)(2,1)S(1)}, bf16[128,512]{1,0:T(8,128)(2,1)S(1)}, u32[]{:S(2)}, u32[]{:S(2)}) collective-permute-start(bf16[128,512]{1,0:T(8,128)(2,1)S(1)} %copy-done.1), channel_id=1, source_target_pairs={{0,32},{1,33},{4,36},{5,37},{8,40},{9,41},{12,44},{13,45},{16,48},... | collective-permute-start | bytes 393224 | tf_op jit(solution)/shard_map/ppermute | solution.py:25
  5.8 19.9 %collective-permute-start.2 = (bf16[128,512]{1,0:T(8,128)(2,1)S(1)}, bf16[128,512]{1,0:T(8,128)(2,1)S(1)}, u32[]{:S(2)}, u32[]{:S(2)}) collective-permute-start(bf16[128,512]{1,0:T(8,128)(2,1)S(1)} %copy-done.1), channel_id=1, source_target_pairs={{0,64},{1,65},{4,68},{5,69},{8,72},{9,73},{12,76},{13,77},{16,80},... | collective-permute-start | bytes 393224 | tf_op jit(solution)/shard_map/ppermute | solution.py:25
  7.2 18.9 %collective-permute-start.3 = (bf16[128,512]{1,0:T(8,128)(2,1)S(1)}, bf16[128,512]{1,0:T(8,128)(2,1)S(1)}, u32[]{:S(2)}, u32[]{:S(2)}) collective-permute-start(bf16[128,512]{1,0:T(8,128)(2,1)S(1)} %copy-done.1), channel_id=1, source_target_pairs={{0,96},{1,97},{4,100},{5,101},{8,104},{9,105},{12,108},{13,109},{1... | collective-permute-start | bytes 393224 | tf_op jit(solution)/shard_map/ppermute | solution.py:25
  9.1 14.9 %collective-permute-start.8 = (bf16[2,128,512]{2,1,0:T(8,128)(2,1)S(1)}, bf16[2,128,512]{2,1,0:T(8,128)(2,1)S(1)}, u32[]{:S(2)}, u32[]{:S(2)}) collective-permute-start(bf16[2,128,512]{2,1,0:T(8,128)(2,1)S(1)} %get-tuple-element.20), channel_id=1, source_target_pairs={{0,64},{1,65},{4,68},{5,69},{8,72},{9,73},{12,76},{13,77},{16,80},... | collective-permute-start | bytes 786440 | tf_op jit(solution)/shard_map/ppermute | solution.py:25
  11.7 14.5 %collective-permute-start.9 = (bf16[2,128,512]{2,1,0:T(8,128)(2,1)S(1)}, bf16[2,128,512]{2,1,0:T(8,128)(2,1)S(1)}, u32[]{:S(2)}, u32[]{:S(2)}) collective-permute-start(bf16[2,128,512]{2,1,0:T(8,128)(2,1)S(1)} %get-tuple-element.21), channel_id=1, source_target_pairs={{0,96},{1,97},{4,100},{5,101},{8,104},{9,105},{12,108},{13,109},{1... | collective-permute-start | bytes 786440 | tf_op jit(solution)/shard_map/ppermute | solution.py:25
  23.9 3.2 %collective-permute-start.14 = (bf16[128,512]{1,0:T(8,128)(2,1)S(1)}, bf16[128,512]{1,0:T(8,128)(2,1)S(1)}, u32[]{:S(2)}, u32[]{:S(2)}) collective-permute-start(bf16[128,512]{1,0:T(8,128)(2,1)S(1)} %copy-done.1), channel_id=1, source_target_pairs={{0,1},{1,0},{4,5},{5,4},{8,9},{9,8},{12,13},{13,12},{16,17},{17,16... | collective-permute-start | bytes 393224 | tf_op jit(solution)/shard_map/ppermute | solution.py:25
  25.5 1.4 %collective-permute-start.10 = (bf16[128,512]{1,0:T(8,128)(2,1)S(1)}, bf16[128,512]{1,0:T(8,128)(2,1)S(1)}, u32[]{:S(2)}, u32[]{:S(2)}) collective-permute-start(bf16[128,512]{1,0:T(8,128)(2,1)S(1)} %slice_bitcast_fusion.3), channel_id=1, source_target_pairs={{0,1},{1,0},{4,5},{5,4},{8,9},{9,8},{12,13},{13,12},{16,17},{17,16... | collective-permute-start | bytes 393224 | tf_op jit(solution)/shard_map/ppermute | solution.py:25
  25.6 1.8 %collective-permute-start.15 = (bf16[128,512]{1,0:T(8,128)(2,1)S(1)}, bf16[128,512]{1,0:T(8,128)(2,1)S(1)}, u32[]{:S(2)}, u32[]{:S(2)}) collective-permute-start(bf16[128,512]{1,0:T(8,128)(2,1)S(1)} %collective-permute-done.1.refs_1_.refs_9_), channel_id=1, source_target_pairs={{0,1},{1,0},{4,5},{5,4},{8,9},{9,8},{12,13},{13,12},{16,17},{17,16... | collective-permute-start | bytes 393224 | tf_op jit(solution)/shard_map/ppermute | solution.py:25
  26.1 1.7 %collective-permute-start.16 = (bf16[128,512]{1,0:T(8,128)(2,1)S(1)}, bf16[128,512]{1,0:T(8,128)(2,1)S(1)}, u32[]{:S(2)}, u32[]{:S(2)}) collective-permute-start(bf16[128,512]{1,0:T(8,128)(2,1)S(1)} %collective-permute-done.2.refs_2_.refs_10_), channel_id=1, source_target_pairs={{0,1},{1,0},{4,5},{5,4},{8,9},{9,8},{12,13},{13,12},{16,17},{17,16... | collective-permute-start | bytes 393224 | tf_op jit(solution)/shard_map/ppermute | solution.py:25
  26.2 2.1 %collective-permute-start.17 = (bf16[128,512]{1,0:T(8,128)(2,1)S(1)}, bf16[128,512]{1,0:T(8,128)(2,1)S(1)}, u32[]{:S(2)}, u32[]{:S(2)}) collective-permute-start(bf16[128,512]{1,0:T(8,128)(2,1)S(1)} %collective-permute-done.3.refs_3_.refs_11_), channel_id=1, source_target_pairs={{0,1},{1,0},{4,5},{5,4},{8,9},{9,8},{12,13},{13,12},{16,17},{17,16... | collective-permute-start | bytes 393224 | tf_op jit(solution)/shard_map/ppermute | solution.py:25
  26.9 1.4 %collective-permute-start.11 = (bf16[128,512]{1,0:T(8,128)(2,1)S(1)}, bf16[128,512]{1,0:T(8,128)(2,1)S(1)}, u32[]{:S(2)}, u32[]{:S(2)}) collective-permute-start(bf16[128,512]{1,0:T(8,128)(2,1)S(1)} %slice_bitcast_fusion.2), channel_id=1, source_target_pairs={{0,1},{1,0},{4,5},{5,4},{8,9},{9,8},{12,13},{13,12},{16,17},{17,16... | collective-permute-start | bytes 393224 | tf_op jit(solution)/shard_map/ppermute | solution.py:25
  27.1 1.4 %collective-permute-start.12 = (bf16[128,512]{1,0:T(8,128)(2,1)S(1)}, bf16[128,512]{1,0:T(8,128)(2,1)S(1)}, u32[]{:S(2)}, u32[]{:S(2)}) collective-permute-start(bf16[128,512]{1,0:T(8,128)(2,1)S(1)} %slice_bitcast_fusion.1), channel_id=1, source_target_pairs={{0,1},{1,0},{4,5},{5,4},{8,9},{9,8},{12,13},{13,12},{16,17},{17,16... | collective-permute-start | bytes 393224 | tf_op jit(solution)/shard_map/ppermute | solution.py:25
  27.5 1.3 %collective-permute-start.13 = (bf16[128,512]{1,0:T(8,128)(2,1)S(1)}, bf16[128,512]{1,0:T(8,128)(2,1)S(1)}, u32[]{:S(2)}, u32[]{:S(2)}) collective-permute-start(bf16[128,512]{1,0:T(8,128)(2,1)S(1)} %slice_bitcast_fusion), channel_id=1, source_target_pairs={{0,1},{1,0},{4,5},{5,4},{8,9},{9,8},{12,13},{13,12},{16,17},{17,16... | collective-permute-start | bytes 393224 | tf_op jit(solution)/shard_map/ppermute | solution.py:25
  27.8 23.9 %collective-permute-start = (bf16[512,512]{1,0:T(8,128)(2,1)S(1)}, bf16[512,512]{1,0:T(8,128)(2,1)S(1)}, u32[]{:S(2)}, u32[]{:S(2)}) collective-permute-start(bf16[512,512]{1,0:T(8,128)(2,1)S(1)} %multiply_convert_fusion.own_ref), channel_id=1, source_target_pairs={{0,128},{1,131},{4,132},{5,135},{8,136},{9,139},{12,140},{13,143},... | collective-permute-start | bytes 1572872 | tf_op jit(solution)/shard_map/ppermute | solution.py:25
  30.1 5.7 %collective-permute-start.18 = (bf16[128,512]{1,0:T(8,128)(2,1)S(1)}, bf16[128,512]{1,0:T(8,128)(2,1)S(1)}, u32[]{:S(2)}, u32[]{:S(2)}) collective-permute-start(bf16[128,512]{1,0:T(8,128)(2,1)S(1)} %get-tuple-element.23), channel_id=1, source_target_pairs={{0,128},{1,129},{4,132},{5,133},{8,136},{9,137},{12,140},{13,141},... | collective-permute-start | bytes 393224 | tf_op jit(solution)/shard_map/ppermute | solution.py:25
  32.0 7.0 %collective-permute-start.19 = (bf16[128,512]{1,0:T(8,128)(2,1)S(1)}, bf16[128,512]{1,0:T(8,128)(2,1)S(1)}, u32[]{:S(2)}, u32[]{:S(2)}) collective-permute-start(bf16[128,512]{1,0:T(8,128)(2,1)S(1)} %get-tuple-element.24), channel_id=1, source_target_pairs={{0,2},{1,3},{4,6},{5,7},{8,10},{9,11},{12,14},{13,15},{16,18},{17,... | collective-permute-start | bytes 393224 | tf_op jit(solution)/shard_map/ppermute | solution.py:25
  32.5 10.3 %collective-permute-start.20 = (bf16[128,512]{1,0:T(8,128)(2,1)S(1)}, bf16[128,512]{1,0:T(8,128)(2,1)S(1)}, u32[]{:S(2)}, u32[]{:S(2)}) collective-permute-start(bf16[128,512]{1,0:T(8,128)(2,1)S(1)} %get-tuple-element.25), channel_id=1, source_target_pairs={{0,130},{1,131},{4,134},{5,135},{8,138},{9,139},{12,142},{13,143},... | collective-permute-start | bytes 393224 | tf_op jit(solution)/shard_map/ppermute | solution.py:25
  43.5 17.8 %all-to-all-start = ((bf16[8,16,512]{2,1,0:T(8,128)(2,1)}), bf16[8,16,512]{2,1,0:T(8,128)(2,1)S(1)}, u32[]{:S(2)}, u32[]{:S(2)}) async-start(bf16[8,16,512]{2,1,0:T(8,128)(2,1)} %bitcast.7), calls=%async_computation | async-start | bytes 262144 | tf_op jit(solution)/shard_map/all_to_all | solution.py:164
  53.7 13.4 %collective-permute-start.4 = (bf16[128,1024]{1,0:T(8,128)(2,1)S(1)}, bf16[128,1024]{1,0:T(8,128)(2,1)S(1)}, u32[]{:S(2)}, u32[]{:S(2)}) collective-permute-start(bf16[128,1024]{1,0:T(8,128)(2,1)S(1)} %get-tuple-element.15), channel_id=1, source_target_pairs={{0,96},{1,97},{4,100},{5,101},{8,104},{9,105},{12,108},{13,109},{1... | collective-permute-start | bytes 786440 | tf_op jit(solution)/shard_map/ppermute | solution.py:25
  55.7 11.3 %collective-permute-start.5 = (bf16[128,1024]{1,0:T(8,128)(2,1)S(1)}, bf16[128,1024]{1,0:T(8,128)(2,1)S(1)}, u32[]{:S(2)}, u32[]{:S(2)}) collective-permute-start(bf16[128,1024]{1,0:T(8,128)(2,1)S(1)} %get-tuple-element.16), channel_id=1, source_target_pairs={{0,64},{1,65},{4,68},{5,69},{8,72},{9,73},{12,76},{13,77},{16,80},... | collective-permute-start | bytes 786440 | tf_op jit(solution)/shard_map/ppermute | solution.py:25
  56.4 14.6 %collective-permute-start.6 = (bf16[128,1024]{1,0:T(8,128)(2,1)S(1)}, bf16[128,1024]{1,0:T(8,128)(2,1)S(1)}, u32[]{:S(2)}, u32[]{:S(2)}) collective-permute-start(bf16[128,1024]{1,0:T(8,128)(2,1)S(1)} %get-tuple-element.17), channel_id=1, source_target_pairs={{0,32},{1,33},{4,36},{5,37},{8,40},{9,41},{12,44},{13,45},{16,48},... | collective-permute-start | bytes 786440 | tf_op jit(solution)/shard_map/ppermute | solution.py:25
  (2 other events, 1.9 us)

commit v3 on v2

v3 whole, which is shorter than its diff:
```python
import functools
import math

import jax
import jax.numpy as jnp
from jax import lax
from jax.experimental import pallas as pl
from jax.experimental.pallas import tpu as pltpu
from jax.sharding import Mesh
from jax.sharding import PartitionSpec as P

NYL, NX, NZ, NYH, NC = 2, 4, 8, 2, 2
NY = NYL * NYH
AXES = ("yl", "x", "z", "yh", "c")
BF16, F32 = jnp.bfloat16, jnp.float32


def device(x, y, z, c):
    x, y, z = x % NX, y % NY, z % NZ
    return (((y % NYL * NX + x) * NZ + z) * NYH + y // NYL) * NC + c


def moved(value, step):
    places = [(x, y, z, c) for x in range(NX) for y in range(NY) for z in range(NZ) for c in range(NC)]
    moves = [(device(*p), device(*step(*p))) for p in places if step(*p) is not None]
    return lax.ppermute(value, AXES, moves)


def in_first_ring(value, by):
    return moved(value, lambda x, y, z, c: (x, y + by, z, c) if c else (x + by, y, z, c))


def weights_moved(value, turn):
    def step(x, y, z, c):
        if c:
            return (x - turn, y, z, c)
        return None if turn == 3 else (x, y + (1 if turn == 2 else -1), z, c)

    return moved(value, step)


def in_other_ring(value, by):
    return moved(value, lambda x, y, z, c: (x + by, y, z, 0) if c else (x, y + by, z, 1))


def in_second_ring(value, by):
    return moved(value, lambda x, y, z, c: (x + by, y, z, c) if c else (x, y + by, z, c))


def to_other_core(value):
    return moved(value, lambda x, y, z, c: (x, y, z, 1 - c))


def call(kernel, outs, place, *arrays, after=(), spaces=None, scratch=(), vmem=12):
    def body(place_ref, *refs):
        kernel(place_ref, *refs[: len(arrays)], *refs[len(arrays) + len(after) :])

    spaces = spaces or [pltpu.VMEM] * len(arrays)

    moved_bytes = sum(a.size * a.dtype.itemsize for a in arrays)
    return pl.pallas_call(
        body,
        out_shape=outs,
        in_specs=[pl.BlockSpec(memory_space=pltpu.SMEM)]
        + [pl.BlockSpec(memory_space=space) for space in spaces]
        + [pl.BlockSpec(memory_space=pl.ANY)] * len(after),
        out_specs=jax.tree.map(lambda _: pl.BlockSpec(memory_space=pltpu.VMEM), outs),
        scratch_shapes=list(scratch),
        cost_estimate=pl.CostEstimate(flops=0, bytes_accessed=moved_bytes, transcendentals=0),
        compiler_params=pltpu.CompilerParams(vmem_limit_bytes=vmem * 2**20),
    )(place, *arrays, *after)


def start(multiple, factor):
    return pl.multiple_of(multiple * factor, factor)


def pack_kernel(rows, place_ref, acts_ref, cot_ref, *refs):
    own, swap, (acts_here, sorted_here, sems) = refs[:NX], refs[NX : 2 * NX], refs[2 * NX :]
    x, y, c = place_ref[0], place_ref[1], place_ref[2]
    ring = jnp.where(c == 0, x, y)
    other_ring = jnp.where(c == 0, y, x)
    blocks = NYL * NX
    copies = []
    for b in range(blocks):
        at = pl.ds(b * rows, rows)
        copies.append(pltpu.make_async_copy(acts_ref.at[:, at], acts_here.at[b], sems.at[b]))
    copies.append(pltpu.make_async_copy(cot_ref, own[0].at[1], sems.at[blocks]))
    for copy in copies:
        copy.start()
    unit = rows // (NZ * NYH * NC)
    bits = [n.bit_length() - 1 for n in (unit, NZ, NYH)]
    row = lax.broadcasted_iota(jnp.int32, (rows, rows), 0)
    col = lax.broadcasted_iota(jnp.int32, (1, rows), 1)
    low = col & (unit - 1)
    z = (col >> bits[0]) & (NZ - 1)
    yh = (col >> (bits[0] + bits[1])) & (NYH - 1)
    core = col >> (bits[0] + bits[1] + bits[2])
    source = (((z << bits[2]) | yh) * NC + core) * unit + low
    order = (row == source).astype(F32).astype(BF16)
    part = rows // (NC * NYH)
    tokens = acts_ref.shape[0]
    for yl in range(NYL):
        for b in range(yl * NX, (yl + 1) * NX):
            copies[b].wait()
        block = acts_here[yl * NX : (yl + 1) * NX].reshape(NX * tokens, rows)
        block = jnp.dot(block, order, preferred_element_type=F32).astype(BF16)
        block = block.reshape(NX, tokens, rows)
        for yh in range(NYH):
            yy = NYL * yh + yl
            at = yh * part
            sorted_here[0, :, :, yy * part : (yy + 1) * part] = block[:, :, at : at + part]
            at = (NYH + yh) * part
            for chip in range(NX):
                sorted_here[1, yy, :, chip * part : (chip + 1) * part] = block[chip, :, at : at + part]
    copies[blocks].wait()
    cot = own[0][1]
    for s in range(NX):
        own[s][0] = sorted_here[c, lax.rem(ring + s, NX)]
        swap[s][0] = sorted_here[1 - c, lax.rem(other_ring + s, NX)]
        swap[s][1] = cot
        if s:
            own[s][1] = cot


def weight_kernel(place_ref, codes_ref, scales_ref, out_ref, *refs):
    sent, (codes_here, sem) = refs[:2], refs[2:]
    c, yh = place_ref[2], place_ref[1] // NYL
    half = sent[0].shape[0]
    copy = pltpu.make_async_copy(codes_ref, codes_here, sem)
    copy.start()
    copy.wait()
    out_ref[...] = (codes_here[...].astype(F32) * scales_ref[...]).astype(BF16)
    for k, half_ref in enumerate(sent):
        half_ref[...] = out_ref[pl.ds(start(jnp.where(c == 0, k, yh), half), half), :]


def sum_kernel(place_ref, own_ref, *refs):
    total = own_ref[...]
    for part in refs[:-1]:
        total = total + part[...].astype(F32)
    refs[-1][...] = total.astype(BF16)


def last_kernel(place_ref, parts_ref, out_ref):
    out_ref[...] = parts_ref[...].astype(F32).sum(axis=0)


def pieces_kernel(place_ref, own_ref, *refs):
    arrived, refs, weight_ref = refs[:3], refs[3:-1], refs[-1]
    x, y, c = place_ref[0], place_ref[1], place_ref[2]
    yl, yh = lax.rem(y, NYL), y // NYL
    half = arrived[0].shape[0]
    on_0 = c == 0
    taken = [
        own_ref[pl.ds(start(jnp.where(on_0, 0, yh), half), half), :],
        jnp.where(on_0, own_ref[half:, :], arrived[0][...]),
        jnp.where(on_0, arrived[0][...], arrived[1][...]),
        jnp.where(on_0, arrived[1][...], arrived[2][...]),
    ]
    for k, part in enumerate(taken):
        first = 2 * jnp.where(k < 2, yl, 1 - yl) + k % 2
        at = jnp.where(on_0, first, lax.rem(x + k, NX))
        weight_ref[pl.ds(start(at, half), half), :] = part
    n = len(refs) // 2
    for block, out in zip(refs[:n], refs[n:]):
        out[...] = lax.dot_general(
            block[1], weight_ref[...], (((1,), (1,)), ((), ())), preferred_element_type=F32
        ).astype(BF16)


def laid_kernel(rows, place_ref, *refs):
    x, y, c = place_ref[0], place_ref[1], place_ref[2]
    out, done_ref = refs[-2:]
    done_ref[...] = jnp.zeros_like(done_ref)
    half = rows // 2
    for s, piece in enumerate(refs[:-2]):
        chip, other = lax.rem(x + s, NX), lax.rem(y + s, NY)
        for q in range(4):
            on_0 = ((q // 2) * NX + chip) * 2 + q % 2
            on_1 = (lax.rem(other, NYL) * NX + q) * 2 + other // NYL
            at = pl.ds(start(jnp.where(c == 0, on_0, on_1), half), half)
            out[:, at] = piece[:, q * half : (q + 1) * half]


def terms_kernel(factor, place_ref, *refs):
    x, y, c = place_ref[0], place_ref[1], place_ref[2]
    to = jnp.where(c == 0, y, x)
    first, second, outs = refs[:NX], refs[NX : 2 * NX], refs[2 * NX :]
    rows = outs[0].shape[0]
    for t, out in enumerate(outs):
        at = pl.ds(start(lax.rem(to + t, NY), rows), rows)
        total = None
        for a, b in zip(first, second):
            left = jnp.concatenate([a[0, :, at], b[0, :, at]], axis=0)
            right = jnp.concatenate([a[1], b[1]], axis=0)
            term = lax.dot_general(
                left, right, (((0,), (0,)), ((), ())), preferred_element_type=F32
            )
            total = term if total is None else total + term
        out[...] = (total * factor).astype(out.dtype)


def per_device(acts, grad_out, codes, scales):
    tokens, width = acts.shape
    rows, kv = codes.shape
    yl, x, yh, c = (lax.axis_index(a) for a in ("yl", "x", "yh", "c"))
    place = jnp.stack([x, NYL * yh + yl, c]).astype(jnp.int32)
    factor = 1.0 / math.sqrt(tokens * NYL * NX * NZ * NYH * NC)
    shifts = (1, 2, 3)
    shape = jax.ShapeDtypeStruct
    cols = rows * NYL // NC

    packed = call(
        functools.partial(pack_kernel, rows),
        [shape((2, tokens, cols), BF16)] * (2 * NX),
        place,
        acts,
        grad_out,
        spaces=[pltpu.HBM, pltpu.HBM],
        scratch=[
            pltpu.VMEM((NYL * NX, tokens, rows), BF16),
            pltpu.VMEM((NC, NX, tokens, cols), BF16),
            pltpu.SemaphoreType.DMA((NYL * NX + 1,)),
        ],
        vmem=60,
    )
    first = [packed[0]] + [in_first_ring(packed[s], s) for s in shifts]
    second = [to_other_core(packed[NX])] + [in_other_ring(packed[NX + s], s) for s in shifts]

    part = cols // NY
    terms = call(
        functools.partial(terms_kernel, factor),
        [shape((part, kv), F32)] + [shape((part, kv), BF16)] * (NY - 1),
        place,
        *first,
        *second,
    )

    own, *halves = call(
        weight_kernel,
        [shape((rows, kv), BF16)] + [shape((rows // 2, kv), BF16)] * 2,
        place,
        codes,
        jnp.repeat(scales, 2)[:, None],
        after=[first[2]],
        spaces=[pltpu.HBM, pltpu.VMEM],
        scratch=[pltpu.VMEM((rows, kv), codes.dtype), pltpu.SemaphoreType.DMA],
    )
    sent_pieces = call(
        pieces_kernel,
        [shape((tokens, NYL * rows), BF16)] * NX,
        place,
        own,
        *[weights_moved(halves[turn > 1], turn) for turn in (1, 2, 3)],
        *first,
        after=[terms[0]],
        scratch=[pltpu.VMEM((NYL * rows, kv), BF16)],
    )
    pieces = [sent_pieces[0]] + [in_first_ring(sent_pieces[s], -s) for s in shifts]
    grad_in, laid = call(
        functools.partial(laid_kernel, rows),
        [shape((tokens, width), BF16), shape((8, 128), F32)],
        place,
        *pieces,
    )
    column = call(
        sum_kernel,
        shape((part, kv), BF16),
        place,
        terms[0],
        *[in_second_ring(terms[t], t) for t in shifts],
        after=[sent_pieces[0]],
    ).reshape(NZ, part // NZ, kv)
    ring = lax.all_to_all(column, "z", split_axis=0, concat_axis=0, tiled=True)
    grad_w = call(last_kernel, shape((part // NZ, kv), F32), place, ring, after=[laid])
    return (grad_in, grad_w)


def solution(mesh):
    fine = Mesh(mesh.devices.reshape(NYL, NX, NZ, NYH, NC), AXES)
    in_specs = (P(AXES, None), P(AXES, None), P(("yl", "x"), None), P(("yl", "x")))
    out_specs = (P(AXES, None), P(AXES, None))
    return jax.shard_map(
        per_device, mesh=fine, in_specs=in_specs, out_specs=out_specs, check_vma=False
    )
```

time: 72.9 us -> 60.5 us (0.83)
  the two profiles are of different devices: /device:TPU:25 before, /device:TPU:1 now
where the time goes in v3:
time: 60.5 us; the launch traced here: 60.2 us
  starting transfers between devices  36.5 us (60%)
  Pallas kernels  12.4 us (20%)
  waiting for transfers between devices  9.17 us (15%)
  between operations  0.77 us (1%)
  local copies, waits for them, and re-layouts  0.74 us (1%)
  other arithmetic  0.65 us (1%)
    ppermute x16, starting transfers between devices, moved(): return lax.ppermute(value, AXES, moves)  28.3 us
    pallas_call x7, Pallas kernels, call(): pl.pallas_call(body, out_shape=outs, in_specs=[pl.BlockSpec(memory_space=...  12.4 us
    all_to_all x1, starting transfers between devices, per_device(): ring = lax.all_to_all(column, 'z', split_axis=0, concat_axis=0, tiled=True)  8.19 us
    all_to_all x1, waiting for transfers between devices, per_device(): ring = lax.all_to_all(column, 'z', split_axis=0, concat_axis=0, tiled=True)  6.87 us
    ppermute x16, waiting for transfers between devices, moved(): return lax.ppermute(value, AXES, moves)  2.3 us
  transfers between devices with their start and end apart: 17, of which 2 were waited for; matrix products, arithmetic and copies ran while one was open for 0% of the time, Pallas kernels for 12%

profile of v3, /device:TPU:1, one launch (start us, length us, event | category | flops | bytes accessed | tf_op | source)
XLA Modules:
  0.0 60.2 jit_solution(16292179074946737126)
XLA Ops:
  0.6 0.7 %pad_add_fusion.place_ref = s32[3]{0:T(128)} fusion(s32[1]{0:T(128)} %bitcast.2, s32[1]{0:T(128)} %bitcast.1, s32[1]{0:T(128)} %bitcast), kind=kLoop, calls=%fused_computation | loop fusion | flops 6 | bytes 24 | tf_op jit(solution)/shard_map/stack | solution.py:208
  1.3 4.1 %shard_map.59 = (bf16[2,128,512]{2,1,0:T(8,128)(2,1)}, bf16[2,128,512]{2,1,0:T(8,128)(2,1)}, bf16[2,128,512]{2,1,0:T(8,128)(2,1)}, bf16[2,128,512]{2,1,0:T(8,128...) custom-call(s32[3]{0:T(128)} %pad_add_fusion.place_ref, ...), custom_call_target="tpu_custom_call" | custom-call | bytes 1179648 | tf_op jit(solution)/shard_map/pallas_call | solution.py:61
  5.4 3.8 %collective-permute-start = (bf16[2,128,512]{2,1,0:T(8,128)(2,1)}, bf16[2,128,512]{2,1,0:T(8,128)(2,1)S(1)}, u32[]{:S(2)}, u32[]{:S(2)}) collective-permute-start(bf16[2,128,512]{2,1,0:T(8,128)(2,1)} %get-tuple-element.23), channel_id=1, source_target_pairs={{0,64},{1,3},{4,68},{5,7},{8,72},{9,11},{12,76},{13,15},{16,80},{1... | collective-permute-start | bytes 786440 | tf_op jit(solution)/shard_map/ppermute | solution.py:26
  9.6 2.3 %collective-permute-start.5 = (bf16[2,128,512]{2,1,0:T(8,128)(2,1)}, bf16[2,128,512]{2,1,0:T(8,128)(2,1)S(1)}, u32[]{:S(2)}, u32[]{:S(2)}) collective-permute-start(bf16[2,128,512]{2,1,0:T(8,128)(2,1)} %get-tuple-element.29), channel_id=1, source_target_pairs={{0,96},{1,131},{4,100},{5,135},{8,104},{9,139},{12,108},{13,143},{... | collective-permute-start | bytes 786440 | tf_op jit(solution)/shard_map/ppermute | solution.py:26
  11.9 1.3 %collective-permute-start.6 = (bf16[2,128,512]{2,1,0:T(8,128)(2,1)}, bf16[2,128,512]{2,1,0:T(8,128)(2,1)S(1)}, u32[]{:S(2)}, u32[]{:S(2)}) collective-permute-start(bf16[2,128,512]{2,1,0:T(8,128)(2,1)} %get-tuple-element.30), channel_id=1, source_target_pairs={{0,1},{1,0},{4,5},{5,4},{8,9},{9,8},{12,13},{13,12},{16,17},{17,16... | collective-permute-start | bytes 786440 | tf_op jit(solution)/shard_map/ppermute | solution.py:26
  13.5 4.3 %collective-permute-start.8 = (bf16[2,128,512]{2,1,0:T(8,128)(2,1)}, bf16[2,128,512]{2,1,0:T(8,128)(2,1)S(1)}, u32[]{:S(2)}, u32[]{:S(2)}) collective-permute-start(bf16[2,128,512]{2,1,0:T(8,128)(2,1)} %get-tuple-element.32), channel_id=1, source_target_pairs={{0,3},{1,64},{4,7},{5,68},{8,11},{9,72},{12,15},{13,76},{16,19},{1... | collective-permute-start | bytes 786440 | tf_op jit(solution)/shard_map/ppermute | solution.py:26
  17.8 3.8 %collective-permute-start.9 = (bf16[2,128,512]{2,1,0:T(8,128)(2,1)}, bf16[2,128,512]{2,1,0:T(8,128)(2,1)S(1)}, u32[]{:S(2)}, u32[]{:S(2)}) collective-permute-start(bf16[2,128,512]{2,1,0:T(8,128)(2,1)} %get-tuple-element.33), channel_id=1, source_target_pairs={{0,131},{1,96},{4,135},{5,100},{8,139},{9,104},{12,143},{13,108},{... | collective-permute-start | bytes 786440 | tf_op jit(solution)/shard_map/ppermute | solution.py:26
  22.4 0.8 %shard_map.60 = (bf16[512,512]{1,0:T(8,128)(2,1)S(1)}, bf16[256,512]{1,0:T(8,128)(2,1)S(1)}, bf16[256,512]{1,0:T(8,128)(2,1)S(1)}) custom-call(s32[3]{0:T(128)S(1)} %copy-done.2, s32[512,512]{1,0:T(8,128)S(1)} %copy-done, f32[512,1]{1,0:T(8,128)S(1)} %broadcast_in_dim_reshape.4.refs_1_, bf16[2,128,512]{2,1,0:T(8,128)(2,1)S(1)} %collective-permute-done.refs_2_.refs_6_), custom_call_target="tpu_custom_call" | custom-call | bytes 1050624 | tf_op jit(solution)/shard_map/pallas_call | solution.py:61
  23.2 1.5 %collective-permute-start.1 = (bf16[256,512]{1,0:T(8,128)(2,1)S(1)}, bf16[256,512]{1,0:T(8,128)(2,1)S(1)}, u32[]{:S(2)}, u32[]{:S(2)}) collective-permute-start(bf16[256,512]{1,0:T(8,128)(2,1)S(1)} %get-tuple-element.25), channel_id=1, source_target_pairs={{0,130},{1,97},{4,134},{5,101},{8,138},{9,105},{12,142},{13,109},{... | collective-permute-start | bytes 786440 | tf_op jit(solution)/shard_map/ppermute | solution.py:26
  24.7 2.0 %collective-permute-start.3 = (bf16[256,512]{1,0:T(8,128)(2,1)S(1)}, bf16[256,512]{1,0:T(8,128)(2,1)S(1)}, u32[]{:S(2)}, u32[]{:S(2)}) collective-permute-start(bf16[256,512]{1,0:T(8,128)(2,1)S(1)} %get-tuple-element.26), channel_id=1, source_target_pairs={{1,33},{5,37},{9,41},{13,45},{17,49},{21,53},{25,57},{29,61},{129,... | collective-permute-start | bytes 786440 | tf_op jit(solution)/shard_map/ppermute | solution.py:26
  26.7 1.7 %collective-permute-start.2 = (bf16[256,512]{1,0:T(8,128)(2,1)S(1)}, bf16[256,512]{1,0:T(8,128)(2,1)S(1)}, u32[]{:S(2)}, u32[]{:S(2)}) collective-permute-start(bf16[256,512]{1,0:T(8,128)(2,1)S(1)} %get-tuple-element.26), channel_id=1, source_target_pairs={{0,128},{1,65},{4,132},{5,69},{8,136},{9,73},{12,140},{13,77},{16,... | collective-permute-start | bytes 786440 | tf_op jit(solution)/shard_map/ppermute | solution.py:26
  28.4 1.3 %shard_map.61 = (f32[128,512]{1,0:T(8,128)S(1)}, bf16[128,512]{1,0:T(8,128)(2,1)S(1)}, bf16[128,512]{1,0:T(8,128)(2,1)S(1)}, bf16[128,512]{1,0:T(8,128)(2,1)S(1)}) custom-call(s32[3]{0:T(128)S(1)} %copy-done.2, bf16[2,128,512]{2,1,0:T(8,128)(2,1)S(1)} %copy-done.1, bf16[2,128,512]{2,1,0:T(8,128)(2,1)S(1)} %collective-permute-done.4.refs_1_.refs_5_, ...), custom_call_target="tpu_custom_call" | custom-call | bytes 2097152 | tf_op jit(solution)/shard_map/pallas_call | solution.py:61
  29.7 1.7 %collective-permute-start.13 = (bf16[128,512]{1,0:T(8,128)(2,1)S(1)}, bf16[128,512]{1,0:T(8,128)(2,1)S(1)}, u32[]{:S(2)}, u32[]{:S(2)}) collective-permute-start(bf16[128,512]{1,0:T(8,128)(2,1)S(1)} %get-tuple-element.40), channel_id=1, source_target_pairs={{0,128},{1,33},{4,132},{5,37},{8,136},{9,41},{12,140},{13,45},{16,... | collective-permute-start | bytes 393224 | tf_op jit(solution)/shard_map/ppermute | solution.py:26
  31.3 1.6 %collective-permute-start.14 = (bf16[128,512]{1,0:T(8,128)(2,1)S(1)}, bf16[128,512]{1,0:T(8,128)(2,1)S(1)}, u32[]{:S(2)}, u32[]{:S(2)}) collective-permute-start(bf16[128,512]{1,0:T(8,128)(2,1)S(1)} %get-tuple-element.41), channel_id=1, source_target_pairs={{0,2},{1,65},{4,6},{5,69},{8,10},{9,73},{12,14},{13,77},{16,18},{1... | collective-permute-start | bytes 393224 | tf_op jit(solution)/shard_map/ppermute | solution.py:26
  33.0 0.8 %collective-permute-start.15 = (bf16[128,512]{1,0:T(8,128)(2,1)S(1)}, bf16[128,512]{1,0:T(8,128)(2,1)S(1)}, u32[]{:S(2)}, u32[]{:S(2)}) collective-permute-start(bf16[128,512]{1,0:T(8,128)(2,1)S(1)} %get-tuple-element.42), channel_id=1, source_target_pairs={{0,130},{1,97},{4,134},{5,101},{8,138},{9,105},{12,142},{13,109},{... | collective-permute-start | bytes 393224 | tf_op jit(solution)/shard_map/ppermute | solution.py:26
  33.8 2.3 %collective-permute-done.3.refs_3_ = bf16[256,512]{1,0:T(8,128)(2,1)S(1)} collective-permute-done((bf16[256,512]{1,0:T(8,128)(2,1)S(1)}, bf16[256,512]{1,0:T(8,128)(2,1)S(1)}, u32[]{:S(2)}, u32[]{:S(2)}) %collective-permute-start.3) | collective-permute-done | bytes 262176 | tf_op jit(solution)/shard_map/ppermute | solution.py:26
  36.1 2.1 %shard_map.62 = (bf16[128,1024]{1,0:T(8,128)(2,1)S(1)}, bf16[128,1024]{1,0:T(8,128)(2,1)S(1)}, bf16[128,1024]{1,0:T(8,128)(2,1)S(1)}, bf16[128,1024]{1,0:T(8,128)(2,1)S(1)}) custom-call(s32[3]{0:T(128)S(1)} %copy-done.2, bf16[512,512]{1,0:T(8,128)(2,1)S(1)} %get-tuple-element.24.refs_0_, bf16[256,512]{1,0:T(8,128)(2,1)S(1)} %collective-permute-done.1.refs_1_, ...), custom_call_target="tpu_custom_call" | custom-call | bytes 2359296 | tf_op jit(solution)/shard_map/pallas_call | solution.py:61
  38.2 1.9 %collective-permute-start.10 = (bf16[128,1024]{1,0:T(8,128)(2,1)S(1)}, bf16[128,1024]{1,0:T(8,128)(2,1)S(1)}, u32[]{:S(2)}, u32[]{:S(2)}) collective-permute-start(bf16[128,1024]{1,0:T(8,128)(2,1)S(1)} %get-tuple-element.36), channel_id=1, source_target_pairs={{0,96},{1,131},{4,100},{5,135},{8,104},{9,139},{12,108},{13,143},{... | collective-permute-start | bytes 786440 | tf_op jit(solution)/shard_map/ppermute | solution.py:26
  40.4 0.7 %collective-permute-start.12 = (bf16[128,1024]{1,0:T(8,128)(2,1)S(1)}, bf16[128,1024]{1,0:T(8,128)(2,1)S(1)}, u32[]{:S(2)}, u32[]{:S(2)}) collective-permute-start(bf16[128,1024]{1,0:T(8,128)(2,1)S(1)} %get-tuple-element.38), channel_id=1, source_target_pairs={{0,32},{1,129},{4,36},{5,133},{8,40},{9,137},{12,44},{13,141},{16,... | collective-permute-start | bytes 786440 | tf_op jit(solution)/shard_map/ppermute | solution.py:26
  41.1 1.3 %shard_map.64 = bf16[128,512]{1,0:T(8,128)(2,1)} custom-call(s32[3]{0:T(128)S(1)} %copy-done.2, f32[128,512]{1,0:T(8,128)S(1)} %get-tuple-element.34.refs_8_.refs_0_, bf16[128,512]{1,0:T(8,128)(2,1)S(1)} %collective-permute-done.13.refs_1_, bf16[128,512]{1,0:T(8,128)(2,1)S(1)} %collective-permute-done.14.refs_2_, ...), custom_call_target="tpu_custom_call" | custom-call | bytes 655360 | tf_op jit(solution)/shard_map/pallas_call | solution.py:61
  42.3 8.2 %all-to-all-start = ((bf16[8,16,512]{2,1,0:T(8,128)(2,1)}), bf16[8,16,512]{2,1,0:T(8,128)(2,1)S(1)}, u32[]{:S(2)}, u32[]{:S(2)}) async-start(bf16[8,16,512]{2,1,0:T(8,128)(2,1)} %bitcast.3), calls=%async_computation | async-start | bytes 262144 | tf_op jit(solution)/shard_map/all_to_all | solution.py:275
  50.6 1.6 %shard_map.63 = (bf16[128,4096]{1,0:T(8,128)(2,1)}, f32[8,128]{1,0:T(8,128)S(1)}) custom-call(s32[3]{0:T(128)S(1)} %copy-done.2, bf16[128,1024]{1,0:T(8,128)(2,1)S(1)} %get-tuple-element.35.refs_0_.refs_4_, bf16[128,1024]{1,0:T(8,128)(2,1)S(1)} %collective-permute-done.10.refs_1_, bf16[128,1024]{1,0:T(8,128)(2,1)S(1)} %collective-permute-done.11.refs_2_, ...), custom_call_target="tpu_custom_call" | custom-call | bytes 1048576 | tf_op jit(solution)/shard_map/pallas_call | solution.py:61
  52.2 6.9 %all-to-all-done.refs_0_ = bf16[8,16,512]{2,1,0:T(8,128)(2,1)S(1)} async-done(((bf16[8,16,512]{2,1,0:T(8,128)(2,1)}), bf16[8,16,512]{2,1,0:T(8,128)(2,1)S(1)}, u32[]{:S(2)}, u32[]{:S(2)}) %all-to-all-start) | async-done | bytes 131104 | tf_op jit(solution)/shard_map/all_to_all | solution.py:275
  59.1 1.2 %shard_map.65 = f32[16,512]{1,0:T(8,128)} custom-call(s32[3]{0:T(128)S(1)} %copy-done.2, bf16[8,16,512]{2,1,0:T(8,128)(2,1)S(1)} %all-to-all-done.refs_0_, f32[8,128]{1,0:T(8,128)S(1)} %get-tuple-element.43.refs_1_), custom_call_target="tpu_custom_call" | custom-call | bytes 131072 | tf_op jit(solution)/shard_map/pallas_call | solution.py:61
  (28 shorter events, 1.7 us)
Async XLA Ops:
  0.6 21.2 %copy-start = (s32[512,512]{1,0:T(8,128)S(1)}, s32[512,512]{1,0:T(8,128)}, u32[]{:S(2)}) copy-start(s32[512,512]{1,0:T(8,128)} %refs_0_.3) | copy-start | bytes 3145732
  5.4 8.1 %collective-permute-start = (bf16[2,128,512]{2,1,0:T(8,128)(2,1)}, bf16[2,128,512]{2,1,0:T(8,128)(2,1)S(1)}, u32[]{:S(2)}, u32[]{:S(2)}) collective-permute-start(bf16[2,128,512]{2,1,0:T(8,128)(2,1)} %get-tuple-element.23), channel_id=1, source_target_pairs={{0,64},{1,3},{4,68},{5,7},{8,72},{9,11},{12,76},{13,15},{16,80},{1... | collective-permute-start | bytes 786440 | tf_op jit(solution)/shard_map/ppermute | solution.py:26
  9.2 8.6 %collective-permute-start.4 = (bf16[2,128,512]{2,1,0:T(8,128)(2,1)}, bf16[2,128,512]{2,1,0:T(8,128)(2,1)S(1)}, u32[]{:S(2)}, u32[]{:S(2)}) collective-permute-start(bf16[2,128,512]{2,1,0:T(8,128)(2,1)} %get-tuple-element.28), channel_id=1, source_target_pairs={{0,32},{1,129},{4,36},{5,133},{8,40},{9,137},{12,44},{13,141},{16,... | collective-permute-start | bytes 786440 | tf_op jit(solution)/shard_map/ppermute | solution.py:26
  9.6 13.6 %collective-permute-start.5 = (bf16[2,128,512]{2,1,0:T(8,128)(2,1)}, bf16[2,128,512]{2,1,0:T(8,128)(2,1)S(1)}, u32[]{:S(2)}, u32[]{:S(2)}) collective-permute-start(bf16[2,128,512]{2,1,0:T(8,128)(2,1)} %get-tuple-element.29), channel_id=1, source_target_pairs={{0,96},{1,131},{4,100},{5,135},{8,104},{9,139},{12,108},{13,143},{... | collective-permute-start | bytes 786440 | tf_op jit(solution)/shard_map/ppermute | solution.py:26
  11.9 12.8 %collective-permute-start.6 = (bf16[2,128,512]{2,1,0:T(8,128)(2,1)}, bf16[2,128,512]{2,1,0:T(8,128)(2,1)S(1)}, u32[]{:S(2)}, u32[]{:S(2)}) collective-permute-start(bf16[2,128,512]{2,1,0:T(8,128)(2,1)} %get-tuple-element.30), channel_id=1, source_target_pairs={{0,1},{1,0},{4,5},{5,4},{8,9},{9,8},{12,13},{13,12},{16,17},{17,16... | collective-permute-start | bytes 786440 | tf_op jit(solution)/shard_map/ppermute | solution.py:26
  13.2 13.4 %collective-permute-start.7 = (bf16[2,128,512]{2,1,0:T(8,128)(2,1)}, bf16[2,128,512]{2,1,0:T(8,128)(2,1)S(1)}, u32[]{:S(2)}, u32[]{:S(2)}) collective-permute-start(bf16[2,128,512]{2,1,0:T(8,128)(2,1)} %get-tuple-element.31), channel_id=1, source_target_pairs={{0,129},{1,32},{4,133},{5,36},{8,137},{9,40},{12,141},{13,44},{16,... | collective-permute-start | bytes 786440 | tf_op jit(solution)/shard_map/ppermute | solution.py:26
  13.5 8.1 %copy-start.3 = (f32[256]{0:T(256)S(1)}, f32[256]{0:T(256)}, u32[]{:S(2)}) copy-start(f32[256]{0:T(256)} %param.7) | copy-start | bytes 3076
  13.5 14.8 %collective-permute-start.8 = (bf16[2,128,512]{2,1,0:T(8,128)(2,1)}, bf16[2,128,512]{2,1,0:T(8,128)(2,1)S(1)}, u32[]{:S(2)}, u32[]{:S(2)}) collective-permute-start(bf16[2,128,512]{2,1,0:T(8,128)(2,1)} %get-tuple-element.32), channel_id=1, source_target_pairs={{0,3},{1,64},{4,7},{5,68},{8,11},{9,72},{12,15},{13,76},{16,19},{1... | collective-permute-start | bytes 786440 | tf_op jit(solution)/shard_map/ppermute | solution.py:26
  17.8 10.5 %collective-permute-start.9 = (bf16[2,128,512]{2,1,0:T(8,128)(2,1)}, bf16[2,128,512]{2,1,0:T(8,128)(2,1)S(1)}, u32[]{:S(2)}, u32[]{:S(2)}) collective-permute-start(bf16[2,128,512]{2,1,0:T(8,128)(2,1)} %get-tuple-element.33), channel_id=1, source_target_pairs={{0,131},{1,96},{4,135},{5,100},{8,139},{9,104},{12,143},{13,108},{... | collective-permute-start | bytes 786440 | tf_op jit(solution)/shard_map/ppermute | solution.py:26
  21.7 0.7 %copy-start.2 = (s32[3]{0:T(128)S(1)}, s32[3]{0:T(128)}, u32[]{:S(2)}) copy-start(s32[3]{0:T(128)} %pad_add_fusion.place_ref) | copy-start | bytes 40
  22.4 6.0 %copy-start.1 = (bf16[2,128,512]{2,1,0:T(8,128)(2,1)S(1)}, bf16[2,128,512]{2,1,0:T(8,128)(2,1)}, u32[]{:S(2)}) copy-start(bf16[2,128,512]{2,1,0:T(8,128)(2,1)} %get-tuple-element.27.refs_0_.refs_4_) | copy-start | bytes 786436
  23.2 9.8 %collective-permute-start.1 = (bf16[256,512]{1,0:T(8,128)(2,1)S(1)}, bf16[256,512]{1,0:T(8,128)(2,1)S(1)}, u32[]{:S(2)}, u32[]{:S(2)}) collective-permute-start(bf16[256,512]{1,0:T(8,128)(2,1)S(1)} %get-tuple-element.25), channel_id=1, source_target_pairs={{0,130},{1,97},{4,134},{5,101},{8,138},{9,105},{12,142},{13,109},{... | collective-permute-start | bytes 786440 | tf_op jit(solution)/shard_map/ppermute | solution.py:26
  24.7 11.4 %collective-permute-start.3 = (bf16[256,512]{1,0:T(8,128)(2,1)S(1)}, bf16[256,512]{1,0:T(8,128)(2,1)S(1)}, u32[]{:S(2)}, u32[]{:S(2)}) collective-permute-start(bf16[256,512]{1,0:T(8,128)(2,1)S(1)} %get-tuple-element.26), channel_id=1, source_target_pairs={{1,33},{5,37},{9,41},{13,45},{17,49},{21,53},{25,57},{29,61},{129,... | collective-permute-start | bytes 786440 | tf_op jit(solution)/shard_map/ppermute | solution.py:26
  26.7 9.4 %collective-permute-start.2 = (bf16[256,512]{1,0:T(8,128)(2,1)S(1)}, bf16[256,512]{1,0:T(8,128)(2,1)S(1)}, u32[]{:S(2)}, u32[]{:S(2)}) collective-permute-start(bf16[256,512]{1,0:T(8,128)(2,1)S(1)} %get-tuple-element.26), channel_id=1, source_target_pairs={{0,128},{1,65},{4,132},{5,69},{8,136},{9,73},{12,140},{13,77},{16,... | collective-permute-start | bytes 786440 | tf_op jit(solution)/shard_map/ppermute | solution.py:26
  29.7 10.7 %collective-permute-start.13 = (bf16[128,512]{1,0:T(8,128)(2,1)S(1)}, bf16[128,512]{1,0:T(8,128)(2,1)S(1)}, u32[]{:S(2)}, u32[]{:S(2)}) collective-permute-start(bf16[128,512]{1,0:T(8,128)(2,1)S(1)} %get-tuple-element.40), channel_id=1, source_target_pairs={{0,128},{1,33},{4,132},{5,37},{8,136},{9,41},{12,140},{13,45},{16,... | collective-permute-start | bytes 393224 | tf_op jit(solution)/shard_map/ppermute | solution.py:26
  31.3 9.7 %collective-permute-start.14 = (bf16[128,512]{1,0:T(8,128)(2,1)S(1)}, bf16[128,512]{1,0:T(8,128)(2,1)S(1)}, u32[]{:S(2)}, u32[]{:S(2)}) collective-permute-start(bf16[128,512]{1,0:T(8,128)(2,1)S(1)} %get-tuple-element.41), channel_id=1, source_target_pairs={{0,2},{1,65},{4,6},{5,69},{8,10},{9,73},{12,14},{13,77},{16,18},{1... | collective-permute-start | bytes 393224 | tf_op jit(solution)/shard_map/ppermute | solution.py:26
  33.0 8.1 %collective-permute-start.15 = (bf16[128,512]{1,0:T(8,128)(2,1)S(1)}, bf16[128,512]{1,0:T(8,128)(2,1)S(1)}, u32[]{:S(2)}, u32[]{:S(2)}) collective-permute-start(bf16[128,512]{1,0:T(8,128)(2,1)S(1)} %get-tuple-element.42), channel_id=1, source_target_pairs={{0,130},{1,97},{4,134},{5,101},{8,138},{9,105},{12,142},{13,109},{... | collective-permute-start | bytes 393224 | tf_op jit(solution)/shard_map/ppermute | solution.py:26
  38.2 12.3 %collective-permute-start.10 = (bf16[128,1024]{1,0:T(8,128)(2,1)S(1)}, bf16[128,1024]{1,0:T(8,128)(2,1)S(1)}, u32[]{:S(2)}, u32[]{:S(2)}) collective-permute-start(bf16[128,1024]{1,0:T(8,128)(2,1)S(1)} %get-tuple-element.36), channel_id=1, source_target_pairs={{0,96},{1,131},{4,100},{5,135},{8,104},{9,139},{12,108},{13,143},{... | collective-permute-start | bytes 786440 | tf_op jit(solution)/shard_map/ppermute | solution.py:26
  40.2 10.4 %collective-permute-start.11 = (bf16[128,1024]{1,0:T(8,128)(2,1)S(1)}, bf16[128,1024]{1,0:T(8,128)(2,1)S(1)}, u32[]{:S(2)}, u32[]{:S(2)}) collective-permute-start(bf16[128,1024]{1,0:T(8,128)(2,1)S(1)} %get-tuple-element.37), channel_id=1, source_target_pairs={{0,64},{1,3},{4,68},{5,7},{8,72},{9,11},{12,76},{13,15},{16,80},{1... | collective-permute-start | bytes 786440 | tf_op jit(solution)/shard_map/ppermute | solution.py:26
  40.4 10.2 %collective-permute-start.12 = (bf16[128,1024]{1,0:T(8,128)(2,1)S(1)}, bf16[128,1024]{1,0:T(8,128)(2,1)S(1)}, u32[]{:S(2)}, u32[]{:S(2)}) collective-permute-start(bf16[128,1024]{1,0:T(8,128)(2,1)S(1)} %get-tuple-element.38), channel_id=1, source_target_pairs={{0,32},{1,129},{4,36},{5,133},{8,40},{9,137},{12,44},{13,141},{16,... | collective-permute-start | bytes 786440 | tf_op jit(solution)/shard_map/ppermute | solution.py:26
  42.3 16.7 %all-to-all-start = ((bf16[8,16,512]{2,1,0:T(8,128)(2,1)}), bf16[8,16,512]{2,1,0:T(8,128)(2,1)S(1)}, u32[]{:S(2)}, u32[]{:S(2)}) async-start(bf16[8,16,512]{2,1,0:T(8,128)(2,1)} %bitcast.3), calls=%async_computation | async-start | bytes 262144 | tf_op jit(solution)/shard_map/all_to_all | solution.py:275

commit v4 on v3

--- a/solution.py
+++ b/solution.py
@@ -51,9 +51,10 @@
     return moved(value, lambda x, y, z, c: (x, y, z, 1 - c))
 
 
-def call(kernel, outs, place, *arrays, after=(), spaces=None, scratch=(), vmem=12):
-    def body(place_ref, *refs):
-        kernel(place_ref, *refs[: len(arrays)], *refs[len(arrays) + len(after) :])
+def call(kernel, outs, *arrays, after=(), spaces=None, scratch=(), vmem=12):
+    def body(*refs):
+        x, yl, yh, c = (lax.axis_index(a) for a in ("x", "yl", "yh", "c"))
+        kernel((x, NYL * yh + yl, c), *refs[: len(arrays)], *refs[len(arrays) + len(after) :])
 
     spaces = spaces or [pltpu.VMEM] * len(arrays)
 
@@ -61,23 +62,22 @@
     return pl.pallas_call(
         body,
         out_shape=outs,
-        in_specs=[pl.BlockSpec(memory_space=pltpu.SMEM)]
-        + [pl.BlockSpec(memory_space=space) for space in spaces]
+        in_specs=[pl.BlockSpec(memory_space=space) for space in spaces]
         + [pl.BlockSpec(memory_space=pl.ANY)] * len(after),
         out_specs=jax.tree.map(lambda _: pl.BlockSpec(memory_space=pltpu.VMEM), outs),
         scratch_shapes=list(scratch),
         cost_estimate=pl.CostEstimate(flops=0, bytes_accessed=moved_bytes, transcendentals=0),
         compiler_params=pltpu.CompilerParams(vmem_limit_bytes=vmem * 2**20),
-    )(place, *arrays, *after)
+    )(*arrays, *after)
 
 
 def start(multiple, factor):
     return pl.multiple_of(multiple * factor, factor)
 
 
-def pack_kernel(rows, place_ref, acts_ref, cot_ref, *refs):
+def pack_kernel(rows, place, acts_ref, cot_ref, *refs):
     own, swap, (acts_here, sorted_here, sems) = refs[:NX], refs[NX : 2 * NX], refs[2 * NX :]
-    x, y, c = place_ref[0], place_ref[1], place_ref[2]
+    x, y, c = place[0], place[1], place[2]
     ring = jnp.where(c == 0, x, y)
     other_ring = jnp.where(c == 0, y, x)
     blocks = NYL * NX
@@ -123,9 +123,9 @@
             own[s][1] = cot
 
 
-def weight_kernel(place_ref, codes_ref, scales_ref, out_ref, *refs):
+def weight_kernel(place, codes_ref, scales_ref, out_ref, *refs):
     sent, (codes_here, sem) = refs[:2], refs[2:]
-    c, yh = place_ref[2], place_ref[1] // NYL
+    c, yh = place[2], place[1] // NYL
     half = sent[0].shape[0]
     copy = pltpu.make_async_copy(codes_ref, codes_here, sem)
     copy.start()
@@ -135,20 +135,20 @@
         half_ref[...] = out_ref[pl.ds(start(jnp.where(c == 0, k, yh), half), half), :]
 
 
-def sum_kernel(place_ref, own_ref, *refs):
+def sum_kernel(place, own_ref, *refs):
     total = own_ref[...]
     for part in refs[:-1]:
         total = total + part[...].astype(F32)
     refs[-1][...] = total.astype(BF16)
 
 
-def last_kernel(place_ref, parts_ref, out_ref):
+def last_kernel(place, parts_ref, out_ref):
     out_ref[...] = parts_ref[...].astype(F32).sum(axis=0)
 
 
-def pieces_kernel(place_ref, own_ref, *refs):
+def pieces_kernel(place, own_ref, *refs):
     arrived, refs, weight_ref = refs[:3], refs[3:-1], refs[-1]
-    x, y, c = place_ref[0], place_ref[1], place_ref[2]
+    x, y, c = place[0], place[1], place[2]
     yl, yh = lax.rem(y, NYL), y // NYL
     half = arrived[0].shape[0]
     on_0 = c == 0
@@ -169,8 +169,8 @@
         ).astype(BF16)
 
 
-def laid_kernel(rows, place_ref, *refs):
-    x, y, c = place_ref[0], place_ref[1], place_ref[2]
+def laid_kernel(rows, place, *refs):
+    x, y, c = place[0], place[1], place[2]
     out, done_ref = refs[-2:]
     done_ref[...] = jnp.zeros_like(done_ref)
     half = rows // 2
@@ -183,8 +183,8 @@
             out[:, at] = piece[:, q * half : (q + 1) * half]
 
 
-def terms_kernel(factor, place_ref, *refs):
-    x, y, c = place_ref[0], place_ref[1], place_ref[2]
+def terms_kernel(factor, place, *refs):
+    x, y, c = place[0], place[1], place[2]
     to = jnp.where(c == 0, y, x)
     first, second, outs = refs[:NX], refs[NX : 2 * NX], refs[2 * NX :]
     rows = outs[0].shape[0]
@@ -204,8 +204,6 @@
 def per_device(acts, grad_out, codes, scales):
     tokens, width = acts.shape
     rows, kv = codes.shape
-    yl, x, yh, c = (lax.axis_index(a) for a in ("yl", "x", "yh", "c"))
-    place = jnp.stack([x, NYL * yh + yl, c]).astype(jnp.int32)
     factor = 1.0 / math.sqrt(tokens * NYL * NX * NZ * NYH * NC)
     shifts = (1, 2, 3)
     shape = jax.ShapeDtypeStruct
@@ -214,7 +212,6 @@
     packed = call(
         functools.partial(pack_kernel, rows),
         [shape((2, tokens, cols), BF16)] * (2 * NX),
-        place,
         acts,
         grad_out,
         spaces=[pltpu.HBM, pltpu.HBM],
@@ -232,7 +229,6 @@
     terms = call(
         functools.partial(terms_kernel, factor),
         [shape((part, kv), F32)] + [shape((part, kv), BF16)] * (NY - 1),
-        place,
         *first,
         *second,
     )
@@ -240,7 +236,6 @@
     own, *halves = call(
         weight_kernel,
         [shape((rows, kv), BF16)] + [shape((rows // 2, kv), BF16)] * 2,
-        place,
         codes,
         jnp.repeat(scales, 2)[:, None],
         after=[first[2]],
@@ -250,7 +245,6 @@
     sent_pieces = call(
         pieces_kernel,
         [shape((tokens, NYL * rows), BF16)] * NX,
-        place,
         own,
         *[weights_moved(halves[turn > 1], turn) for turn in (1, 2, 3)],
         *first,
@@ -261,19 +255,17 @@
     grad_in, laid = call(
         functools.partial(laid_kernel, rows),
         [shape((tokens, width), BF16), shape((8, 128), F32)],
-        place,
         *pieces,
     )
     column = call(
         sum_kernel,
         shape((part, kv), BF16),
-        place,
         terms[0],
         *[in_second_ring(terms[t], t) for t in shifts],
         after=[sent_pieces[0]],
     ).reshape(NZ, part // NZ, kv)
     ring = lax.all_to_all(column, "z", split_axis=0, concat_axis=0, tiled=True)
-    grad_w = call(last_kernel, shape((part // NZ, kv), F32), place, ring, after=[laid])
+    grad_w = call(last_kernel, shape((part // NZ, kv), F32), ring, after=[laid])
     return (grad_in, grad_w)
 
 

time: 60.5 us -> 57.3 us (0.947)
  Pallas kernels: 12.4 us -> 8.62 us
  waiting for transfers between devices: 9.17 us -> 10.9 us
  other arithmetic: 0.65 us -> 0 us
    pallas_call x7, Pallas kernels: 12.4 us -> 8.62 us  [call(): pl.pallas_call(body, out_shape=outs, in_specs=[pl.BlockSpec(memory_space=...]
    all_to_all x1, waiting for transfers between devices: 6.87 us -> 8.09 us  [per_device(): ring = lax.all_to_all(column, 'z', split_axis=0, concat_axis=0, tiled=True)]
    another operation x1 -> x0, other arithmetic: 0.65 us -> none  [per_device(): place = jnp.stack([x, NYL * yh + yl, c]).astype(jnp.int32)]
  transfers between devices with their start and end apart: 17 -> 17, of which waited for: 2 -> 2; matrix products, arithmetic and copies ran while one was open for 0% -> 0% of each run, Pallas kernels for 12% -> 8%
where the time goes in v4:
time: 57.3 us; the launch traced here: 57 us
  starting transfers between devices  36.5 us (64%)
  waiting for transfers between devices  10.9 us (19%)
  Pallas kernels  8.62 us (15%)
  between operations  0.76 us (1%)
    ppermute x16, starting transfers between devices, moved(): return lax.ppermute(value, AXES, moves)  28.3 us
    pallas_call x7, Pallas kernels, call(): pl.pallas_call(body, out_shape=outs, in_specs=[pl.BlockSpec(memory_space=...  8.62 us
    all_to_all x1, starting transfers between devices, per_device(): ring = lax.all_to_all(column, 'z', split_axis=0, concat_axis=0, tiled=True)  8.17 us
    all_to_all x1, waiting for transfers between devices, per_device(): ring = lax.all_to_all(column, 'z', split_axis=0, concat_axis=0, tiled=True)  8.09 us
    ppermute x16, waiting for transfers between devices, moved(): return lax.ppermute(value, AXES, moves)  2.85 us
  transfers between devices with their start and end apart: 17, of which 2 were waited for; matrix products, arithmetic and copies ran while one was open for 0% of the time, Pallas kernels for 8%

profile of v4, /device:TPU:1, one launch (start us, length us, event | category | flops | bytes accessed | tf_op | source)
XLA Modules:
  0.0 57.0 jit_solution(7172896344903161657)
XLA Ops:
  0.6 3.5 %shard_map.59 = (bf16[2,128,512]{2,1,0:T(8,128)(2,1)}, bf16[2,128,512]{2,1,0:T(8,128)(2,1)}, bf16[2,128,512]{2,1,0:T(8,128)(2,1)}, bf16[2,128,512]{2,1,0:T(8,128...) custom-call(bf16[128,4096]{1,0:T(8,128)(2,1)} %refs_0_.2, ...), custom_call_target="tpu_custom_call" | custom-call | bytes 1179648 | tf_op jit(solution)/shard_map/pallas_call | solution.py:62
  4.2 3.8 %collective-permute-start = (bf16[2,128,512]{2,1,0:T(8,128)(2,1)}, bf16[2,128,512]{2,1,0:T(8,128)(2,1)S(1)}, u32[]{:S(2)}, u32[]{:S(2)}) collective-permute-start(bf16[2,128,512]{2,1,0:T(8,128)(2,1)} %get-tuple-element.23), channel_id=1, source_target_pairs={{0,64},{1,3},{4,68},{5,7},{8,72},{9,11},{12,76},{13,15},{16,80},{1... | collective-permute-start | bytes 786440 | tf_op jit(solution)/shard_map/ppermute | solution.py:26
  8.0 0.4 collective-permute-start.4
  8.4 2.3 %collective-permute-start.5 = (bf16[2,128,512]{2,1,0:T(8,128)(2,1)}, bf16[2,128,512]{2,1,0:T(8,128)(2,1)S(1)}, u32[]{:S(2)}, u32[]{:S(2)}) collective-permute-start(bf16[2,128,512]{2,1,0:T(8,128)(2,1)} %get-tuple-element.29), channel_id=1, source_target_pairs={{0,96},{1,131},{4,100},{5,135},{8,104},{9,139},{12,108},{13,143},{... | collective-permute-start | bytes 786440 | tf_op jit(solution)/shard_map/ppermute | solution.py:26
  10.7 1.3 %collective-permute-start.6 = (bf16[2,128,512]{2,1,0:T(8,128)(2,1)}, bf16[2,128,512]{2,1,0:T(8,128)(2,1)S(1)}, u32[]{:S(2)}, u32[]{:S(2)}) collective-permute-start(bf16[2,128,512]{2,1,0:T(8,128)(2,1)} %get-tuple-element.30), channel_id=1, source_target_pairs={{0,1},{1,0},{4,5},{5,4},{8,9},{9,8},{12,13},{13,12},{16,17},{17,16... | collective-permute-start | bytes 786440 | tf_op jit(solution)/shard_map/ppermute | solution.py:26
  12.3 4.3 %collective-permute-start.8 = (bf16[2,128,512]{2,1,0:T(8,128)(2,1)}, bf16[2,128,512]{2,1,0:T(8,128)(2,1)S(1)}, u32[]{:S(2)}, u32[]{:S(2)}) collective-permute-start(bf16[2,128,512]{2,1,0:T(8,128)(2,1)} %get-tuple-element.32), channel_id=1, source_target_pairs={{0,3},{1,64},{4,7},{5,68},{8,11},{9,72},{12,15},{13,76},{16,19},{1... | collective-permute-start | bytes 786440 | tf_op jit(solution)/shard_map/ppermute | solution.py:26
  16.6 3.8 %collective-permute-start.9 = (bf16[2,128,512]{2,1,0:T(8,128)(2,1)}, bf16[2,128,512]{2,1,0:T(8,128)(2,1)S(1)}, u32[]{:S(2)}, u32[]{:S(2)}) collective-permute-start(bf16[2,128,512]{2,1,0:T(8,128)(2,1)} %get-tuple-element.33), channel_id=1, source_target_pairs={{0,131},{1,96},{4,135},{5,100},{8,139},{9,104},{12,143},{13,108},{... | collective-permute-start | bytes 786440 | tf_op jit(solution)/shard_map/ppermute | solution.py:26
  20.6 0.3 shard_map.60
  20.9 1.5 %collective-permute-start.1 = (bf16[256,512]{1,0:T(8,128)(2,1)S(1)}, bf16[256,512]{1,0:T(8,128)(2,1)S(1)}, u32[]{:S(2)}, u32[]{:S(2)}) collective-permute-start(bf16[256,512]{1,0:T(8,128)(2,1)S(1)} %get-tuple-element.25), channel_id=1, source_target_pairs={{0,130},{1,97},{4,134},{5,101},{8,138},{9,105},{12,142},{13,109},{... | collective-permute-start | bytes 786440 | tf_op jit(solution)/shard_map/ppermute | solution.py:26
  22.4 2.0 %collective-permute-start.3 = (bf16[256,512]{1,0:T(8,128)(2,1)S(1)}, bf16[256,512]{1,0:T(8,128)(2,1)S(1)}, u32[]{:S(2)}, u32[]{:S(2)}) collective-permute-start(bf16[256,512]{1,0:T(8,128)(2,1)S(1)} %get-tuple-element.26), channel_id=1, source_target_pairs={{1,33},{5,37},{9,41},{13,45},{17,49},{21,53},{25,57},{29,61},{129,... | collective-permute-start | bytes 786440 | tf_op jit(solution)/shard_map/ppermute | solution.py:26
  24.4 1.7 %collective-permute-start.2 = (bf16[256,512]{1,0:T(8,128)(2,1)S(1)}, bf16[256,512]{1,0:T(8,128)(2,1)S(1)}, u32[]{:S(2)}, u32[]{:S(2)}) collective-permute-start(bf16[256,512]{1,0:T(8,128)(2,1)S(1)} %get-tuple-element.26), channel_id=1, source_target_pairs={{0,128},{1,65},{4,132},{5,69},{8,136},{9,73},{12,140},{13,77},{16,... | collective-permute-start | bytes 786440 | tf_op jit(solution)/shard_map/ppermute | solution.py:26
  26.0 0.8 %shard_map.61 = (f32[128,512]{1,0:T(8,128)S(1)}, bf16[128,512]{1,0:T(8,128)(2,1)S(1)}, bf16[128,512]{1,0:T(8,128)(2,1)S(1)}, bf16[128,512]{1,0:T(8,128)(2,1)S(1)}) custom-call(bf16[2,128,512]{2,1,0:T(8,128)(2,1)S(1)} %copy-done.1, bf16[2,128,512]{2,1,0:T(8,128)(2,1)S(1)} %collective-permute-done.4.refs_1_.refs_5_, ...), custom_call_target="tpu_custom_call" | custom-call | bytes 2097152 | tf_op jit(solution)/shard_map/pallas_call | solution.py:62
  26.8 1.7 %collective-permute-start.13 = (bf16[128,512]{1,0:T(8,128)(2,1)S(1)}, bf16[128,512]{1,0:T(8,128)(2,1)S(1)}, u32[]{:S(2)}, u32[]{:S(2)}) collective-permute-start(bf16[128,512]{1,0:T(8,128)(2,1)S(1)} %get-tuple-element.40), channel_id=1, source_target_pairs={{0,128},{1,33},{4,132},{5,37},{8,136},{9,41},{12,140},{13,45},{16,... | collective-permute-start | bytes 393224 | tf_op jit(solution)/shard_map/ppermute | solution.py:26
  28.5 1.7 %collective-permute-start.14 = (bf16[128,512]{1,0:T(8,128)(2,1)S(1)}, bf16[128,512]{1,0:T(8,128)(2,1)S(1)}, u32[]{:S(2)}, u32[]{:S(2)}) collective-permute-start(bf16[128,512]{1,0:T(8,128)(2,1)S(1)} %get-tuple-element.41), channel_id=1, source_target_pairs={{0,2},{1,65},{4,6},{5,69},{8,10},{9,73},{12,14},{13,77},{16,18},{1... | collective-permute-start | bytes 393224 | tf_op jit(solution)/shard_map/ppermute | solution.py:26
  30.2 0.8 %collective-permute-start.15 = (bf16[128,512]{1,0:T(8,128)(2,1)S(1)}, bf16[128,512]{1,0:T(8,128)(2,1)S(1)}, u32[]{:S(2)}, u32[]{:S(2)}) collective-permute-start(bf16[128,512]{1,0:T(8,128)(2,1)S(1)} %get-tuple-element.42), channel_id=1, source_target_pairs={{0,130},{1,97},{4,134},{5,101},{8,138},{9,105},{12,142},{13,109},{... | collective-permute-start | bytes 393224 | tf_op jit(solution)/shard_map/ppermute | solution.py:26
  31.0 2.8 %collective-permute-done.3.refs_3_ = bf16[256,512]{1,0:T(8,128)(2,1)S(1)} collective-permute-done((bf16[256,512]{1,0:T(8,128)(2,1)S(1)}, bf16[256,512]{1,0:T(8,128)(2,1)S(1)}, u32[]{:S(2)}, u32[]{:S(2)}) %collective-permute-start.3) | collective-permute-done | bytes 262176 | tf_op jit(solution)/shard_map/ppermute | solution.py:26
  33.8 1.6 %shard_map.62 = (bf16[128,1024]{1,0:T(8,128)(2,1)S(1)}, bf16[128,1024]{1,0:T(8,128)(2,1)S(1)}, bf16[128,1024]{1,0:T(8,128)(2,1)S(1)}, bf16[128,1024]{1,0:T(8,128)(2,1)S(1)}) custom-call(bf16[512,512]{1,0:T(8,128)(2,1)S(1)} %get-tuple-element.24.refs_0_, bf16[256,512]{1,0:T(8,128)(2,1)S(1)} %collective-permute-done.1.refs_1_, ...), custom_call_target="tpu_custom_call" | custom-call | bytes 2359296 | tf_op jit(solution)/shard_map/pallas_call | solution.py:62
  35.4 2.0 %collective-permute-start.10 = (bf16[128,1024]{1,0:T(8,128)(2,1)S(1)}, bf16[128,1024]{1,0:T(8,128)(2,1)S(1)}, u32[]{:S(2)}, u32[]{:S(2)}) collective-permute-start(bf16[128,1024]{1,0:T(8,128)(2,1)S(1)} %get-tuple-element.36), channel_id=1, source_target_pairs={{0,96},{1,131},{4,100},{5,135},{8,104},{9,139},{12,108},{13,143},{... | collective-permute-start | bytes 786440 | tf_op jit(solution)/shard_map/ppermute | solution.py:26
  37.6 0.7 %collective-permute-start.12 = (bf16[128,1024]{1,0:T(8,128)(2,1)S(1)}, bf16[128,1024]{1,0:T(8,128)(2,1)S(1)}, u32[]{:S(2)}, u32[]{:S(2)}) collective-permute-start(bf16[128,1024]{1,0:T(8,128)(2,1)S(1)} %get-tuple-element.38), channel_id=1, source_target_pairs={{0,32},{1,129},{4,36},{5,133},{8,40},{9,137},{12,44},{13,141},{16,... | collective-permute-start | bytes 786440 | tf_op jit(solution)/shard_map/ppermute | solution.py:26
  38.3 0.7 %shard_map.64 = bf16[128,512]{1,0:T(8,128)(2,1)} custom-call(f32[128,512]{1,0:T(8,128)S(1)} %get-tuple-element.34.refs_8_.refs_0_, bf16[128,512]{1,0:T(8,128)(2,1)S(1)} %collective-permute-done.13.refs_1_, bf16[128,512]{1,0:T(8,128)(2,1)S(1)} %collective-permute-done.14.refs_2_, bf16[128,512]{1,0:T(8,128)(2,1)S(1)} %collective-permute-done.15.refs_3_, ...), custom_call_target="tpu_custom_call" | custom-call | bytes 655360 | tf_op jit(solution)/shard_map/pallas_call | solution.py:62
  39.0 8.2 %all-to-all-start = ((bf16[8,16,512]{2,1,0:T(8,128)(2,1)}), bf16[8,16,512]{2,1,0:T(8,128)(2,1)S(1)}, u32[]{:S(2)}, u32[]{:S(2)}) async-start(bf16[8,16,512]{2,1,0:T(8,128)(2,1)} %bitcast), calls=%async_computation | async-start | bytes 262144 | tf_op jit(solution)/shard_map/all_to_all | solution.py:267
  47.2 1.1 %shard_map.63 = (bf16[128,4096]{1,0:T(8,128)(2,1)}, f32[8,128]{1,0:T(8,128)S(1)}) custom-call(bf16[128,1024]{1,0:T(8,128)(2,1)S(1)} %get-tuple-element.35.refs_0_.refs_4_, bf16[128,1024]{1,0:T(8,128)(2,1)S(1)} %collective-permute-done.10.refs_1_, bf16[128,1024]{1,0:T(8,128)(2,1)S(1)} %collective-permute-done.11.refs_2_, ...), custom_call_target="tpu_custom_call" | custom-call | bytes 1048576 | tf_op jit(solution)/shard_map/pallas_call | solution.py:62
  48.3 8.1 %all-to-all-done.refs_0_ = bf16[8,16,512]{2,1,0:T(8,128)(2,1)S(1)} async-done(((bf16[8,16,512]{2,1,0:T(8,128)(2,1)}), bf16[8,16,512]{2,1,0:T(8,128)(2,1)S(1)}, u32[]{:S(2)}, u32[]{:S(2)}) %all-to-all-start) | async-done | bytes 131104 | tf_op jit(solution)/shard_map/all_to_all | solution.py:267
  56.4 0.6 %shard_map.65 = f32[16,512]{1,0:T(8,128)} custom-call(bf16[8,16,512]{2,1,0:T(8,128)(2,1)S(1)} %all-to-all-done.refs_0_, f32[8,128]{1,0:T(8,128)S(1)} %get-tuple-element.43.refs_1_), custom_call_target="tpu_custom_call" | custom-call | bytes 131072 | tf_op jit(solution)/shard_map/pallas_call | solution.py:62
  (25 shorter events, 0.6 us)
Async XLA Ops:
  0.6 19.9 %copy-start = (s32[512,512]{1,0:T(8,128)S(1)}, s32[512,512]{1,0:T(8,128)}, u32[]{:S(2)}) copy-start(s32[512,512]{1,0:T(8,128)} %refs_0_.3) | copy-start | bytes 3145732
  4.2 8.1 %collective-permute-start = (bf16[2,128,512]{2,1,0:T(8,128)(2,1)}, bf16[2,128,512]{2,1,0:T(8,128)(2,1)S(1)}, u32[]{:S(2)}, u32[]{:S(2)}) collective-permute-start(bf16[2,128,512]{2,1,0:T(8,128)(2,1)} %get-tuple-element.23), channel_id=1, source_target_pairs={{0,64},{1,3},{4,68},{5,7},{8,72},{9,11},{12,76},{13,15},{16,80},{1... | collective-permute-start | bytes 786440 | tf_op jit(solution)/shard_map/ppermute | solution.py:26
  8.0 8.6 %collective-permute-start.4 = (bf16[2,128,512]{2,1,0:T(8,128)(2,1)}, bf16[2,128,512]{2,1,0:T(8,128)(2,1)S(1)}, u32[]{:S(2)}, u32[]{:S(2)}) collective-permute-start(bf16[2,128,512]{2,1,0:T(8,128)(2,1)} %get-tuple-element.28), channel_id=1, source_target_pairs={{0,32},{1,129},{4,36},{5,133},{8,40},{9,137},{12,44},{13,141},{16,... | collective-permute-start | bytes 786440 | tf_op jit(solution)/shard_map/ppermute | solution.py:26
  8.4 12.5 %collective-permute-start.5 = (bf16[2,128,512]{2,1,0:T(8,128)(2,1)}, bf16[2,128,512]{2,1,0:T(8,128)(2,1)S(1)}, u32[]{:S(2)}, u32[]{:S(2)}) collective-permute-start(bf16[2,128,512]{2,1,0:T(8,128)(2,1)} %get-tuple-element.29), channel_id=1, source_target_pairs={{0,96},{1,131},{4,100},{5,135},{8,104},{9,139},{12,108},{13,143},{... | collective-permute-start | bytes 786440 | tf_op jit(solution)/shard_map/ppermute | solution.py:26
  10.7 11.7 %collective-permute-start.6 = (bf16[2,128,512]{2,1,0:T(8,128)(2,1)}, bf16[2,128,512]{2,1,0:T(8,128)(2,1)S(1)}, u32[]{:S(2)}, u32[]{:S(2)}) collective-permute-start(bf16[2,128,512]{2,1,0:T(8,128)(2,1)} %get-tuple-element.30), channel_id=1, source_target_pairs={{0,1},{1,0},{4,5},{5,4},{8,9},{9,8},{12,13},{13,12},{16,17},{17,16... | collective-permute-start | bytes 786440 | tf_op jit(solution)/shard_map/ppermute | solution.py:26
  12.0 12.3 %collective-permute-start.7 = (bf16[2,128,512]{2,1,0:T(8,128)(2,1)}, bf16[2,128,512]{2,1,0:T(8,128)(2,1)S(1)}, u32[]{:S(2)}, u32[]{:S(2)}) collective-permute-start(bf16[2,128,512]{2,1,0:T(8,128)(2,1)} %get-tuple-element.31), channel_id=1, source_target_pairs={{0,129},{1,32},{4,133},{5,36},{8,137},{9,40},{12,141},{13,44},{16,... | collective-permute-start | bytes 786440 | tf_op jit(solution)/shard_map/ppermute | solution.py:26
  12.3 8.1 %copy-start.2 = (f32[256]{0:T(256)S(1)}, f32[256]{0:T(256)}, u32[]{:S(2)}) copy-start(f32[256]{0:T(256)} %param.7) | copy-start | bytes 3076
  12.3 13.8 %collective-permute-start.8 = (bf16[2,128,512]{2,1,0:T(8,128)(2,1)}, bf16[2,128,512]{2,1,0:T(8,128)(2,1)S(1)}, u32[]{:S(2)}, u32[]{:S(2)}) collective-permute-start(bf16[2,128,512]{2,1,0:T(8,128)(2,1)} %get-tuple-element.32), channel_id=1, source_target_pairs={{0,3},{1,64},{4,7},{5,68},{8,11},{9,72},{12,15},{13,76},{16,19},{1... | collective-permute-start | bytes 786440 | tf_op jit(solution)/shard_map/ppermute | solution.py:26
  16.6 9.5 %collective-permute-start.9 = (bf16[2,128,512]{2,1,0:T(8,128)(2,1)}, bf16[2,128,512]{2,1,0:T(8,128)(2,1)S(1)}, u32[]{:S(2)}, u32[]{:S(2)}) collective-permute-start(bf16[2,128,512]{2,1,0:T(8,128)(2,1)} %get-tuple-element.33), channel_id=1, source_target_pairs={{0,131},{1,96},{4,135},{5,100},{8,139},{9,104},{12,143},{13,108},{... | collective-permute-start | bytes 786440 | tf_op jit(solution)/shard_map/ppermute | solution.py:26
  20.6 5.5 %copy-start.1 = (bf16[2,128,512]{2,1,0:T(8,128)(2,1)S(1)}, bf16[2,128,512]{2,1,0:T(8,128)(2,1)}, u32[]{:S(2)}) copy-start(bf16[2,128,512]{2,1,0:T(8,128)(2,1)} %get-tuple-element.27.refs_0_.refs_4_) | copy-start | bytes 786436
  20.9 9.3 %collective-permute-start.1 = (bf16[256,512]{1,0:T(8,128)(2,1)S(1)}, bf16[256,512]{1,0:T(8,128)(2,1)S(1)}, u32[]{:S(2)}, u32[]{:S(2)}) collective-permute-start(bf16[256,512]{1,0:T(8,128)(2,1)S(1)} %get-tuple-element.25), channel_id=1, source_target_pairs={{0,130},{1,97},{4,134},{5,101},{8,138},{9,105},{12,142},{13,109},{... | collective-permute-start | bytes 786440 | tf_op jit(solution)/shard_map/ppermute | solution.py:26
  22.4 11.4 %collective-permute-start.3 = (bf16[256,512]{1,0:T(8,128)(2,1)S(1)}, bf16[256,512]{1,0:T(8,128)(2,1)S(1)}, u32[]{:S(2)}, u32[]{:S(2)}) collective-permute-start(bf16[256,512]{1,0:T(8,128)(2,1)S(1)} %get-tuple-element.26), channel_id=1, source_target_pairs={{1,33},{5,37},{9,41},{13,45},{17,49},{21,53},{25,57},{29,61},{129,... | collective-permute-start | bytes 786440 | tf_op jit(solution)/shard_map/ppermute | solution.py:26
  24.4 9.4 %collective-permute-start.2 = (bf16[256,512]{1,0:T(8,128)(2,1)S(1)}, bf16[256,512]{1,0:T(8,128)(2,1)S(1)}, u32[]{:S(2)}, u32[]{:S(2)}) collective-permute-start(bf16[256,512]{1,0:T(8,128)(2,1)S(1)} %get-tuple-element.26), channel_id=1, source_target_pairs={{0,128},{1,65},{4,132},{5,69},{8,136},{9,73},{12,140},{13,77},{16,... | collective-permute-start | bytes 786440 | tf_op jit(solution)/shard_map/ppermute | solution.py:26
  26.8 10.7 %collective-permute-start.13 = (bf16[128,512]{1,0:T(8,128)(2,1)S(1)}, bf16[128,512]{1,0:T(8,128)(2,1)S(1)}, u32[]{:S(2)}, u32[]{:S(2)}) collective-permute-start(bf16[128,512]{1,0:T(8,128)(2,1)S(1)} %get-tuple-element.40), channel_id=1, source_target_pairs={{0,128},{1,33},{4,132},{5,37},{8,136},{9,41},{12,140},{13,45},{16,... | collective-permute-start | bytes 393224 | tf_op jit(solution)/shard_map/ppermute | solution.py:26
  28.5 9.8 %collective-permute-start.14 = (bf16[128,512]{1,0:T(8,128)(2,1)S(1)}, bf16[128,512]{1,0:T(8,128)(2,1)S(1)}, u32[]{:S(2)}, u32[]{:S(2)}) collective-permute-start(bf16[128,512]{1,0:T(8,128)(2,1)S(1)} %get-tuple-element.41), channel_id=1, source_target_pairs={{0,2},{1,65},{4,6},{5,69},{8,10},{9,73},{12,14},{13,77},{16,18},{1... | collective-permute-start | bytes 393224 | tf_op jit(solution)/shard_map/ppermute | solution.py:26
  30.2 8.1 %collective-permute-start.15 = (bf16[128,512]{1,0:T(8,128)(2,1)S(1)}, bf16[128,512]{1,0:T(8,128)(2,1)S(1)}, u32[]{:S(2)}, u32[]{:S(2)}) collective-permute-start(bf16[128,512]{1,0:T(8,128)(2,1)S(1)} %get-tuple-element.42), channel_id=1, source_target_pairs={{0,130},{1,97},{4,134},{5,101},{8,138},{9,105},{12,142},{13,109},{... | collective-permute-start | bytes 393224 | tf_op jit(solution)/shard_map/ppermute | solution.py:26
  35.4 11.7 %collective-permute-start.10 = (bf16[128,1024]{1,0:T(8,128)(2,1)S(1)}, bf16[128,1024]{1,0:T(8,128)(2,1)S(1)}, u32[]{:S(2)}, u32[]{:S(2)}) collective-permute-start(bf16[128,1024]{1,0:T(8,128)(2,1)S(1)} %get-tuple-element.36), channel_id=1, source_target_pairs={{0,96},{1,131},{4,100},{5,135},{8,104},{9,139},{12,108},{13,143},{... | collective-permute-start | bytes 786440 | tf_op jit(solution)/shard_map/ppermute | solution.py:26
  37.4 9.7 %collective-permute-start.11 = (bf16[128,1024]{1,0:T(8,128)(2,1)S(1)}, bf16[128,1024]{1,0:T(8,128)(2,1)S(1)}, u32[]{:S(2)}, u32[]{:S(2)}) collective-permute-start(bf16[128,1024]{1,0:T(8,128)(2,1)S(1)} %get-tuple-element.37), channel_id=1, source_target_pairs={{0,64},{1,3},{4,68},{5,7},{8,72},{9,11},{12,76},{13,15},{16,80},{1... | collective-permute-start | bytes 786440 | tf_op jit(solution)/shard_map/ppermute | solution.py:26
  37.6 9.6 %collective-permute-start.12 = (bf16[128,1024]{1,0:T(8,128)(2,1)S(1)}, bf16[128,1024]{1,0:T(8,128)(2,1)S(1)}, u32[]{:S(2)}, u32[]{:S(2)}) collective-permute-start(bf16[128,1024]{1,0:T(8,128)(2,1)S(1)} %get-tuple-element.38), channel_id=1, source_target_pairs={{0,32},{1,129},{4,36},{5,133},{8,40},{9,137},{12,44},{13,141},{16,... | collective-permute-start | bytes 786440 | tf_op jit(solution)/shard_map/ppermute | solution.py:26
  39.0 17.4 %all-to-all-start = ((bf16[8,16,512]{2,1,0:T(8,128)(2,1)}), bf16[8,16,512]{2,1,0:T(8,128)(2,1)S(1)}, u32[]{:S(2)}, u32[]{:S(2)}) async-start(bf16[8,16,512]{2,1,0:T(8,128)(2,1)} %bitcast), calls=%async_computation | async-start | bytes 262144 | tf_op jit(solution)/shard_map/all_to_all | solution.py:267

commit v5 on v4

--- a/solution.py
+++ b/solution.py
@@ -69,6 +69,16 @@
         cost_estimate=pl.CostEstimate(flops=0, bytes_accessed=moved_bytes, transcendentals=0),
         compiler_params=pltpu.CompilerParams(vmem_limit_bytes=vmem * 2**20),
     )(*arrays, *after)
+
+
+def held_until(value, after):
+    return pl.pallas_call(
+        lambda *refs: None,
+        out_shape=jax.ShapeDtypeStruct(value.shape, value.dtype),
+        in_specs=[pl.BlockSpec(memory_space=pl.ANY)] * 2,
+        out_specs=pl.BlockSpec(memory_space=pl.ANY),
+        input_output_aliases={0: 0},
+    )(value, after)
 
 
 def start(multiple, factor):
@@ -223,6 +233,9 @@
         vmem=60,
     )
     first = [packed[0]] + [in_first_ring(packed[s], s) for s in shifts]
+    packed = list(packed)
+    packed[NX + 0] = held_until(packed[NX + 0], first[1])
+    packed[NX + 3] = held_until(packed[NX + 3], first[2])
     second = [to_other_core(packed[NX])] + [in_other_ring(packed[NX + s], s) for s in shifts]
 
     part = cols // NY

time: 57.3 us -> 57 us (level)
  local copies, waits for them, and re-layouts: 0.21 us -> 1.64 us
  starting transfers between devices: 36.5 us -> 35.6 us
  waiting for transfers between devices: 10.9 us -> 10.1 us
    unnamed x6 -> x14, local copies, waits for them, and re-layouts: 0.01 us -> 1.44 us
    ppermute x16, starting transfers between devices: 28.3 us -> 27.5 us  [moved(): return lax.ppermute(value, AXES, moves)]
    all_to_all x1, waiting for transfers between devices: 8.09 us -> 7.31 us  [per_device(): ring = lax.all_to_all(column, 'z', split_axis=0, concat_axis=0, tiled=True)]
where the time goes in v5:
time: 57 us; the launch traced here: 56.8 us
  starting transfers between devices  35.6 us (62%)
  waiting for transfers between devices  10.1 us (18%)
  Pallas kernels  8.53 us (15%)
  local copies, waits for them, and re-layouts  1.64 us (3%)
  between operations  0.79 us (1%)
    ppermute x16, starting transfers between devices, moved(): return lax.ppermute(value, AXES, moves)  27.5 us
    pallas_call x7, Pallas kernels, call(): pl.pallas_call(body, out_shape=outs, in_specs=[pl.BlockSpec(memory_space=...  8.53 us
    all_to_all x1, starting transfers between devices, per_device(): ring = lax.all_to_all(column, 'z', split_axis=0, concat_axis=0, tiled=True)  8.2 us
    all_to_all x1, waiting for transfers between devices, per_device(): ring = lax.all_to_all(column, 'z', split_axis=0, concat_axis=0, tiled=True)  7.31 us
    ppermute x16, waiting for transfers between devices, moved(): return lax.ppermute(value, AXES, moves)  2.84 us
    unnamed x14, local copies, waits for them, and re-layouts  1.44 us
  transfers between devices with their start and end apart: 17, of which 2 were waited for; matrix products, arithmetic and copies ran while one was open for 0% of the time, Pallas kernels for 8%

profile of v5, /device:TPU:1, one launch (start us, length us, event | category | flops | bytes accessed | tf_op | source)
XLA Modules:
  0.0 56.8 jit_solution(2892589760579109379)
XLA Ops:
  0.6 3.4 %shard_map.59 = (bf16[2,128,512]{2,1,0:T(8,128)(2,1)}, bf16[2,128,512]{2,1,0:T(8,128)(2,1)}, bf16[2,128,512]{2,1,0:T(8,128)(2,1)}, bf16[2,128,512]{2,1,0:T(8,128...) custom-call(bf16[128,4096]{1,0:T(8,128)(2,1)} %refs_0_.2, ...), custom_call_target="tpu_custom_call" | custom-call | bytes 1179648 | tf_op jit(solution)/shard_map/pallas_call | solution.py:62
  4.1 3.8 %collective-permute-start = (bf16[2,128,512]{2,1,0:T(8,128)(2,1)}, bf16[2,128,512]{2,1,0:T(8,128)(2,1)S(1)}, u32[]{:S(2)}, u32[]{:S(2)}) collective-permute-start(bf16[2,128,512]{2,1,0:T(8,128)(2,1)} %get-tuple-element.23), channel_id=1, source_target_pairs={{0,64},{1,3},{4,68},{5,7},{8,72},{9,11},{12,76},{13,15},{16,80},{1... | collective-permute-start | bytes 786440 | tf_op jit(solution)/shard_map/ppermute | solution.py:26
  8.3 2.3 %collective-permute-start.5 = (bf16[2,128,512]{2,1,0:T(8,128)(2,1)}, bf16[2,128,512]{2,1,0:T(8,128)(2,1)S(1)}, u32[]{:S(2)}, u32[]{:S(2)}) collective-permute-start(bf16[2,128,512]{2,1,0:T(8,128)(2,1)} %get-tuple-element.29), channel_id=1, source_target_pairs={{0,96},{1,131},{4,100},{5,135},{8,104},{9,139},{12,108},{13,143},{... | collective-permute-start | bytes 786440 | tf_op jit(solution)/shard_map/ppermute | solution.py:26
  10.9 1.9 %collective-permute-start.8 = (bf16[2,128,512]{2,1,0:T(8,128)(2,1)}, bf16[2,128,512]{2,1,0:T(8,128)(2,1)S(1)}, u32[]{:S(2)}, u32[]{:S(2)}) collective-permute-start(bf16[2,128,512]{2,1,0:T(8,128)(2,1)} %get-tuple-element.32), channel_id=1, source_target_pairs={{0,3},{1,64},{4,7},{5,68},{8,11},{9,72},{12,15},{13,76},{16,19},{1... | collective-permute-start | bytes 786440 | tf_op jit(solution)/shard_map/ppermute | solution.py:26
  12.8 0.7 %copy-done = bf16[2,128,512]{2,1,0:T(8,128)(2,1)} copy-done((bf16[2,128,512]{2,1,0:T(8,128)(2,1)}, bf16[2,128,512]{2,1,0:T(8,128)(2,1)S(1)}, u32[]{:S(2)}) %copy-start) | copy-done | bytes 262168
  13.5 4.9 %collective-permute-start.9 = (bf16[2,128,512]{2,1,0:T(8,128)(2,1)}, bf16[2,128,512]{2,1,0:T(8,128)(2,1)S(1)}, u32[]{:S(2)}, u32[]{:S(2)}) collective-permute-start(bf16[2,128,512]{2,1,0:T(8,128)(2,1)} %shard_map.62), channel_id=1, source_target_pairs={{0,131},{1,96},{4,135},{5,100},{8,139},{9,104},{12,143},{13,108},{... | collective-permute-start | bytes 786440 | tf_op jit(solution)/shard_map/ppermute | solution.py:26
  18.4 0.7 %copy-done.2 = bf16[2,128,512]{2,1,0:T(8,128)(2,1)} copy-done((bf16[2,128,512]{2,1,0:T(8,128)(2,1)}, bf16[2,128,512]{2,1,0:T(8,128)(2,1)S(1)}, u32[]{:S(2)}) %copy-start.2) | copy-done | bytes 262168
  19.1 1.8 %collective-permute-start.6 = (bf16[2,128,512]{2,1,0:T(8,128)(2,1)}, bf16[2,128,512]{2,1,0:T(8,128)(2,1)S(1)}, u32[]{:S(2)}, u32[]{:S(2)}) collective-permute-start(bf16[2,128,512]{2,1,0:T(8,128)(2,1)} %shard_map.61), channel_id=1, source_target_pairs={{0,1},{1,0},{4,5},{5,4},{8,9},{9,8},{12,13},{13,12},{16,17},{17,16... | collective-permute-start | bytes 786440 | tf_op jit(solution)/shard_map/ppermute | solution.py:26
  21.4 1.5 %collective-permute-start.1 = (bf16[256,512]{1,0:T(8,128)(2,1)S(1)}, bf16[256,512]{1,0:T(8,128)(2,1)S(1)}, u32[]{:S(2)}, u32[]{:S(2)}) collective-permute-start(bf16[256,512]{1,0:T(8,128)(2,1)S(1)} %get-tuple-element.25), channel_id=1, source_target_pairs={{0,130},{1,97},{4,134},{5,101},{8,138},{9,105},{12,142},{13,109},{... | collective-permute-start | bytes 786440 | tf_op jit(solution)/shard_map/ppermute | solution.py:26
  23.0 1.9 %collective-permute-start.3 = (bf16[256,512]{1,0:T(8,128)(2,1)S(1)}, bf16[256,512]{1,0:T(8,128)(2,1)S(1)}, u32[]{:S(2)}, u32[]{:S(2)}) collective-permute-start(bf16[256,512]{1,0:T(8,128)(2,1)S(1)} %get-tuple-element.26), channel_id=1, source_target_pairs={{1,33},{5,37},{9,41},{13,45},{17,49},{21,53},{25,57},{29,61},{129,... | collective-permute-start | bytes 786440 | tf_op jit(solution)/shard_map/ppermute | solution.py:26
  24.9 2.5 %collective-permute-start.2 = (bf16[256,512]{1,0:T(8,128)(2,1)S(1)}, bf16[256,512]{1,0:T(8,128)(2,1)S(1)}, u32[]{:S(2)}, u32[]{:S(2)}) collective-permute-start(bf16[256,512]{1,0:T(8,128)(2,1)S(1)} %get-tuple-element.26), channel_id=1, source_target_pairs={{0,128},{1,65},{4,132},{5,69},{8,136},{9,73},{12,140},{13,77},{16,... | collective-permute-start | bytes 786440 | tf_op jit(solution)/shard_map/ppermute | solution.py:26
  27.4 0.8 %shard_map.63 = (f32[128,512]{1,0:T(8,128)S(1)}, bf16[128,512]{1,0:T(8,128)(2,1)S(1)}, bf16[128,512]{1,0:T(8,128)(2,1)S(1)}, bf16[128,512]{1,0:T(8,128)(2,1)S(1)}) custom-call(bf16[2,128,512]{2,1,0:T(8,128)(2,1)S(1)} %copy-done.5, bf16[2,128,512]{2,1,0:T(8,128)(2,1)S(1)} %copy-done.3, bf16[2,128,512]{2,1,0:T(8,128)(2,1)S(1)} %copy-done.1, ...), custom_call_target="tpu_custom_call" | custom-call | bytes 2097152 | tf_op jit(solution)/shard_map/pallas_call | solution.py:62
  28.2 0.9 %collective-permute-start.13 = (bf16[128,512]{1,0:T(8,128)(2,1)S(1)}, bf16[128,512]{1,0:T(8,128)(2,1)S(1)}, u32[]{:S(2)}, u32[]{:S(2)}) collective-permute-start(bf16[128,512]{1,0:T(8,128)(2,1)S(1)} %get-tuple-element.40), channel_id=1, source_target_pairs={{0,128},{1,33},{4,132},{5,37},{8,136},{9,41},{12,140},{13,45},{16,... | collective-permute-start | bytes 393224 | tf_op jit(solution)/shard_map/ppermute | solution.py:26
  29.1 1.5 %collective-permute-start.14 = (bf16[128,512]{1,0:T(8,128)(2,1)S(1)}, bf16[128,512]{1,0:T(8,128)(2,1)S(1)}, u32[]{:S(2)}, u32[]{:S(2)}) collective-permute-start(bf16[128,512]{1,0:T(8,128)(2,1)S(1)} %get-tuple-element.41), channel_id=1, source_target_pairs={{0,2},{1,65},{4,6},{5,69},{8,10},{9,73},{12,14},{13,77},{16,18},{1... | collective-permute-start | bytes 393224 | tf_op jit(solution)/shard_map/ppermute | solution.py:26
  30.6 1.0 %collective-permute-start.15 = (bf16[128,512]{1,0:T(8,128)(2,1)S(1)}, bf16[128,512]{1,0:T(8,128)(2,1)S(1)}, u32[]{:S(2)}, u32[]{:S(2)}) collective-permute-start(bf16[128,512]{1,0:T(8,128)(2,1)S(1)} %get-tuple-element.42), channel_id=1, source_target_pairs={{0,130},{1,97},{4,134},{5,101},{8,138},{9,105},{12,142},{13,109},{... | collective-permute-start | bytes 393224 | tf_op jit(solution)/shard_map/ppermute | solution.py:26
  31.6 2.8 %collective-permute-done.3.refs_3_ = bf16[256,512]{1,0:T(8,128)(2,1)S(1)} collective-permute-done((bf16[256,512]{1,0:T(8,128)(2,1)S(1)}, bf16[256,512]{1,0:T(8,128)(2,1)S(1)}, u32[]{:S(2)}, u32[]{:S(2)}) %collective-permute-start.3) | collective-permute-done | bytes 262176 | tf_op jit(solution)/shard_map/ppermute | solution.py:26
  34.4 1.6 %shard_map.64 = (bf16[128,1024]{1,0:T(8,128)(2,1)S(1)}, bf16[128,1024]{1,0:T(8,128)(2,1)S(1)}, bf16[128,1024]{1,0:T(8,128)(2,1)S(1)}, bf16[128,1024]{1,0:T(8,128)(2,1)S(1)}) custom-call(bf16[512,512]{1,0:T(8,128)(2,1)S(1)} %get-tuple-element.24.refs_0_, bf16[256,512]{1,0:T(8,128)(2,1)S(1)} %collective-permute-done.1.refs_1_, ...), custom_call_target="tpu_custom_call" | custom-call | bytes 2359296 | tf_op jit(solution)/shard_map/pallas_call | solution.py:62
  36.0 1.5 %collective-permute-start.10 = (bf16[128,1024]{1,0:T(8,128)(2,1)S(1)}, bf16[128,1024]{1,0:T(8,128)(2,1)S(1)}, u32[]{:S(2)}, u32[]{:S(2)}) collective-permute-start(bf16[128,1024]{1,0:T(8,128)(2,1)S(1)} %get-tuple-element.36), channel_id=1, source_target_pairs={{0,96},{1,131},{4,100},{5,135},{8,104},{9,139},{12,108},{13,143},{... | collective-permute-start | bytes 786440 | tf_op jit(solution)/shard_map/ppermute | solution.py:26
  37.5 1.2 %collective-permute-start.11 = (bf16[128,1024]{1,0:T(8,128)(2,1)S(1)}, bf16[128,1024]{1,0:T(8,128)(2,1)S(1)}, u32[]{:S(2)}, u32[]{:S(2)}) collective-permute-start(bf16[128,1024]{1,0:T(8,128)(2,1)S(1)} %get-tuple-element.37), channel_id=1, source_target_pairs={{0,64},{1,3},{4,68},{5,7},{8,72},{9,11},{12,76},{13,15},{16,80},{1... | collective-permute-start | bytes 786440 | tf_op jit(solution)/shard_map/ppermute | solution.py:26
  38.8 0.7 %shard_map.66 = bf16[128,512]{1,0:T(8,128)(2,1)} custom-call(f32[128,512]{1,0:T(8,128)S(1)} %get-tuple-element.34.refs_8_.refs_0_, bf16[128,512]{1,0:T(8,128)(2,1)S(1)} %collective-permute-done.13.refs_1_, bf16[128,512]{1,0:T(8,128)(2,1)S(1)} %collective-permute-done.14.refs_2_, bf16[128,512]{1,0:T(8,128)(2,1)S(1)} %collective-permute-done.15.refs_3_, ...), custom_call_target="tpu_custom_call" | custom-call | bytes 655360 | tf_op jit(solution)/shard_map/pallas_call | solution.py:62
  39.5 8.2 %all-to-all-start = ((bf16[8,16,512]{2,1,0:T(8,128)(2,1)}), bf16[8,16,512]{2,1,0:T(8,128)(2,1)S(1)}, u32[]{:S(2)}, u32[]{:S(2)}) async-start(bf16[8,16,512]{2,1,0:T(8,128)(2,1)} %bitcast), calls=%async_computation | async-start | bytes 262144 | tf_op jit(solution)/shard_map/all_to_all | solution.py:280
  47.7 1.1 %shard_map.65 = (bf16[128,4096]{1,0:T(8,128)(2,1)}, f32[8,128]{1,0:T(8,128)S(1)}) custom-call(bf16[128,1024]{1,0:T(8,128)(2,1)S(1)} %get-tuple-element.35.refs_0_.refs_4_, bf16[128,1024]{1,0:T(8,128)(2,1)S(1)} %collective-permute-done.10.refs_1_, bf16[128,1024]{1,0:T(8,128)(2,1)S(1)} %collective-permute-done.11.refs_2_, ...), custom_call_target="tpu_custom_call" | custom-call | bytes 1048576 | tf_op jit(solution)/shard_map/pallas_call | solution.py:62
  48.8 7.3 %all-to-all-done.refs_0_ = bf16[8,16,512]{2,1,0:T(8,128)(2,1)S(1)} async-done(((bf16[8,16,512]{2,1,0:T(8,128)(2,1)}), bf16[8,16,512]{2,1,0:T(8,128)(2,1)S(1)}, u32[]{:S(2)}, u32[]{:S(2)}) %all-to-all-start) | async-done | bytes 131104 | tf_op jit(solution)/shard_map/all_to_all | solution.py:280
  56.1 0.6 %shard_map.67 = f32[16,512]{1,0:T(8,128)} custom-call(bf16[8,16,512]{2,1,0:T(8,128)(2,1)S(1)} %all-to-all-done.refs_0_, f32[8,128]{1,0:T(8,128)S(1)} %get-tuple-element.43.refs_1_), custom_call_target="tpu_custom_call" | custom-call | bytes 131072 | tf_op jit(solution)/shard_map/pallas_call | solution.py:62
  (35 shorter events, 1.3 us)
Async XLA Ops:
  4.1 8.7 %collective-permute-start = (bf16[2,128,512]{2,1,0:T(8,128)(2,1)}, bf16[2,128,512]{2,1,0:T(8,128)(2,1)S(1)}, u32[]{:S(2)}, u32[]{:S(2)}) collective-permute-start(bf16[2,128,512]{2,1,0:T(8,128)(2,1)} %get-tuple-element.23), channel_id=1, source_target_pairs={{0,64},{1,3},{4,68},{5,7},{8,72},{9,11},{12,76},{13,15},{16,80},{1... | collective-permute-start | bytes 786440 | tf_op jit(solution)/shard_map/ppermute | solution.py:26
  7.9 10.5 %collective-permute-start.4 = (bf16[2,128,512]{2,1,0:T(8,128)(2,1)}, bf16[2,128,512]{2,1,0:T(8,128)(2,1)S(1)}, u32[]{:S(2)}, u32[]{:S(2)}) collective-permute-start(bf16[2,128,512]{2,1,0:T(8,128)(2,1)} %get-tuple-element.28), channel_id=1, source_target_pairs={{0,32},{1,129},{4,36},{5,133},{8,40},{9,137},{12,44},{13,141},{16,... | collective-permute-start | bytes 786440 | tf_op jit(solution)/shard_map/ppermute | solution.py:26
  8.3 13.1 %collective-permute-start.5 = (bf16[2,128,512]{2,1,0:T(8,128)(2,1)}, bf16[2,128,512]{2,1,0:T(8,128)(2,1)S(1)}, u32[]{:S(2)}, u32[]{:S(2)}) collective-permute-start(bf16[2,128,512]{2,1,0:T(8,128)(2,1)} %get-tuple-element.29), channel_id=1, source_target_pairs={{0,96},{1,131},{4,100},{5,135},{8,104},{9,139},{12,108},{13,143},{... | collective-permute-start | bytes 786440 | tf_op jit(solution)/shard_map/ppermute | solution.py:26
  10.6 12.4 %collective-permute-start.7 = (bf16[2,128,512]{2,1,0:T(8,128)(2,1)}, bf16[2,128,512]{2,1,0:T(8,128)(2,1)S(1)}, u32[]{:S(2)}, u32[]{:S(2)}) collective-permute-start(bf16[2,128,512]{2,1,0:T(8,128)(2,1)} %get-tuple-element.31), channel_id=1, source_target_pairs={{0,129},{1,32},{4,133},{5,36},{8,137},{9,40},{12,141},{13,44},{16,... | collective-permute-start | bytes 786440 | tf_op jit(solution)/shard_map/ppermute | solution.py:26
  10.9 14.0 %collective-permute-start.8 = (bf16[2,128,512]{2,1,0:T(8,128)(2,1)}, bf16[2,128,512]{2,1,0:T(8,128)(2,1)S(1)}, u32[]{:S(2)}, u32[]{:S(2)}) collective-permute-start(bf16[2,128,512]{2,1,0:T(8,128)(2,1)} %get-tuple-element.32), channel_id=1, source_target_pairs={{0,3},{1,64},{4,7},{5,68},{8,11},{9,72},{12,15},{13,76},{16,19},{1... | collective-permute-start | bytes 786440 | tf_op jit(solution)/shard_map/ppermute | solution.py:26
  12.8 0.7 %copy-start = (bf16[2,128,512]{2,1,0:T(8,128)(2,1)}, bf16[2,128,512]{2,1,0:T(8,128)(2,1)S(1)}, u32[]{:S(2)}) copy-start(bf16[2,128,512]{2,1,0:T(8,128)(2,1)S(1)} %collective-permute-done.refs_2_.refs_1_.refs_6_) | copy-start | bytes 786436
  13.5 7.6 %copy-start.4 = (s32[512,512]{1,0:T(8,128)S(1)}, s32[512,512]{1,0:T(8,128)}, u32[]{:S(2)}) copy-start(s32[512,512]{1,0:T(8,128)} %refs_0_.3) | copy-start | bytes 3145732
  13.5 13.9 %collective-permute-start.9 = (bf16[2,128,512]{2,1,0:T(8,128)(2,1)}, bf16[2,128,512]{2,1,0:T(8,128)(2,1)S(1)}, u32[]{:S(2)}, u32[]{:S(2)}) collective-permute-start(bf16[2,128,512]{2,1,0:T(8,128)(2,1)} %shard_map.62), channel_id=1, source_target_pairs={{0,131},{1,96},{4,135},{5,100},{8,139},{9,104},{12,143},{13,108},{... | collective-permute-start | bytes 786440 | tf_op jit(solution)/shard_map/ppermute | solution.py:26
  18.4 0.7 %copy-start.2 = (bf16[2,128,512]{2,1,0:T(8,128)(2,1)}, bf16[2,128,512]{2,1,0:T(8,128)(2,1)S(1)}, u32[]{:S(2)}) copy-start(bf16[2,128,512]{2,1,0:T(8,128)(2,1)S(1)} %collective-permute-done.4.refs_1_.refs_5_) | copy-start | bytes 786436
  19.1 1.8 %copy-start.6 = (f32[256]{0:T(256)S(1)}, f32[256]{0:T(256)}, u32[]{:S(2)}) copy-start(f32[256]{0:T(256)} %param.7) | copy-start | bytes 3076
  19.1 2.0 %copy-start.1 = (bf16[2,128,512]{2,1,0:T(8,128)(2,1)S(1)}, bf16[2,128,512]{2,1,0:T(8,128)(2,1)}, u32[]{:S(2)}) copy-start(bf16[2,128,512]{2,1,0:T(8,128)(2,1)} %copy-done) | copy-start | bytes 786436
  19.1 8.3 %collective-permute-start.6 = (bf16[2,128,512]{2,1,0:T(8,128)(2,1)}, bf16[2,128,512]{2,1,0:T(8,128)(2,1)S(1)}, u32[]{:S(2)}, u32[]{:S(2)}) collective-permute-start(bf16[2,128,512]{2,1,0:T(8,128)(2,1)} %shard_map.61), channel_id=1, source_target_pairs={{0,1},{1,0},{4,5},{5,4},{8,9},{9,8},{12,13},{13,12},{16,17},{17,16... | collective-permute-start | bytes 786440 | tf_op jit(solution)/shard_map/ppermute | solution.py:26
  21.1 6.3 %copy-start.3 = (bf16[2,128,512]{2,1,0:T(8,128)(2,1)S(1)}, bf16[2,128,512]{2,1,0:T(8,128)(2,1)}, u32[]{:S(2)}) copy-start(bf16[2,128,512]{2,1,0:T(8,128)(2,1)} %copy-done.2) | copy-start | bytes 786436
  21.1 6.3 %copy-start.5 = (bf16[2,128,512]{2,1,0:T(8,128)(2,1)S(1)}, bf16[2,128,512]{2,1,0:T(8,128)(2,1)}, u32[]{:S(2)}) copy-start(bf16[2,128,512]{2,1,0:T(8,128)(2,1)} %get-tuple-element.27.refs_0_.refs_4_) | copy-start | bytes 786436
  21.4 9.2 %collective-permute-start.1 = (bf16[256,512]{1,0:T(8,128)(2,1)S(1)}, bf16[256,512]{1,0:T(8,128)(2,1)S(1)}, u32[]{:S(2)}, u32[]{:S(2)}) collective-permute-start(bf16[256,512]{1,0:T(8,128)(2,1)S(1)} %get-tuple-element.25), channel_id=1, source_target_pairs={{0,130},{1,97},{4,134},{5,101},{8,138},{9,105},{12,142},{13,109},{... | collective-permute-start | bytes 786440 | tf_op jit(solution)/shard_map/ppermute | solution.py:26
  23.0 11.4 %collective-permute-start.3 = (bf16[256,512]{1,0:T(8,128)(2,1)S(1)}, bf16[256,512]{1,0:T(8,128)(2,1)S(1)}, u32[]{:S(2)}, u32[]{:S(2)}) collective-permute-start(bf16[256,512]{1,0:T(8,128)(2,1)S(1)} %get-tuple-element.26), channel_id=1, source_target_pairs={{1,33},{5,37},{9,41},{13,45},{17,49},{21,53},{25,57},{29,61},{129,... | collective-permute-start | bytes 786440 | tf_op jit(solution)/shard_map/ppermute | solution.py:26
  24.9 9.5 %collective-permute-start.2 = (bf16[256,512]{1,0:T(8,128)(2,1)S(1)}, bf16[256,512]{1,0:T(8,128)(2,1)S(1)}, u32[]{:S(2)}, u32[]{:S(2)}) collective-permute-start(bf16[256,512]{1,0:T(8,128)(2,1)S(1)} %get-tuple-element.26), channel_id=1, source_target_pairs={{0,128},{1,65},{4,132},{5,69},{8,136},{9,73},{12,140},{13,77},{16,... | collective-permute-start | bytes 786440 | tf_op jit(solution)/shard_map/ppermute | solution.py:26
  28.2 10.5 %collective-permute-start.13 = (bf16[128,512]{1,0:T(8,128)(2,1)S(1)}, bf16[128,512]{1,0:T(8,128)(2,1)S(1)}, u32[]{:S(2)}, u32[]{:S(2)}) collective-permute-start(bf16[128,512]{1,0:T(8,128)(2,1)S(1)} %get-tuple-element.40), channel_id=1, source_target_pairs={{0,128},{1,33},{4,132},{5,37},{8,136},{9,41},{12,140},{13,45},{16,... | collective-permute-start | bytes 393224 | tf_op jit(solution)/shard_map/ppermute | solution.py:26
  29.1 9.6 %collective-permute-start.14 = (bf16[128,512]{1,0:T(8,128)(2,1)S(1)}, bf16[128,512]{1,0:T(8,128)(2,1)S(1)}, u32[]{:S(2)}, u32[]{:S(2)}) collective-permute-start(bf16[128,512]{1,0:T(8,128)(2,1)S(1)} %get-tuple-element.41), channel_id=1, source_target_pairs={{0,2},{1,65},{4,6},{5,69},{8,10},{9,73},{12,14},{13,77},{16,18},{1... | collective-permute-start | bytes 393224 | tf_op jit(solution)/shard_map/ppermute | solution.py:26
  30.6 8.2 %collective-permute-start.15 = (bf16[128,512]{1,0:T(8,128)(2,1)S(1)}, bf16[128,512]{1,0:T(8,128)(2,1)S(1)}, u32[]{:S(2)}, u32[]{:S(2)}) collective-permute-start(bf16[128,512]{1,0:T(8,128)(2,1)S(1)} %get-tuple-element.42), channel_id=1, source_target_pairs={{0,130},{1,97},{4,134},{5,101},{8,138},{9,105},{12,142},{13,109},{... | collective-permute-start | bytes 393224 | tf_op jit(solution)/shard_map/ppermute | solution.py:26
  36.0 11.7 %collective-permute-start.10 = (bf16[128,1024]{1,0:T(8,128)(2,1)S(1)}, bf16[128,1024]{1,0:T(8,128)(2,1)S(1)}, u32[]{:S(2)}, u32[]{:S(2)}) collective-permute-start(bf16[128,1024]{1,0:T(8,128)(2,1)S(1)} %get-tuple-element.36), channel_id=1, source_target_pairs={{0,96},{1,131},{4,100},{5,135},{8,104},{9,139},{12,108},{13,143},{... | collective-permute-start | bytes 786440 | tf_op jit(solution)/shard_map/ppermute | solution.py:26
  37.5 10.2 %collective-permute-start.11 = (bf16[128,1024]{1,0:T(8,128)(2,1)S(1)}, bf16[128,1024]{1,0:T(8,128)(2,1)S(1)}, u32[]{:S(2)}, u32[]{:S(2)}) collective-permute-start(bf16[128,1024]{1,0:T(8,128)(2,1)S(1)} %get-tuple-element.37), channel_id=1, source_target_pairs={{0,64},{1,3},{4,68},{5,7},{8,72},{9,11},{12,76},{13,15},{16,80},{1... | collective-permute-start | bytes 786440 | tf_op jit(solution)/shard_map/ppermute | solution.py:26
  38.7 8.9 %collective-permute-start.12 = (bf16[128,1024]{1,0:T(8,128)(2,1)S(1)}, bf16[128,1024]{1,0:T(8,128)(2,1)S(1)}, u32[]{:S(2)}, u32[]{:S(2)}) collective-permute-start(bf16[128,1024]{1,0:T(8,128)(2,1)S(1)} %get-tuple-element.38), channel_id=1, source_target_pairs={{0,32},{1,129},{4,36},{5,133},{8,40},{9,137},{12,44},{13,141},{16,... | collective-permute-start | bytes 786440 | tf_op jit(solution)/shard_map/ppermute | solution.py:26
  39.5 16.6 %all-to-all-start = ((bf16[8,16,512]{2,1,0:T(8,128)(2,1)}), bf16[8,16,512]{2,1,0:T(8,128)(2,1)S(1)}, u32[]{:S(2)}, u32[]{:S(2)}) async-start(bf16[8,16,512]{2,1,0:T(8,128)(2,1)} %bitcast), calls=%async_computation | async-start | bytes 262144 | tf_op jit(solution)/shard_map/all_to_all | solution.py:280

commit v6 on v5

--- a/solution.py
+++ b/solution.py
@@ -173,10 +173,17 @@
         at = jnp.where(on_0, first, lax.rem(x + k, NX))
         weight_ref[pl.ds(start(at, half), half), :] = part
     n = len(refs) // 2
-    for block, out in zip(refs[:n], refs[n:]):
-        out[...] = lax.dot_general(
-            block[1], weight_ref[...], (((1,), (1,)), ((), ())), preferred_element_type=F32
+    cots = jnp.concatenate([block[1] for block in refs[:n]], axis=0)
+    tokens = cots.shape[0] // n
+    for k in range(4):
+        product = lax.dot_general(
+            cots,
+            weight_ref[k * half : (k + 1) * half, :],
+            (((1,), (1,)), ((), ())),
+            preferred_element_type=F32,
         ).astype(BF16)
+        for s, out in enumerate(refs[n:]):
+            out[:, k * half : (k + 1) * half] = product[s * tokens : (s + 1) * tokens]
 
 
 def laid_kernel(rows, place, *refs):

time: 57 us -> 56.4 us (0.989)
  Pallas kernels: 8.53 us -> 7.78 us
    pallas_call x7, Pallas kernels: 8.53 us -> 7.78 us  [call(): pl.pallas_call(body, out_shape=outs, in_specs=[pl.BlockSpec(memory_space=...]
  transfers between devices with their start and end apart: 17 -> 17, of which waited for: 2 -> 2; matrix products, arithmetic and copies ran while one was open for 0% -> 0% of each run, Pallas kernels for 8% -> 7%
where the time goes in v6:
time: 56.4 us; the launch traced here: 56.2 us
  starting transfers between devices  35.7 us (63%)
  waiting for transfers between devices  10.2 us (18%)
  Pallas kernels  7.78 us (14%)
  local copies, waits for them, and re-layouts  1.64 us (3%)
  between operations  0.78 us (1%)
    ppermute x16, starting transfers between devices, moved(): return lax.ppermute(value, AXES, moves)  27.5 us
    all_to_all x1, starting transfers between devices, per_device(): ring = lax.all_to_all(column, 'z', split_axis=0, concat_axis=0, tiled=True)  8.18 us
    pallas_call x7, Pallas kernels, call(): pl.pallas_call(body, out_shape=outs, in_specs=[pl.BlockSpec(memory_space=...  7.78 us
    all_to_all x1, waiting for transfers between devices, per_device(): ring = lax.all_to_all(column, 'z', split_axis=0, concat_axis=0, tiled=True)  7.4 us
    ppermute x16, waiting for transfers between devices, moved(): return lax.ppermute(value, AXES, moves)  2.84 us
    unnamed x14, local copies, waits for them, and re-layouts  1.44 us
  transfers between devices with their start and end apart: 17, of which 2 were waited for; matrix products, arithmetic and copies ran while one was open for 0% of the time, Pallas kernels for 7%

profile of v6, /device:TPU:1, one launch (start us, length us, event | category | flops | bytes accessed | tf_op | source)
XLA Modules:
  0.0 56.2 jit_solution(3794107130560730861)
XLA Ops:
  0.6 3.4 %shard_map.59 = (bf16[2,128,512]{2,1,0:T(8,128)(2,1)}, bf16[2,128,512]{2,1,0:T(8,128)(2,1)}, bf16[2,128,512]{2,1,0:T(8,128)(2,1)}, bf16[2,128,512]{2,1,0:T(8,128...) custom-call(bf16[128,4096]{1,0:T(8,128)(2,1)} %refs_0_.2, ...), custom_call_target="tpu_custom_call" | custom-call | bytes 1179648 | tf_op jit(solution)/shard_map/pallas_call | solution.py:62
  4.1 3.8 %collective-permute-start = (bf16[2,128,512]{2,1,0:T(8,128)(2,1)}, bf16[2,128,512]{2,1,0:T(8,128)(2,1)S(1)}, u32[]{:S(2)}, u32[]{:S(2)}) collective-permute-start(bf16[2,128,512]{2,1,0:T(8,128)(2,1)} %get-tuple-element.23), channel_id=1, source_target_pairs={{0,64},{1,3},{4,68},{5,7},{8,72},{9,11},{12,76},{13,15},{16,80},{1... | collective-permute-start | bytes 786440 | tf_op jit(solution)/shard_map/ppermute | solution.py:26
  8.3 2.3 %collective-permute-start.5 = (bf16[2,128,512]{2,1,0:T(8,128)(2,1)}, bf16[2,128,512]{2,1,0:T(8,128)(2,1)S(1)}, u32[]{:S(2)}, u32[]{:S(2)}) collective-permute-start(bf16[2,128,512]{2,1,0:T(8,128)(2,1)} %get-tuple-element.29), channel_id=1, source_target_pairs={{0,96},{1,131},{4,100},{5,135},{8,104},{9,139},{12,108},{13,143},{... | collective-permute-start | bytes 786440 | tf_op jit(solution)/shard_map/ppermute | solution.py:26
  10.9 1.9 %collective-permute-start.8 = (bf16[2,128,512]{2,1,0:T(8,128)(2,1)}, bf16[2,128,512]{2,1,0:T(8,128)(2,1)S(1)}, u32[]{:S(2)}, u32[]{:S(2)}) collective-permute-start(bf16[2,128,512]{2,1,0:T(8,128)(2,1)} %get-tuple-element.32), channel_id=1, source_target_pairs={{0,3},{1,64},{4,7},{5,68},{8,11},{9,72},{12,15},{13,76},{16,19},{1... | collective-permute-start | bytes 786440 | tf_op jit(solution)/shard_map/ppermute | solution.py:26
  12.8 0.7 %copy-done = bf16[2,128,512]{2,1,0:T(8,128)(2,1)} copy-done((bf16[2,128,512]{2,1,0:T(8,128)(2,1)}, bf16[2,128,512]{2,1,0:T(8,128)(2,1)S(1)}, u32[]{:S(2)}) %copy-start) | copy-done | bytes 262168
  13.5 4.9 %collective-permute-start.9 = (bf16[2,128,512]{2,1,0:T(8,128)(2,1)}, bf16[2,128,512]{2,1,0:T(8,128)(2,1)S(1)}, u32[]{:S(2)}, u32[]{:S(2)}) collective-permute-start(bf16[2,128,512]{2,1,0:T(8,128)(2,1)} %shard_map.62), channel_id=1, source_target_pairs={{0,131},{1,96},{4,135},{5,100},{8,139},{9,104},{12,143},{13,108},{... | collective-permute-start | bytes 786440 | tf_op jit(solution)/shard_map/ppermute | solution.py:26
  18.4 0.7 %copy-done.2 = bf16[2,128,512]{2,1,0:T(8,128)(2,1)} copy-done((bf16[2,128,512]{2,1,0:T(8,128)(2,1)}, bf16[2,128,512]{2,1,0:T(8,128)(2,1)S(1)}, u32[]{:S(2)}) %copy-start.2) | copy-done | bytes 262168
  19.1 1.8 %collective-permute-start.6 = (bf16[2,128,512]{2,1,0:T(8,128)(2,1)}, bf16[2,128,512]{2,1,0:T(8,128)(2,1)S(1)}, u32[]{:S(2)}, u32[]{:S(2)}) collective-permute-start(bf16[2,128,512]{2,1,0:T(8,128)(2,1)} %shard_map.61), channel_id=1, source_target_pairs={{0,1},{1,0},{4,5},{5,4},{8,9},{9,8},{12,13},{13,12},{16,17},{17,16... | collective-permute-start | bytes 786440 | tf_op jit(solution)/shard_map/ppermute | solution.py:26
  21.4 1.5 %collective-permute-start.1 = (bf16[256,512]{1,0:T(8,128)(2,1)S(1)}, bf16[256,512]{1,0:T(8,128)(2,1)S(1)}, u32[]{:S(2)}, u32[]{:S(2)}) collective-permute-start(bf16[256,512]{1,0:T(8,128)(2,1)S(1)} %get-tuple-element.25), channel_id=1, source_target_pairs={{0,130},{1,97},{4,134},{5,101},{8,138},{9,105},{12,142},{13,109},{... | collective-permute-start | bytes 786440 | tf_op jit(solution)/shard_map/ppermute | solution.py:26
  23.0 1.9 %collective-permute-start.3 = (bf16[256,512]{1,0:T(8,128)(2,1)S(1)}, bf16[256,512]{1,0:T(8,128)(2,1)S(1)}, u32[]{:S(2)}, u32[]{:S(2)}) collective-permute-start(bf16[256,512]{1,0:T(8,128)(2,1)S(1)} %get-tuple-element.26), channel_id=1, source_target_pairs={{1,33},{5,37},{9,41},{13,45},{17,49},{21,53},{25,57},{29,61},{129,... | collective-permute-start | bytes 786440 | tf_op jit(solution)/shard_map/ppermute | solution.py:26
  24.9 2.5 %collective-permute-start.2 = (bf16[256,512]{1,0:T(8,128)(2,1)S(1)}, bf16[256,512]{1,0:T(8,128)(2,1)S(1)}, u32[]{:S(2)}, u32[]{:S(2)}) collective-permute-start(bf16[256,512]{1,0:T(8,128)(2,1)S(1)} %get-tuple-element.26), channel_id=1, source_target_pairs={{0,128},{1,65},{4,132},{5,69},{8,136},{9,73},{12,140},{13,77},{16,... | collective-permute-start | bytes 786440 | tf_op jit(solution)/shard_map/ppermute | solution.py:26
  27.4 0.8 %shard_map.63 = (f32[128,512]{1,0:T(8,128)S(1)}, bf16[128,512]{1,0:T(8,128)(2,1)S(1)}, bf16[128,512]{1,0:T(8,128)(2,1)S(1)}, bf16[128,512]{1,0:T(8,128)(2,1)S(1)}) custom-call(bf16[2,128,512]{2,1,0:T(8,128)(2,1)S(1)} %copy-done.5, bf16[2,128,512]{2,1,0:T(8,128)(2,1)S(1)} %copy-done.3, bf16[2,128,512]{2,1,0:T(8,128)(2,1)S(1)} %copy-done.1, ...), custom_call_target="tpu_custom_call" | custom-call | bytes 2097152 | tf_op jit(solution)/shard_map/pallas_call | solution.py:62
  28.2 0.9 %collective-permute-start.13 = (bf16[128,512]{1,0:T(8,128)(2,1)S(1)}, bf16[128,512]{1,0:T(8,128)(2,1)S(1)}, u32[]{:S(2)}, u32[]{:S(2)}) collective-permute-start(bf16[128,512]{1,0:T(8,128)(2,1)S(1)} %get-tuple-element.40), channel_id=1, source_target_pairs={{0,128},{1,33},{4,132},{5,37},{8,136},{9,41},{12,140},{13,45},{16,... | collective-permute-start | bytes 393224 | tf_op jit(solution)/shard_map/ppermute | solution.py:26
  29.1 1.5 %collective-permute-start.14 = (bf16[128,512]{1,0:T(8,128)(2,1)S(1)}, bf16[128,512]{1,0:T(8,128)(2,1)S(1)}, u32[]{:S(2)}, u32[]{:S(2)}) collective-permute-start(bf16[128,512]{1,0:T(8,128)(2,1)S(1)} %get-tuple-element.41), channel_id=1, source_target_pairs={{0,2},{1,65},{4,6},{5,69},{8,10},{9,73},{12,14},{13,77},{16,18},{1... | collective-permute-start | bytes 393224 | tf_op jit(solution)/shard_map/ppermute | solution.py:26
  30.6 1.0 %collective-permute-start.15 = (bf16[128,512]{1,0:T(8,128)(2,1)S(1)}, bf16[128,512]{1,0:T(8,128)(2,1)S(1)}, u32[]{:S(2)}, u32[]{:S(2)}) collective-permute-start(bf16[128,512]{1,0:T(8,128)(2,1)S(1)} %get-tuple-element.42), channel_id=1, source_target_pairs={{0,130},{1,97},{4,134},{5,101},{8,138},{9,105},{12,142},{13,109},{... | collective-permute-start | bytes 393224 | tf_op jit(solution)/shard_map/ppermute | solution.py:26
  31.6 2.8 %collective-permute-done.3.refs_3_ = bf16[256,512]{1,0:T(8,128)(2,1)S(1)} collective-permute-done((bf16[256,512]{1,0:T(8,128)(2,1)S(1)}, bf16[256,512]{1,0:T(8,128)(2,1)S(1)}, u32[]{:S(2)}, u32[]{:S(2)}) %collective-permute-start.3) | collective-permute-done | bytes 262176 | tf_op jit(solution)/shard_map/ppermute | solution.py:26
  34.4 0.8 %shard_map.64 = (bf16[128,1024]{1,0:T(8,128)(2,1)S(1)}, bf16[128,1024]{1,0:T(8,128)(2,1)S(1)}, bf16[128,1024]{1,0:T(8,128)(2,1)S(1)}, bf16[128,1024]{1,0:T(8,128)(2,1)S(1)}) custom-call(bf16[512,512]{1,0:T(8,128)(2,1)S(1)} %get-tuple-element.24.refs_0_, bf16[256,512]{1,0:T(8,128)(2,1)S(1)} %collective-permute-done.1.refs_1_, ...), custom_call_target="tpu_custom_call" | custom-call | bytes 2359296 | tf_op jit(solution)/shard_map/pallas_call | solution.py:62
  35.2 1.5 %collective-permute-start.10 = (bf16[128,1024]{1,0:T(8,128)(2,1)S(1)}, bf16[128,1024]{1,0:T(8,128)(2,1)S(1)}, u32[]{:S(2)}, u32[]{:S(2)}) collective-permute-start(bf16[128,1024]{1,0:T(8,128)(2,1)S(1)} %get-tuple-element.36), channel_id=1, source_target_pairs={{0,96},{1,131},{4,100},{5,135},{8,104},{9,139},{12,108},{13,143},{... | collective-permute-start | bytes 786440 | tf_op jit(solution)/shard_map/ppermute | solution.py:26
  36.7 1.2 %collective-permute-start.11 = (bf16[128,1024]{1,0:T(8,128)(2,1)S(1)}, bf16[128,1024]{1,0:T(8,128)(2,1)S(1)}, u32[]{:S(2)}, u32[]{:S(2)}) collective-permute-start(bf16[128,1024]{1,0:T(8,128)(2,1)S(1)} %get-tuple-element.37), channel_id=1, source_target_pairs={{0,64},{1,3},{4,68},{5,7},{8,72},{9,11},{12,76},{13,15},{16,80},{1... | collective-permute-start | bytes 786440 | tf_op jit(solution)/shard_map/ppermute | solution.py:26
  38.1 0.7 %shard_map.66 = bf16[128,512]{1,0:T(8,128)(2,1)} custom-call(f32[128,512]{1,0:T(8,128)S(1)} %get-tuple-element.34.refs_8_.refs_0_, bf16[128,512]{1,0:T(8,128)(2,1)S(1)} %collective-permute-done.13.refs_1_, bf16[128,512]{1,0:T(8,128)(2,1)S(1)} %collective-permute-done.14.refs_2_, bf16[128,512]{1,0:T(8,128)(2,1)S(1)} %collective-permute-done.15.refs_3_, ...), custom_call_target="tpu_custom_call" | custom-call | bytes 655360 | tf_op jit(solution)/shard_map/pallas_call | solution.py:62
  38.8 8.2 %all-to-all-start = ((bf16[8,16,512]{2,1,0:T(8,128)(2,1)}), bf16[8,16,512]{2,1,0:T(8,128)(2,1)S(1)}, u32[]{:S(2)}, u32[]{:S(2)}) async-start(bf16[8,16,512]{2,1,0:T(8,128)(2,1)} %bitcast), calls=%async_computation | async-start | bytes 262144 | tf_op jit(solution)/shard_map/all_to_all | solution.py:287
  47.0 1.1 %shard_map.65 = (bf16[128,4096]{1,0:T(8,128)(2,1)}, f32[8,128]{1,0:T(8,128)S(1)}) custom-call(bf16[128,1024]{1,0:T(8,128)(2,1)S(1)} %get-tuple-element.35.refs_0_.refs_4_, bf16[128,1024]{1,0:T(8,128)(2,1)S(1)} %collective-permute-done.10.refs_1_, bf16[128,1024]{1,0:T(8,128)(2,1)S(1)} %collective-permute-done.11.refs_2_, ...), custom_call_target="tpu_custom_call" | custom-call | bytes 1048576 | tf_op jit(solution)/shard_map/pallas_call | solution.py:62
  48.1 7.4 %all-to-all-done.refs_0_ = bf16[8,16,512]{2,1,0:T(8,128)(2,1)S(1)} async-done(((bf16[8,16,512]{2,1,0:T(8,128)(2,1)}), bf16[8,16,512]{2,1,0:T(8,128)(2,1)S(1)}, u32[]{:S(2)}, u32[]{:S(2)}) %all-to-all-start) | async-done | bytes 131104 | tf_op jit(solution)/shard_map/all_to_all | solution.py:287
  55.5 0.6 %shard_map.67 = f32[16,512]{1,0:T(8,128)} custom-call(bf16[8,16,512]{2,1,0:T(8,128)(2,1)S(1)} %all-to-all-done.refs_0_, f32[8,128]{1,0:T(8,128)S(1)} %get-tuple-element.43.refs_1_), custom_call_target="tpu_custom_call" | custom-call | bytes 131072 | tf_op jit(solution)/shard_map/pallas_call | solution.py:62
  (35 shorter events, 1.4 us)
Async XLA Ops:
  4.1 8.7 %collective-permute-start = (bf16[2,128,512]{2,1,0:T(8,128)(2,1)}, bf16[2,128,512]{2,1,0:T(8,128)(2,1)S(1)}, u32[]{:S(2)}, u32[]{:S(2)}) collective-permute-start(bf16[2,128,512]{2,1,0:T(8,128)(2,1)} %get-tuple-element.23), channel_id=1, source_target_pairs={{0,64},{1,3},{4,68},{5,7},{8,72},{9,11},{12,76},{13,15},{16,80},{1... | collective-permute-start | bytes 786440 | tf_op jit(solution)/shard_map/ppermute | solution.py:26
  7.9 10.5 %collective-permute-start.4 = (bf16[2,128,512]{2,1,0:T(8,128)(2,1)}, bf16[2,128,512]{2,1,0:T(8,128)(2,1)S(1)}, u32[]{:S(2)}, u32[]{:S(2)}) collective-permute-start(bf16[2,128,512]{2,1,0:T(8,128)(2,1)} %get-tuple-element.28), channel_id=1, source_target_pairs={{0,32},{1,129},{4,36},{5,133},{8,40},{9,137},{12,44},{13,141},{16,... | collective-permute-start | bytes 786440 | tf_op jit(solution)/shard_map/ppermute | solution.py:26
  8.3 13.1 %collective-permute-start.5 = (bf16[2,128,512]{2,1,0:T(8,128)(2,1)}, bf16[2,128,512]{2,1,0:T(8,128)(2,1)S(1)}, u32[]{:S(2)}, u32[]{:S(2)}) collective-permute-start(bf16[2,128,512]{2,1,0:T(8,128)(2,1)} %get-tuple-element.29), channel_id=1, source_target_pairs={{0,96},{1,131},{4,100},{5,135},{8,104},{9,139},{12,108},{13,143},{... | collective-permute-start | bytes 786440 | tf_op jit(solution)/shard_map/ppermute | solution.py:26
  10.6 12.4 %collective-permute-start.7 = (bf16[2,128,512]{2,1,0:T(8,128)(2,1)}, bf16[2,128,512]{2,1,0:T(8,128)(2,1)S(1)}, u32[]{:S(2)}, u32[]{:S(2)}) collective-permute-start(bf16[2,128,512]{2,1,0:T(8,128)(2,1)} %get-tuple-element.31), channel_id=1, source_target_pairs={{0,129},{1,32},{4,133},{5,36},{8,137},{9,40},{12,141},{13,44},{16,... | collective-permute-start | bytes 786440 | tf_op jit(solution)/shard_map/ppermute | solution.py:26
  10.9 14.0 %collective-permute-start.8 = (bf16[2,128,512]{2,1,0:T(8,128)(2,1)}, bf16[2,128,512]{2,1,0:T(8,128)(2,1)S(1)}, u32[]{:S(2)}, u32[]{:S(2)}) collective-permute-start(bf16[2,128,512]{2,1,0:T(8,128)(2,1)} %get-tuple-element.32), channel_id=1, source_target_pairs={{0,3},{1,64},{4,7},{5,68},{8,11},{9,72},{12,15},{13,76},{16,19},{1... | collective-permute-start | bytes 786440 | tf_op jit(solution)/shard_map/ppermute | solution.py:26
  12.8 0.7 %copy-start = (bf16[2,128,512]{2,1,0:T(8,128)(2,1)}, bf16[2,128,512]{2,1,0:T(8,128)(2,1)S(1)}, u32[]{:S(2)}) copy-start(bf16[2,128,512]{2,1,0:T(8,128)(2,1)S(1)} %collective-permute-done.refs_2_.refs_1_.refs_6_) | copy-start | bytes 786436
  13.5 7.6 %copy-start.4 = (s32[512,512]{1,0:T(8,128)S(1)}, s32[512,512]{1,0:T(8,128)}, u32[]{:S(2)}) copy-start(s32[512,512]{1,0:T(8,128)} %refs_0_.3) | copy-start | bytes 3145732
  13.5 13.9 %collective-permute-start.9 = (bf16[2,128,512]{2,1,0:T(8,128)(2,1)}, bf16[2,128,512]{2,1,0:T(8,128)(2,1)S(1)}, u32[]{:S(2)}, u32[]{:S(2)}) collective-permute-start(bf16[2,128,512]{2,1,0:T(8,128)(2,1)} %shard_map.62), channel_id=1, source_target_pairs={{0,131},{1,96},{4,135},{5,100},{8,139},{9,104},{12,143},{13,108},{... | collective-permute-start | bytes 786440 | tf_op jit(solution)/shard_map/ppermute | solution.py:26
  18.4 0.7 %copy-start.2 = (bf16[2,128,512]{2,1,0:T(8,128)(2,1)}, bf16[2,128,512]{2,1,0:T(8,128)(2,1)S(1)}, u32[]{:S(2)}) copy-start(bf16[2,128,512]{2,1,0:T(8,128)(2,1)S(1)} %collective-permute-done.4.refs_1_.refs_5_) | copy-start | bytes 786436
  19.1 1.8 %copy-start.6 = (f32[256]{0:T(256)S(1)}, f32[256]{0:T(256)}, u32[]{:S(2)}) copy-start(f32[256]{0:T(256)} %param.7) | copy-start | bytes 3076
  19.1 2.0 %copy-start.1 = (bf16[2,128,512]{2,1,0:T(8,128)(2,1)S(1)}, bf16[2,128,512]{2,1,0:T(8,128)(2,1)}, u32[]{:S(2)}) copy-start(bf16[2,128,512]{2,1,0:T(8,128)(2,1)} %copy-done) | copy-start | bytes 786436
  19.1 8.3 %collective-permute-start.6 = (bf16[2,128,512]{2,1,0:T(8,128)(2,1)}, bf16[2,128,512]{2,1,0:T(8,128)(2,1)S(1)}, u32[]{:S(2)}, u32[]{:S(2)}) collective-permute-start(bf16[2,128,512]{2,1,0:T(8,128)(2,1)} %shard_map.61), channel_id=1, source_target_pairs={{0,1},{1,0},{4,5},{5,4},{8,9},{9,8},{12,13},{13,12},{16,17},{17,16... | collective-permute-start | bytes 786440 | tf_op jit(solution)/shard_map/ppermute | solution.py:26
  21.1 6.3 %copy-start.3 = (bf16[2,128,512]{2,1,0:T(8,128)(2,1)S(1)}, bf16[2,128,512]{2,1,0:T(8,128)(2,1)}, u32[]{:S(2)}) copy-start(bf16[2,128,512]{2,1,0:T(8,128)(2,1)} %copy-done.2) | copy-start | bytes 786436
  21.1 6.3 %copy-start.5 = (bf16[2,128,512]{2,1,0:T(8,128)(2,1)S(1)}, bf16[2,128,512]{2,1,0:T(8,128)(2,1)}, u32[]{:S(2)}) copy-start(bf16[2,128,512]{2,1,0:T(8,128)(2,1)} %get-tuple-element.27.refs_0_.refs_4_) | copy-start | bytes 786436
  21.4 9.2 %collective-permute-start.1 = (bf16[256,512]{1,0:T(8,128)(2,1)S(1)}, bf16[256,512]{1,0:T(8,128)(2,1)S(1)}, u32[]{:S(2)}, u32[]{:S(2)}) collective-permute-start(bf16[256,512]{1,0:T(8,128)(2,1)S(1)} %get-tuple-element.25), channel_id=1, source_target_pairs={{0,130},{1,97},{4,134},{5,101},{8,138},{9,105},{12,142},{13,109},{... | collective-permute-start | bytes 786440 | tf_op jit(solution)/shard_map/ppermute | solution.py:26
  23.0 11.4 %collective-permute-start.3 = (bf16[256,512]{1,0:T(8,128)(2,1)S(1)}, bf16[256,512]{1,0:T(8,128)(2,1)S(1)}, u32[]{:S(2)}, u32[]{:S(2)}) collective-permute-start(bf16[256,512]{1,0:T(8,128)(2,1)S(1)} %get-tuple-element.26), channel_id=1, source_target_pairs={{1,33},{5,37},{9,41},{13,45},{17,49},{21,53},{25,57},{29,61},{129,... | collective-permute-start | bytes 786440 | tf_op jit(solution)/shard_map/ppermute | solution.py:26
  24.9 9.5 %collective-permute-start.2 = (bf16[256,512]{1,0:T(8,128)(2,1)S(1)}, bf16[256,512]{1,0:T(8,128)(2,1)S(1)}, u32[]{:S(2)}, u32[]{:S(2)}) collective-permute-start(bf16[256,512]{1,0:T(8,128)(2,1)S(1)} %get-tuple-element.26), channel_id=1, source_target_pairs={{0,128},{1,65},{4,132},{5,69},{8,136},{9,73},{12,140},{13,77},{16,... | collective-permute-start | bytes 786440 | tf_op jit(solution)/shard_map/ppermute | solution.py:26
  28.2 9.7 %collective-permute-start.13 = (bf16[128,512]{1,0:T(8,128)(2,1)S(1)}, bf16[128,512]{1,0:T(8,128)(2,1)S(1)}, u32[]{:S(2)}, u32[]{:S(2)}) collective-permute-start(bf16[128,512]{1,0:T(8,128)(2,1)S(1)} %get-tuple-element.40), channel_id=1, source_target_pairs={{0,128},{1,33},{4,132},{5,37},{8,136},{9,41},{12,140},{13,45},{16,... | collective-permute-start | bytes 393224 | tf_op jit(solution)/shard_map/ppermute | solution.py:26
  29.1 9.0 %collective-permute-start.14 = (bf16[128,512]{1,0:T(8,128)(2,1)S(1)}, bf16[128,512]{1,0:T(8,128)(2,1)S(1)}, u32[]{:S(2)}, u32[]{:S(2)}) collective-permute-start(bf16[128,512]{1,0:T(8,128)(2,1)S(1)} %get-tuple-element.41), channel_id=1, source_target_pairs={{0,2},{1,65},{4,6},{5,69},{8,10},{9,73},{12,14},{13,77},{16,18},{1... | collective-permute-start | bytes 393224 | tf_op jit(solution)/shard_map/ppermute | solution.py:26
  30.6 7.5 %collective-permute-start.15 = (bf16[128,512]{1,0:T(8,128)(2,1)S(1)}, bf16[128,512]{1,0:T(8,128)(2,1)S(1)}, u32[]{:S(2)}, u32[]{:S(2)}) collective-permute-start(bf16[128,512]{1,0:T(8,128)(2,1)S(1)} %get-tuple-element.42), channel_id=1, source_target_pairs={{0,130},{1,97},{4,134},{5,101},{8,138},{9,105},{12,142},{13,109},{... | collective-permute-start | bytes 393224 | tf_op jit(solution)/shard_map/ppermute | solution.py:26
  35.2 11.8 %collective-permute-start.10 = (bf16[128,1024]{1,0:T(8,128)(2,1)S(1)}, bf16[128,1024]{1,0:T(8,128)(2,1)S(1)}, u32[]{:S(2)}, u32[]{:S(2)}) collective-permute-start(bf16[128,1024]{1,0:T(8,128)(2,1)S(1)} %get-tuple-element.36), channel_id=1, source_target_pairs={{0,96},{1,131},{4,100},{5,135},{8,104},{9,139},{12,108},{13,143},{... | collective-permute-start | bytes 786440 | tf_op jit(solution)/shard_map/ppermute | solution.py:26
  36.7 10.3 %collective-permute-start.11 = (bf16[128,1024]{1,0:T(8,128)(2,1)S(1)}, bf16[128,1024]{1,0:T(8,128)(2,1)S(1)}, u32[]{:S(2)}, u32[]{:S(2)}) collective-permute-start(bf16[128,1024]{1,0:T(8,128)(2,1)S(1)} %get-tuple-element.37), channel_id=1, source_target_pairs={{0,64},{1,3},{4,68},{5,7},{8,72},{9,11},{12,76},{13,15},{16,80},{1... | collective-permute-start | bytes 786440 | tf_op jit(solution)/shard_map/ppermute | solution.py:26
  38.0 9.0 %collective-permute-start.12 = (bf16[128,1024]{1,0:T(8,128)(2,1)S(1)}, bf16[128,1024]{1,0:T(8,128)(2,1)S(1)}, u32[]{:S(2)}, u32[]{:S(2)}) collective-permute-start(bf16[128,1024]{1,0:T(8,128)(2,1)S(1)} %get-tuple-element.38), channel_id=1, source_target_pairs={{0,32},{1,129},{4,36},{5,133},{8,40},{9,137},{12,44},{13,141},{16,... | collective-permute-start | bytes 786440 | tf_op jit(solution)/shard_map/ppermute | solution.py:26
  38.8 16.7 %all-to-all-start = ((bf16[8,16,512]{2,1,0:T(8,128)(2,1)}), bf16[8,16,512]{2,1,0:T(8,128)(2,1)S(1)}, u32[]{:S(2)}, u32[]{:S(2)}) async-start(bf16[8,16,512]{2,1,0:T(8,128)(2,1)} %bitcast), calls=%async_computation | async-start | bytes 262144 | tf_op jit(solution)/shard_map/all_to_all | solution.py:287

commit v7 on v6

--- a/solution.py
+++ b/solution.py
@@ -110,19 +110,24 @@
     order = (row == source).astype(F32).astype(BF16)
     part = rows // (NC * NYH)
     tokens = acts_ref.shape[0]
-    for yl in range(NYL):
-        for b in range(yl * NX, (yl + 1) * NX):
-            copies[b].wait()
-        block = acts_here[yl * NX : (yl + 1) * NX].reshape(NX * tokens, rows)
-        block = jnp.dot(block, order, preferred_element_type=F32).astype(BF16)
-        block = block.reshape(NX, tokens, rows)
+    for copy in copies[:blocks]:
+        copy.wait()
+    block = acts_here[...].reshape(blocks * tokens, rows)
+    for core in range(NC):
         for yh in range(NYH):
-            yy = NYL * yh + yl
-            at = yh * part
-            sorted_here[0, :, :, yy * part : (yy + 1) * part] = block[:, :, at : at + part]
-            at = (NYH + yh) * part
-            for chip in range(NX):
-                sorted_here[1, yy, :, chip * part : (chip + 1) * part] = block[chip, :, at : at + part]
+            at = (core * NYH + yh) * part
+            if yh == 0:
+                wide = jnp.dot(
+                    block, order[:, at : at + NYH * part], preferred_element_type=F32
+                ).astype(BF16).reshape(NYL, NX, tokens, NYH * part)
+            for yl in range(NYL):
+                yy = NYL * yh + yl
+                got = wide[yl, :, :, yh * part : (yh + 1) * part]
+                if core == 0:
+                    sorted_here[0, :, :, yy * part : (yy + 1) * part] = got
+                else:
+                    for chip in range(NX):
+                        sorted_here[1, yy, :, chip * part : (chip + 1) * part] = got[chip]
     copies[blocks].wait()
     cot = own[0][1]
     for s in range(NX):

time: 56.4 us -> 56.4 us (level)
  no operation moved by 1% of the time
where the time goes in v7:
time: 56.4 us; the launch traced here: 56.2 us
  starting transfers between devices  35.7 us (63%)
  waiting for transfers between devices  10.3 us (18%)
  Pallas kernels  7.79 us (14%)
  local copies, waits for them, and re-layouts  1.64 us (3%)
  between operations  0.78 us (1%)
    ppermute x16, starting transfers between devices, moved(): return lax.ppermute(value, AXES, moves)  27.6 us
    all_to_all x1, starting transfers between devices, per_device(): ring = lax.all_to_all(column, 'z', split_axis=0, concat_axis=0, tiled=True)  8.19 us
    pallas_call x7, Pallas kernels, call(): pl.pallas_call(body, out_shape=outs, in_specs=[pl.BlockSpec(memory_space=...  7.78 us
    all_to_all x1, waiting for transfers between devices, per_device(): ring = lax.all_to_all(column, 'z', split_axis=0, concat_axis=0, tiled=True)  7.42 us
    ppermute x16, waiting for transfers between devices, moved(): return lax.ppermute(value, AXES, moves)  2.84 us
    unnamed x14, local copies, waits for them, and re-layouts  1.44 us
  transfers between devices with their start and end apart: 17, of which 2 were waited for; matrix products, arithmetic and copies ran while one was open for 0% of the time, Pallas kernels for 7%

profile of v7, /device:TPU:1, one launch (start us, length us, event | category | flops | bytes accessed | tf_op | source)
XLA Modules:
  0.0 56.2 jit_solution(7361515385720797933)
XLA Ops:
  0.6 3.4 %shard_map.59 = (bf16[2,128,512]{2,1,0:T(8,128)(2,1)}, bf16[2,128,512]{2,1,0:T(8,128)(2,1)}, bf16[2,128,512]{2,1,0:T(8,128)(2,1)}, bf16[2,128,512]{2,1,0:T(8,128...) custom-call(bf16[128,4096]{1,0:T(8,128)(2,1)} %refs_0_.2, ...), custom_call_target="tpu_custom_call" | custom-call | bytes 1179648 | tf_op jit(solution)/shard_map/pallas_call | solution.py:62
  4.1 3.8 %collective-permute-start = (bf16[2,128,512]{2,1,0:T(8,128)(2,1)}, bf16[2,128,512]{2,1,0:T(8,128)(2,1)S(1)}, u32[]{:S(2)}, u32[]{:S(2)}) collective-permute-start(bf16[2,128,512]{2,1,0:T(8,128)(2,1)} %get-tuple-element.23), channel_id=1, source_target_pairs={{0,64},{1,3},{4,68},{5,7},{8,72},{9,11},{12,76},{13,15},{16,80},{1... | collective-permute-start | bytes 786440 | tf_op jit(solution)/shard_map/ppermute | solution.py:26
  8.3 2.3 %collective-permute-start.5 = (bf16[2,128,512]{2,1,0:T(8,128)(2,1)}, bf16[2,128,512]{2,1,0:T(8,128)(2,1)S(1)}, u32[]{:S(2)}, u32[]{:S(2)}) collective-permute-start(bf16[2,128,512]{2,1,0:T(8,128)(2,1)} %get-tuple-element.29), channel_id=1, source_target_pairs={{0,96},{1,131},{4,100},{5,135},{8,104},{9,139},{12,108},{13,143},{... | collective-permute-start | bytes 786440 | tf_op jit(solution)/shard_map/ppermute | solution.py:26
  10.9 1.9 %collective-permute-start.8 = (bf16[2,128,512]{2,1,0:T(8,128)(2,1)}, bf16[2,128,512]{2,1,0:T(8,128)(2,1)S(1)}, u32[]{:S(2)}, u32[]{:S(2)}) collective-permute-start(bf16[2,128,512]{2,1,0:T(8,128)(2,1)} %get-tuple-element.32), channel_id=1, source_target_pairs={{0,3},{1,64},{4,7},{5,68},{8,11},{9,72},{12,15},{13,76},{16,19},{1... | collective-permute-start | bytes 786440 | tf_op jit(solution)/shard_map/ppermute | solution.py:26
  12.8 0.7 %copy-done = bf16[2,128,512]{2,1,0:T(8,128)(2,1)} copy-done((bf16[2,128,512]{2,1,0:T(8,128)(2,1)}, bf16[2,128,512]{2,1,0:T(8,128)(2,1)S(1)}, u32[]{:S(2)}) %copy-start) | copy-done | bytes 262168
  13.5 4.9 %collective-permute-start.9 = (bf16[2,128,512]{2,1,0:T(8,128)(2,1)}, bf16[2,128,512]{2,1,0:T(8,128)(2,1)S(1)}, u32[]{:S(2)}, u32[]{:S(2)}) collective-permute-start(bf16[2,128,512]{2,1,0:T(8,128)(2,1)} %shard_map.62), channel_id=1, source_target_pairs={{0,131},{1,96},{4,135},{5,100},{8,139},{9,104},{12,143},{13,108},{... | collective-permute-start | bytes 786440 | tf_op jit(solution)/shard_map/ppermute | solution.py:26
  18.4 0.7 %copy-done.2 = bf16[2,128,512]{2,1,0:T(8,128)(2,1)} copy-done((bf16[2,128,512]{2,1,0:T(8,128)(2,1)}, bf16[2,128,512]{2,1,0:T(8,128)(2,1)S(1)}, u32[]{:S(2)}) %copy-start.2) | copy-done | bytes 262168
  19.1 1.8 %collective-permute-start.6 = (bf16[2,128,512]{2,1,0:T(8,128)(2,1)}, bf16[2,128,512]{2,1,0:T(8,128)(2,1)S(1)}, u32[]{:S(2)}, u32[]{:S(2)}) collective-permute-start(bf16[2,128,512]{2,1,0:T(8,128)(2,1)} %shard_map.61), channel_id=1, source_target_pairs={{0,1},{1,0},{4,5},{5,4},{8,9},{9,8},{12,13},{13,12},{16,17},{17,16... | collective-permute-start | bytes 786440 | tf_op jit(solution)/shard_map/ppermute | solution.py:26
  21.5 1.5 %collective-permute-start.1 = (bf16[256,512]{1,0:T(8,128)(2,1)S(1)}, bf16[256,512]{1,0:T(8,128)(2,1)S(1)}, u32[]{:S(2)}, u32[]{:S(2)}) collective-permute-start(bf16[256,512]{1,0:T(8,128)(2,1)S(1)} %get-tuple-element.25), channel_id=1, source_target_pairs={{0,130},{1,97},{4,134},{5,101},{8,138},{9,105},{12,142},{13,109},{... | collective-permute-start | bytes 786440 | tf_op jit(solution)/shard_map/ppermute | solution.py:26
  23.0 1.9 %collective-permute-start.3 = (bf16[256,512]{1,0:T(8,128)(2,1)S(1)}, bf16[256,512]{1,0:T(8,128)(2,1)S(1)}, u32[]{:S(2)}, u32[]{:S(2)}) collective-permute-start(bf16[256,512]{1,0:T(8,128)(2,1)S(1)} %get-tuple-element.26), channel_id=1, source_target_pairs={{1,33},{5,37},{9,41},{13,45},{17,49},{21,53},{25,57},{29,61},{129,... | collective-permute-start | bytes 786440 | tf_op jit(solution)/shard_map/ppermute | solution.py:26
  24.9 2.5 %collective-permute-start.2 = (bf16[256,512]{1,0:T(8,128)(2,1)S(1)}, bf16[256,512]{1,0:T(8,128)(2,1)S(1)}, u32[]{:S(2)}, u32[]{:S(2)}) collective-permute-start(bf16[256,512]{1,0:T(8,128)(2,1)S(1)} %get-tuple-element.26), channel_id=1, source_target_pairs={{0,128},{1,65},{4,132},{5,69},{8,136},{9,73},{12,140},{13,77},{16,... | collective-permute-start | bytes 786440 | tf_op jit(solution)/shard_map/ppermute | solution.py:26
  27.4 0.8 %shard_map.63 = (f32[128,512]{1,0:T(8,128)S(1)}, bf16[128,512]{1,0:T(8,128)(2,1)S(1)}, bf16[128,512]{1,0:T(8,128)(2,1)S(1)}, bf16[128,512]{1,0:T(8,128)(2,1)S(1)}) custom-call(bf16[2,128,512]{2,1,0:T(8,128)(2,1)S(1)} %copy-done.5, bf16[2,128,512]{2,1,0:T(8,128)(2,1)S(1)} %copy-done.3, bf16[2,128,512]{2,1,0:T(8,128)(2,1)S(1)} %copy-done.1, ...), custom_call_target="tpu_custom_call" | custom-call | bytes 2097152 | tf_op jit(solution)/shard_map/pallas_call | solution.py:62
  28.2 0.9 %collective-permute-start.13 = (bf16[128,512]{1,0:T(8,128)(2,1)S(1)}, bf16[128,512]{1,0:T(8,128)(2,1)S(1)}, u32[]{:S(2)}, u32[]{:S(2)}) collective-permute-start(bf16[128,512]{1,0:T(8,128)(2,1)S(1)} %get-tuple-element.40), channel_id=1, source_target_pairs={{0,128},{1,33},{4,132},{5,37},{8,136},{9,41},{12,140},{13,45},{16,... | collective-permute-start | bytes 393224 | tf_op jit(solution)/shard_map/ppermute | solution.py:26
  29.1 1.5 %collective-permute-start.14 = (bf16[128,512]{1,0:T(8,128)(2,1)S(1)}, bf16[128,512]{1,0:T(8,128)(2,1)S(1)}, u32[]{:S(2)}, u32[]{:S(2)}) collective-permute-start(bf16[128,512]{1,0:T(8,128)(2,1)S(1)} %get-tuple-element.41), channel_id=1, source_target_pairs={{0,2},{1,65},{4,6},{5,69},{8,10},{9,73},{12,14},{13,77},{16,18},{1... | collective-permute-start | bytes 393224 | tf_op jit(solution)/shard_map/ppermute | solution.py:26
  30.6 1.0 %collective-permute-start.15 = (bf16[128,512]{1,0:T(8,128)(2,1)S(1)}, bf16[128,512]{1,0:T(8,128)(2,1)S(1)}, u32[]{:S(2)}, u32[]{:S(2)}) collective-permute-start(bf16[128,512]{1,0:T(8,128)(2,1)S(1)} %get-tuple-element.42), channel_id=1, source_target_pairs={{0,130},{1,97},{4,134},{5,101},{8,138},{9,105},{12,142},{13,109},{... | collective-permute-start | bytes 393224 | tf_op jit(solution)/shard_map/ppermute | solution.py:26
  31.6 2.8 %collective-permute-done.3.refs_3_ = bf16[256,512]{1,0:T(8,128)(2,1)S(1)} collective-permute-done((bf16[256,512]{1,0:T(8,128)(2,1)S(1)}, bf16[256,512]{1,0:T(8,128)(2,1)S(1)}, u32[]{:S(2)}, u32[]{:S(2)}) %collective-permute-start.3) | collective-permute-done | bytes 262176 | tf_op jit(solution)/shard_map/ppermute | solution.py:26
  34.4 0.8 %shard_map.64 = (bf16[128,1024]{1,0:T(8,128)(2,1)S(1)}, bf16[128,1024]{1,0:T(8,128)(2,1)S(1)}, bf16[128,1024]{1,0:T(8,128)(2,1)S(1)}, bf16[128,1024]{1,0:T(8,128)(2,1)S(1)}) custom-call(bf16[512,512]{1,0:T(8,128)(2,1)S(1)} %get-tuple-element.24.refs_0_, bf16[256,512]{1,0:T(8,128)(2,1)S(1)} %collective-permute-done.1.refs_1_, ...), custom_call_target="tpu_custom_call" | custom-call | bytes 2359296 | tf_op jit(solution)/shard_map/pallas_call | solution.py:62
  35.2 1.5 %collective-permute-start.10 = (bf16[128,1024]{1,0:T(8,128)(2,1)S(1)}, bf16[128,1024]{1,0:T(8,128)(2,1)S(1)}, u32[]{:S(2)}, u32[]{:S(2)}) collective-permute-start(bf16[128,1024]{1,0:T(8,128)(2,1)S(1)} %get-tuple-element.36), channel_id=1, source_target_pairs={{0,96},{1,131},{4,100},{5,135},{8,104},{9,139},{12,108},{13,143},{... | collective-permute-start | bytes 786440 | tf_op jit(solution)/shard_map/ppermute | solution.py:26
  36.7 1.2 %collective-permute-start.11 = (bf16[128,1024]{1,0:T(8,128)(2,1)S(1)}, bf16[128,1024]{1,0:T(8,128)(2,1)S(1)}, u32[]{:S(2)}, u32[]{:S(2)}) collective-permute-start(bf16[128,1024]{1,0:T(8,128)(2,1)S(1)} %get-tuple-element.37), channel_id=1, source_target_pairs={{0,64},{1,3},{4,68},{5,7},{8,72},{9,11},{12,76},{13,15},{16,80},{1... | collective-permute-start | bytes 786440 | tf_op jit(solution)/shard_map/ppermute | solution.py:26
  38.1 0.7 %shard_map.66 = bf16[128,512]{1,0:T(8,128)(2,1)} custom-call(f32[128,512]{1,0:T(8,128)S(1)} %get-tuple-element.34.refs_8_.refs_0_, bf16[128,512]{1,0:T(8,128)(2,1)S(1)} %collective-permute-done.13.refs_1_, bf16[128,512]{1,0:T(8,128)(2,1)S(1)} %collective-permute-done.14.refs_2_, bf16[128,512]{1,0:T(8,128)(2,1)S(1)} %collective-permute-done.15.refs_3_, ...), custom_call_target="tpu_custom_call" | custom-call | bytes 655360 | tf_op jit(solution)/shard_map/pallas_call | solution.py:62
  38.8 8.2 %all-to-all-start = ((bf16[8,16,512]{2,1,0:T(8,128)(2,1)}), bf16[8,16,512]{2,1,0:T(8,128)(2,1)S(1)}, u32[]{:S(2)}, u32[]{:S(2)}) async-start(bf16[8,16,512]{2,1,0:T(8,128)(2,1)} %bitcast), calls=%async_computation | async-start | bytes 262144 | tf_op jit(solution)/shard_map/all_to_all | solution.py:292
  47.0 1.1 %shard_map.65 = (bf16[128,4096]{1,0:T(8,128)(2,1)}, f32[8,128]{1,0:T(8,128)S(1)}) custom-call(bf16[128,1024]{1,0:T(8,128)(2,1)S(1)} %get-tuple-element.35.refs_0_.refs_4_, bf16[128,1024]{1,0:T(8,128)(2,1)S(1)} %collective-permute-done.10.refs_1_, bf16[128,1024]{1,0:T(8,128)(2,1)S(1)} %collective-permute-done.11.refs_2_, ...), custom_call_target="tpu_custom_call" | custom-call | bytes 1048576 | tf_op jit(solution)/shard_map/pallas_call | solution.py:62
  48.1 7.4 %all-to-all-done.refs_0_ = bf16[8,16,512]{2,1,0:T(8,128)(2,1)S(1)} async-done(((bf16[8,16,512]{2,1,0:T(8,128)(2,1)}), bf16[8,16,512]{2,1,0:T(8,128)(2,1)S(1)}, u32[]{:S(2)}, u32[]{:S(2)}) %all-to-all-start) | async-done | bytes 131104 | tf_op jit(solution)/shard_map/all_to_all | solution.py:292
  55.6 0.6 %shard_map.67 = f32[16,512]{1,0:T(8,128)} custom-call(bf16[8,16,512]{2,1,0:T(8,128)(2,1)S(1)} %all-to-all-done.refs_0_, f32[8,128]{1,0:T(8,128)S(1)} %get-tuple-element.43.refs_1_), custom_call_target="tpu_custom_call" | custom-call | bytes 131072 | tf_op jit(solution)/shard_map/pallas_call | solution.py:62
  (35 shorter events, 1.4 us)
Async XLA Ops:
  4.1 8.7 %collective-permute-start = (bf16[2,128,512]{2,1,0:T(8,128)(2,1)}, bf16[2,128,512]{2,1,0:T(8,128)(2,1)S(1)}, u32[]{:S(2)}, u32[]{:S(2)}) collective-permute-start(bf16[2,128,512]{2,1,0:T(8,128)(2,1)} %get-tuple-element.23), channel_id=1, source_target_pairs={{0,64},{1,3},{4,68},{5,7},{8,72},{9,11},{12,76},{13,15},{16,80},{1... | collective-permute-start | bytes 786440 | tf_op jit(solution)/shard_map/ppermute | solution.py:26
  7.9 10.5 %collective-permute-start.4 = (bf16[2,128,512]{2,1,0:T(8,128)(2,1)}, bf16[2,128,512]{2,1,0:T(8,128)(2,1)S(1)}, u32[]{:S(2)}, u32[]{:S(2)}) collective-permute-start(bf16[2,128,512]{2,1,0:T(8,128)(2,1)} %get-tuple-element.28), channel_id=1, source_target_pairs={{0,32},{1,129},{4,36},{5,133},{8,40},{9,137},{12,44},{13,141},{16,... | collective-permute-start | bytes 786440 | tf_op jit(solution)/shard_map/ppermute | solution.py:26
  8.3 13.1 %collective-permute-start.5 = (bf16[2,128,512]{2,1,0:T(8,128)(2,1)}, bf16[2,128,512]{2,1,0:T(8,128)(2,1)S(1)}, u32[]{:S(2)}, u32[]{:S(2)}) collective-permute-start(bf16[2,128,512]{2,1,0:T(8,128)(2,1)} %get-tuple-element.29), channel_id=1, source_target_pairs={{0,96},{1,131},{4,100},{5,135},{8,104},{9,139},{12,108},{13,143},{... | collective-permute-start | bytes 786440 | tf_op jit(solution)/shard_map/ppermute | solution.py:26
  10.6 12.4 %collective-permute-start.7 = (bf16[2,128,512]{2,1,0:T(8,128)(2,1)}, bf16[2,128,512]{2,1,0:T(8,128)(2,1)S(1)}, u32[]{:S(2)}, u32[]{:S(2)}) collective-permute-start(bf16[2,128,512]{2,1,0:T(8,128)(2,1)} %get-tuple-element.31), channel_id=1, source_target_pairs={{0,129},{1,32},{4,133},{5,36},{8,137},{9,40},{12,141},{13,44},{16,... | collective-permute-start | bytes 786440 | tf_op jit(solution)/shard_map/ppermute | solution.py:26
  10.9 14.0 %collective-permute-start.8 = (bf16[2,128,512]{2,1,0:T(8,128)(2,1)}, bf16[2,128,512]{2,1,0:T(8,128)(2,1)S(1)}, u32[]{:S(2)}, u32[]{:S(2)}) collective-permute-start(bf16[2,128,512]{2,1,0:T(8,128)(2,1)} %get-tuple-element.32), channel_id=1, source_target_pairs={{0,3},{1,64},{4,7},{5,68},{8,11},{9,72},{12,15},{13,76},{16,19},{1... | collective-permute-start | bytes 786440 | tf_op jit(solution)/shard_map/ppermute | solution.py:26
  12.8 0.7 %copy-start = (bf16[2,128,512]{2,1,0:T(8,128)(2,1)}, bf16[2,128,512]{2,1,0:T(8,128)(2,1)S(1)}, u32[]{:S(2)}) copy-start(bf16[2,128,512]{2,1,0:T(8,128)(2,1)S(1)} %collective-permute-done.refs_2_.refs_1_.refs_6_) | copy-start | bytes 786436
  13.5 7.6 %copy-start.4 = (s32[512,512]{1,0:T(8,128)S(1)}, s32[512,512]{1,0:T(8,128)}, u32[]{:S(2)}) copy-start(s32[512,512]{1,0:T(8,128)} %refs_0_.3) | copy-start | bytes 3145732
  13.5 13.9 %collective-permute-start.9 = (bf16[2,128,512]{2,1,0:T(8,128)(2,1)}, bf16[2,128,512]{2,1,0:T(8,128)(2,1)S(1)}, u32[]{:S(2)}, u32[]{:S(2)}) collective-permute-start(bf16[2,128,512]{2,1,0:T(8,128)(2,1)} %shard_map.62), channel_id=1, source_target_pairs={{0,131},{1,96},{4,135},{5,100},{8,139},{9,104},{12,143},{13,108},{... | collective-permute-start | bytes 786440 | tf_op jit(solution)/shard_map/ppermute | solution.py:26
  18.4 0.7 %copy-start.2 = (bf16[2,128,512]{2,1,0:T(8,128)(2,1)}, bf16[2,128,512]{2,1,0:T(8,128)(2,1)S(1)}, u32[]{:S(2)}) copy-start(bf16[2,128,512]{2,1,0:T(8,128)(2,1)S(1)} %collective-permute-done.4.refs_1_.refs_5_) | copy-start | bytes 786436
  19.1 1.8 %copy-start.6 = (f32[256]{0:T(256)S(1)}, f32[256]{0:T(256)}, u32[]{:S(2)}) copy-start(f32[256]{0:T(256)} %param.7) | copy-start | bytes 3076
  19.1 2.0 %copy-start.1 = (bf16[2,128,512]{2,1,0:T(8,128)(2,1)S(1)}, bf16[2,128,512]{2,1,0:T(8,128)(2,1)}, u32[]{:S(2)}) copy-start(bf16[2,128,512]{2,1,0:T(8,128)(2,1)} %copy-done) | copy-start | bytes 786436
  19.1 8.3 %collective-permute-start.6 = (bf16[2,128,512]{2,1,0:T(8,128)(2,1)}, bf16[2,128,512]{2,1,0:T(8,128)(2,1)S(1)}, u32[]{:S(2)}, u32[]{:S(2)}) collective-permute-start(bf16[2,128,512]{2,1,0:T(8,128)(2,1)} %shard_map.61), channel_id=1, source_target_pairs={{0,1},{1,0},{4,5},{5,4},{8,9},{9,8},{12,13},{13,12},{16,17},{17,16... | collective-permute-start | bytes 786440 | tf_op jit(solution)/shard_map/ppermute | solution.py:26
  21.1 6.3 %copy-start.3 = (bf16[2,128,512]{2,1,0:T(8,128)(2,1)S(1)}, bf16[2,128,512]{2,1,0:T(8,128)(2,1)}, u32[]{:S(2)}) copy-start(bf16[2,128,512]{2,1,0:T(8,128)(2,1)} %copy-done.2) | copy-start | bytes 786436
  21.1 6.3 %copy-start.5 = (bf16[2,128,512]{2,1,0:T(8,128)(2,1)S(1)}, bf16[2,128,512]{2,1,0:T(8,128)(2,1)}, u32[]{:S(2)}) copy-start(bf16[2,128,512]{2,1,0:T(8,128)(2,1)} %get-tuple-element.27.refs_0_.refs_4_) | copy-start | bytes 786436
  21.5 9.1 %collective-permute-start.1 = (bf16[256,512]{1,0:T(8,128)(2,1)S(1)}, bf16[256,512]{1,0:T(8,128)(2,1)S(1)}, u32[]{:S(2)}, u32[]{:S(2)}) collective-permute-start(bf16[256,512]{1,0:T(8,128)(2,1)S(1)} %get-tuple-element.25), channel_id=1, source_target_pairs={{0,130},{1,97},{4,134},{5,101},{8,138},{9,105},{12,142},{13,109},{... | collective-permute-start | bytes 786440 | tf_op jit(solution)/shard_map/ppermute | solution.py:26
  23.0 11.4 %collective-permute-start.3 = (bf16[256,512]{1,0:T(8,128)(2,1)S(1)}, bf16[256,512]{1,0:T(8,128)(2,1)S(1)}, u32[]{:S(2)}, u32[]{:S(2)}) collective-permute-start(bf16[256,512]{1,0:T(8,128)(2,1)S(1)} %get-tuple-element.26), channel_id=1, source_target_pairs={{1,33},{5,37},{9,41},{13,45},{17,49},{21,53},{25,57},{29,61},{129,... | collective-permute-start | bytes 786440 | tf_op jit(solution)/shard_map/ppermute | solution.py:26
  24.9 9.5 %collective-permute-start.2 = (bf16[256,512]{1,0:T(8,128)(2,1)S(1)}, bf16[256,512]{1,0:T(8,128)(2,1)S(1)}, u32[]{:S(2)}, u32[]{:S(2)}) collective-permute-start(bf16[256,512]{1,0:T(8,128)(2,1)S(1)} %get-tuple-element.26), channel_id=1, source_target_pairs={{0,128},{1,65},{4,132},{5,69},{8,136},{9,73},{12,140},{13,77},{16,... | collective-permute-start | bytes 786440 | tf_op jit(solution)/shard_map/ppermute | solution.py:26
  28.2 9.8 %collective-permute-start.13 = (bf16[128,512]{1,0:T(8,128)(2,1)S(1)}, bf16[128,512]{1,0:T(8,128)(2,1)S(1)}, u32[]{:S(2)}, u32[]{:S(2)}) collective-permute-start(bf16[128,512]{1,0:T(8,128)(2,1)S(1)} %get-tuple-element.40), channel_id=1, source_target_pairs={{0,128},{1,33},{4,132},{5,37},{8,136},{9,41},{12,140},{13,45},{16,... | collective-permute-start | bytes 393224 | tf_op jit(solution)/shard_map/ppermute | solution.py:26
  29.1 9.0 %collective-permute-start.14 = (bf16[128,512]{1,0:T(8,128)(2,1)S(1)}, bf16[128,512]{1,0:T(8,128)(2,1)S(1)}, u32[]{:S(2)}, u32[]{:S(2)}) collective-permute-start(bf16[128,512]{1,0:T(8,128)(2,1)S(1)} %get-tuple-element.41), channel_id=1, source_target_pairs={{0,2},{1,65},{4,6},{5,69},{8,10},{9,73},{12,14},{13,77},{16,18},{1... | collective-permute-start | bytes 393224 | tf_op jit(solution)/shard_map/ppermute | solution.py:26
  30.6 7.5 %collective-permute-start.15 = (bf16[128,512]{1,0:T(8,128)(2,1)S(1)}, bf16[128,512]{1,0:T(8,128)(2,1)S(1)}, u32[]{:S(2)}, u32[]{:S(2)}) collective-permute-start(bf16[128,512]{1,0:T(8,128)(2,1)S(1)} %get-tuple-element.42), channel_id=1, source_target_pairs={{0,130},{1,97},{4,134},{5,101},{8,138},{9,105},{12,142},{13,109},{... | collective-permute-start | bytes 393224 | tf_op jit(solution)/shard_map/ppermute | solution.py:26
  35.2 11.8 %collective-permute-start.10 = (bf16[128,1024]{1,0:T(8,128)(2,1)S(1)}, bf16[128,1024]{1,0:T(8,128)(2,1)S(1)}, u32[]{:S(2)}, u32[]{:S(2)}) collective-permute-start(bf16[128,1024]{1,0:T(8,128)(2,1)S(1)} %get-tuple-element.36), channel_id=1, source_target_pairs={{0,96},{1,131},{4,100},{5,135},{8,104},{9,139},{12,108},{13,143},{... | collective-permute-start | bytes 786440 | tf_op jit(solution)/shard_map/ppermute | solution.py:26
  36.7 10.3 %collective-permute-start.11 = (bf16[128,1024]{1,0:T(8,128)(2,1)S(1)}, bf16[128,1024]{1,0:T(8,128)(2,1)S(1)}, u32[]{:S(2)}, u32[]{:S(2)}) collective-permute-start(bf16[128,1024]{1,0:T(8,128)(2,1)S(1)} %get-tuple-element.37), channel_id=1, source_target_pairs={{0,64},{1,3},{4,68},{5,7},{8,72},{9,11},{12,76},{13,15},{16,80},{1... | collective-permute-start | bytes 786440 | tf_op jit(solution)/shard_map/ppermute | solution.py:26
  38.0 9.0 %collective-permute-start.12 = (bf16[128,1024]{1,0:T(8,128)(2,1)S(1)}, bf16[128,1024]{1,0:T(8,128)(2,1)S(1)}, u32[]{:S(2)}, u32[]{:S(2)}) collective-permute-start(bf16[128,1024]{1,0:T(8,128)(2,1)S(1)} %get-tuple-element.38), channel_id=1, source_target_pairs={{0,32},{1,129},{4,36},{5,133},{8,40},{9,137},{12,44},{13,141},{16,... | collective-permute-start | bytes 786440 | tf_op jit(solution)/shard_map/ppermute | solution.py:26
  38.8 16.7 %all-to-all-start = ((bf16[8,16,512]{2,1,0:T(8,128)(2,1)}), bf16[8,16,512]{2,1,0:T(8,128)(2,1)S(1)}, u32[]{:S(2)}, u32[]{:S(2)}) async-start(bf16[8,16,512]{2,1,0:T(8,128)(2,1)} %bitcast), calls=%async_computation | async-start | bytes 262144 | tf_op jit(solution)/shard_map/all_to_all | solution.py:292
